TPU v7x, 256 devices: a whole 4x4x8 slice. The times are simulated.
256 devices in a mesh: samp: 16 (over y_hi, z), par: 16 (over x, y_lo, core).
Axes of the slice: x: 4, y: 4 (y_hi: 2, y_lo: 2; y = y_hi * 2 + y_lo), z: 8, core: 2. Of those that a mesh axis runs over, the one named last changes fastest.
Arguments:
- log_derivs: bfloat16 [6144, 16384], P('samp', 'par'), may hold values from -30 to 30
Outputs:
- gram: float32 [6144, 6144], P(('samp', 'par'))
All inputs are finite; a program needn't handle non-finite values.
Results may differ from a plain program's by a relative error of at most 0.00032.
Values may be sent and summed in bfloat16 or wider, within the bound.
No kernel may reach another device: no remote copies, remote signals or barrier semaphores. Data moves between devices by JAX's collectives and lax.ppermute only.
A program may use at most 64 MiB of HBM per device.

v0:
```python
import jax
import jax.numpy as jnp
from jax import lax
from jax.sharding import PartitionSpec as P


def tile_product(left, right):
    return lax.dot_general(
        left, right, (((1,), (1,)), ((), ())), preferred_element_type=jnp.float32
    )


def local(log_derivs):
    rows = log_derivs.shape[0]
    blocks = lax.axis_size("samp")
    total_rows = rows * blocks
    column_total = lax.psum(jnp.sum(log_derivs.astype(jnp.float32), axis=0), "samp")
    mean = column_total / total_rows
    scale = 1.0 / jnp.sqrt(jnp.float32(total_rows))
    centered = ((log_derivs.astype(jnp.float32) - mean) * scale).astype(jnp.bfloat16)
    partial_value = tile_product(centered, lax.all_gather(centered, "samp", axis=0, tiled=True))
    return lax.psum_scatter(partial_value, "par", scatter_dimension=0, tiled=True)


def solution(mesh):
    return jax.shard_map(
        local,
        mesh=mesh,
        in_specs=(P("samp", "par"),),
        out_specs=P(("samp", "par"), None),
        check_vma=False,
    )
```

profile of v0, /device:TPU:2, one launch (start us, length us, event | category | flops | bytes accessed | tf_op | source)
XLA Modules:
  0.0 354.0 jit_solution(1628943441669496022)
XLA Ops:
  6.5 0.0 all-gather.2.cloned.1.call-start
  6.5 1.3 convert_reduce_fusion
  7.8 45.1 %psum.7 = f32[1024]{0:T(1024)S(1)} all-reduce(f32[1024]{0:T(1024)S(1)} %convert_reduce_fusion), channel_id=1, replica_groups=mesh['samp'=16,'par'=16] {'samp'}, use_global_device_ids=true, to_apply=%region_1.0 | all-reduce | flops 1024 | bytes 8192 | tf_op jit(solution)/shard_map/psum | solution.py:17
  52.9 2.2 fusion.1
  55.2 0.0 all-gather.2.cloned.1.call-update
  55.2 0.0 reduce-scatter.2.cloned.1.call-start
  55.2 172.9 %all-gather.2.cloned.1.call-done = bf16[6144,1024]{1,0:T(8,128)(2,1)} async-done(((bf16[384,1024]{1,0:T(8,128)(2,1)}), bf16[6144,1024]{1,0:T(8,128)(2,1)}) %all-gather.2.cloned.1.call-update) | async-done | bytes 12582928 | tf_op jit(solution)/shard_map/all_gather | solution.py:21
  228.2 15.4 %fusion.2 = f32[384,6144]{1,0:T(8,128)} fusion(bf16[384,1024]{1,0:T(8,128)(2,1)} %fusion.1, bf16[6144,1024]{1,0:T(8,128)(2,1)} %all-gather.2.cloned.1.call-done), kind=kOutput, calls=%fused_computation.5 | convolution fusion | flops 4831838208 | bytes 22806528 | tf_op jit(solution)/shard_map/dot_general | solution.py:8
  243.6 0.0 reduce-scatter.2.cloned.1.call-update
  243.7 103.5 %reduce-scatter.2.cloned.1.call-done = f32[24,6144]{1,0:T(8,128)} async-done(((f32[384,6144]{1,0:T(8,128)}), f32[24,6144]{1,0:T(8,128)}) %reduce-scatter.2.cloned.1.call-update) | async-done | bytes 589840 | tf_op jit(solution)/shard_map/reduce_scatter | solution.py:22
  (1 shorter events, 0.0 us)
Async XLA Ops:
  6.5 221.7 %all-gather.2.cloned.1.call-start = ((), (), s32[]{:S(2)}) async-start(), calls=%async_computation.1 | async-start | bytes 13369344 | tf_op jit(solution)/shard_map/all_gather | solution.py:21
  55.2 292.0 %reduce-scatter.2.cloned.1.call-start = ((), (), s32[]{:S(2)}) async-start(), calls=%async_computation.2 | async-start | bytes 10027008 | tf_op jit(solution)/shard_map/reduce_scatter | solution.py:22
Sparse Core Ops, SparseCore 0:
  55.3 172.8 all-gather.1
  243.8 103.3 reduce-scatter.1
where the time goes:
time: 358 us; the launch traced here: 354 us
  waiting for transfers between devices  277 us (77%)
  blocking collectives  45.1 us (13%)
  matrix products  15.4 us (4%)
  between operations  13.4 us (4%)
    all_gather x1, waiting for transfers between devices, local(): lax.all_gather(centered, 'samp', axis=0, tiled=True)  173 us
    reduce_scatter x1, waiting for transfers between devices, local(): lax.psum_scatter(partial_value, 'par', scatter_dimension=0, tiled=True)  104 us
    psum x1, blocking collectives, local(): lax.psum(jnp.sum(log_derivs.astype(jnp.float32), axis=0), 'samp')  45.1 us
    dot_general x1, matrix products, tile_product(): lax.dot_general(left, right, (((1,), (1,)), ((), ())), preferred_element_...  15.4 us
  transfers between devices with their start and end apart: 2, of which 2 were waited for; matrix products, arithmetic and copies ran while one was open for 0% of the time, Pallas kernels for 0%

commit v1 on v0

v1 whole, which is shorter than its diff:
```python
import jax
import jax.numpy as jnp
from jax import lax
from jax.sharding import Mesh, PartitionSpec as P

AXES = {"yh": 2, "z": 8, "x": 4, "yl": 2, "core": 2}
SAMP = ("yh", "z")
PAR = ("x", "yl", "core")

SLOTS = {
    "S0": ((0, 0), (0, 0)),
    "S1": ((0, 1), (0, -1)),
    "S2": ((0, 2), (0, -2)),
    "T1": ((0, 0), (1, 0)),
    "T2": ((0, -1), (1, 1)),
    "T3": ((0, -2), (1, 2)),
}
GROUPS = (
    (("S0", "T1"), ("T1", "S1")),
    (("S0", "T2"), ("T1", "S2"), ("S2", "T2"), ("T2", "S2")),
    (("S0", "T3"), ("S2", "T3")),
)


def permute(value, route):
    sizes = tuple(AXES.values())

    def number(place):
        index = 0
        for coordinate, size in zip(place, sizes):
            index = index * size + coordinate % size
        return index

    places = [
        (y, z, x, l, c)
        for y in range(sizes[0])
        for z in range(sizes[1])
        for x in range(sizes[2])
        for l in range(sizes[3])
        for c in range(sizes[4])
    ]
    pairs = [(number(p), number(route(*p))) for p in places if route(*p) is not None]
    return lax.ppermute(value, tuple(AXES), pairs)


def along_z(y, z, x, l, c):
    return (y, z - 1 if c == 0 else z + 1, x, l, c)


def along_z_other(y, z, x, l, c):
    return (y, z + 1, x, l, 1) if c == 0 else (y, z - 1, x, l, 0)


def across_y(y, z, x, l, c):
    return (y + 1, z, x, l, 1) if c == 1 else None


def across_y_other(y, z, x, l, c):
    return (y + 1, z, x, l, 1) if c == 0 else None


def crossing(y, z, x, l, c):
    return (y + 1, z, x, l, 1) if c == 0 else (y, z, x, l, 0)


def other_core(y, z, x, l, c):
    return (y, z, x, l, 1 - c)


def to_offset(dy, dz):
    return lambda y, z, x, l, c: (y + dy, z + dz, x, l, c)


def scatter_over_par(value):
    rows, cols = value.shape
    exponent = jnp.clip(jnp.ceil(jnp.log2(jnp.max(jnp.abs(value)))), -100.0, 20.0)
    scaled = (value * jnp.exp2(14.0 - exponent)).astype(jnp.float16)
    note = jnp.full((rows, 128), exponent, jnp.float32).astype(jnp.float16)
    message = jnp.concatenate([scaled, note], axis=1).reshape(16, rows // 16, cols + 128)
    return lax.all_to_all(message, PAR, 0, 0)


def gather_sum(message):
    _, chunk, width = message.shape
    cols = width - 128
    factor = jnp.exp2(message[:, :1, cols : cols + 1].astype(jnp.float32) - 14.0)
    parts = message[:, :, :cols].astype(jnp.float32) * factor
    return jnp.sum(parts.reshape(8, 2, chunk, cols), axis=0)


def local(block):
    rows = block.shape[0]
    chunk = rows // 16
    blocks = AXES["yh"] * AXES["z"]
    total_rows = rows * blocks
    sy, sz, core = (lax.axis_index(axis).astype(jnp.uint32) for axis in ("yh", "z", "core"))
    in_order = lax.optimization_barrier

    other = permute(block, other_core)
    near = permute(block, along_z), permute(block, along_z_other)
    mate = permute(block, across_y), permute(block, across_y_other)

    sums = jnp.concatenate(
        [jnp.sum(part.astype(jnp.float32), axis=0) for part in (block, other)]
    ).reshape(-1, 128)
    sums = lax.all_to_all(jnp.broadcast_to(sums, (blocks, *sums.shape)), SAMP, 0, 0)
    mean = jnp.sum(sums, axis=0).reshape(2, 1, -1) / total_rows
    scale = 1.0 / jnp.sqrt(jnp.float32(total_rows))

    def centre(own, others):
        return jnp.concatenate(
            [
                ((part.astype(jnp.float32) - mean[n]) * scale).astype(jnp.bfloat16)
                for n, part in enumerate((own, others))
            ],
            axis=1,
        )

    def scatter(group):
        products = [
            lax.dot_general(
                held[left],
                held[right],
                (((1,), (1,)), ((), ())),
                preferred_element_type=jnp.float32,
            )
            for left, right in group
        ]
        return scatter_over_par(jnp.concatenate(products, axis=1))

    held = {"S0": in_order(centre(block, other))}
    mean, near, mate = in_order((mean, near, mate))
    near = jnp.concatenate(near, axis=0)
    far = permute(near, along_z)
    near_crossed = permute(near, crossing)
    held["S1"] = centre(near[:rows], near[rows:])
    held["T1"] = in_order(jnp.where(core == 1, centre(*mate), held["S0"]))
    messages = [scatter(GROUPS[0])]

    messages[0], far, near_crossed = in_order((messages[0], far, near_crossed))
    far_crossed = permute(far, crossing)
    held["S2"] = centre(far[:rows], far[rows:])
    held["T2"] = centre(near_crossed[rows:], near_crossed[:rows])
    messages.append(scatter(GROUPS[1]))

    messages[1], far_crossed = in_order((messages[1], far_crossed))
    held["T3"] = centre(far_crossed[rows:], far_crossed[:rows])
    messages.append(scatter(GROUPS[2]))

    finished = {}
    for group, message in zip(GROUPS, messages):
        done = gather_sum(message)
        for n, (left, right) in enumerate(group):
            for c in range(2):
                a, b = SLOTS[left][c], SLOTS[right][c]
                offset = (b[0] - a[0]) % 2, (b[1] - a[1]) % 8
                finished.setdefault((a[0] % 2, a[1] % 8), []).append(
                    (offset, done[c, :, n * rows : (n + 1) * rows])
                )

    out = jnp.zeros((chunk, total_rows), jnp.float32)
    for lead, items in finished.items():
        piece = [value for _, value in items]
        if lead != (0, 0):
            moved = permute(jnp.concatenate(piece, axis=1), to_offset(*lead))
            piece = [moved[:, k * rows : (k + 1) * rows] for k in range(len(items))]
        for (offset, _), value in zip(items, piece):
            place = ((sy + offset[0]) & 1) * 8 + ((sz + offset[1]) & 7)
            out = lax.dynamic_update_slice(out, value, (jnp.uint32(0), place * rows))
    return out


def solution(mesh):
    fine = Mesh(mesh.devices.reshape(tuple(AXES.values())), tuple(AXES))
    return jax.shard_map(
        local,
        mesh=fine,
        in_specs=(P(SAMP, PAR),),
        out_specs=P(SAMP + PAR, None),
        check_vma=False,
    )
```

time: 358 us -> 154 us (0.43)
  waiting for transfers between devices: 277 us -> 29.8 us
  starting transfers between devices: 0.04 us -> 52.5 us
  blocking collectives: 45.1 us -> 0 us
  local copies, waits for them, and re-layouts: 0 us -> 37 us
  other arithmetic: 3.52 us -> 23.3 us
  between operations: 13.4 us -> 2.61 us
  matrix products: 15.4 us -> 7.99 us
    all_gather x1 -> x0, waiting for transfers between devices: 173 us -> none  [local(): lax.all_gather(centered, 'samp', axis=0, tiled=True)]
    reduce_scatter x1 -> x0, waiting for transfers between devices: 104 us -> none  [local(): lax.psum_scatter(partial_value, 'par', scatter_dimension=0, tiled=True)]
    psum x1 -> x0, blocking collectives: 45.1 us -> none  [local(): lax.psum(jnp.sum(log_derivs.astype(jnp.float32), axis=0), 'samp')]
    ppermute x0 -> x13, starting transfers between devices: none -> 30.9 us  [permute(): return lax.ppermute(value, tuple(AXES), pairs)]
    all_to_all x0 -> x4, waiting for transfers between devices: none -> 29.8 us  [the longest x3 19.1 us: scatter_over_par(): return lax.all_to_all(message, PAR, 0, 0)]
    all_to_all x0 -> x4, starting transfers between devices: none -> 21.6 us  [the longest x3 16.4 us: scatter_over_par(): return lax.all_to_all(message, PAR, 0, 0)]
    optimization_barrier x0 -> x2, local copies, waits for them, and re-layouts: none -> 14.7 us  [the longest x1 9.12 us: local(): messages[1], far_crossed = in_order((messages[1], far_crossed))]
    dynamic_update_slice x0 -> x16, local copies, waits for them, and re-layouts: none -> 9.9 us  [local(): out = lax.dynamic_update_slice(out, value, (jnp.uint32(0), place * rows))]
  transfers between devices with their start and end apart: 2 -> 17, of which waited for: 2 -> 3; matrix products, arithmetic and copies ran while one was open for 0% -> 32% of each run, Pallas kernels for 0% -> 0%
where the time goes in v1:
time: 154 us; the launch traced here: 153 us
  starting transfers between devices  52.5 us (34%)
  local copies, waits for them, and re-layouts  37 us (24%)
  waiting for transfers between devices  29.8 us (19%)
  other arithmetic  23.3 us (15%)
  matrix products  7.99 us (5%)
  between operations  2.61 us (2%)
    ppermute x13, starting transfers between devices, permute(): return lax.ppermute(value, tuple(AXES), pairs)  30.9 us
    all_to_all x3, waiting for transfers between devices, scatter_over_par(): return lax.all_to_all(message, PAR, 0, 0)  19.1 us
    all_to_all x3, starting transfers between devices, scatter_over_par(): return lax.all_to_all(message, PAR, 0, 0)  16.4 us
    all_to_all x1, waiting for transfers between devices, local(): lax.all_to_all(jnp.broadcast_to(sums, (blocks, *sums.shape)), SAMP, 0, 0)  10.7 us
    dynamic_update_slice x16, local copies, waits for them, and re-layouts, local(): out = lax.dynamic_update_slice(out, value, (jnp.uint32(0), place * rows))  9.9 us
    optimization_barrier x1, local copies, waits for them, and re-layouts, local(): messages[1], far_crossed = in_order((messages[1], far_crossed))  9.12 us
    dot_general x8, matrix products, scatter(): lax.dot_general(held[left], held[right], (((1,), (1,)), ((), ())), prefer...  7.99 us
    convert_element_type x4, other arithmetic, centre(): ((part.astype(jnp.float32) - mean[n]) * scale).astype(jnp.bfloat16)  7.43 us
  transfers between devices with their start and end apart: 17, of which 3 were waited for; matrix products, arithmetic and copies ran while one was open for 32% of the time, Pallas kernels for 0%

profile of v1, /device:TPU:2, one launch (start us, length us, event | category | flops | bytes accessed | tf_op | source)
XLA Modules:
  0.0 153.2 jit_solution(12445473034149617514)
XLA Ops:
  0.0 2.0 %collective-permute-start.2 = (bf16[384,1024]{1,0:T(8,128)(2,1)}, bf16[384,1024]{1,0:T(8,128)(2,1)S(1)}, u32[]{:S(2)}, u32[]{:S(2)}) collective-permute-start(bf16[384,1024]{1,0:T(8,128)(2,1)} %param.1), channel_id=1, source_target_pairs={{0,17},{1,112},{2,19},{3,114},{4,21},{5,116},{6,23},{7,118},{8,25}... | collective-permute-start | bytes 2359304 | tf_op jit(solution)/shard_map/ppermute | solution.py:43
  2.0 3.9 %collective-permute-start.1 = (bf16[384,1024]{1,0:T(8,128)(2,1)}, bf16[384,1024]{1,0:T(8,128)(2,1)S(1)}, u32[]{:S(2)}, u32[]{:S(2)}) collective-permute-start(bf16[384,1024]{1,0:T(8,128)(2,1)} %param.1), channel_id=1, source_target_pairs={{0,112},{1,17},{2,114},{3,19},{4,116},{5,21},{6,118},{7,23},{8,120... | collective-permute-start | bytes 2359304 | tf_op jit(solution)/shard_map/ppermute | solution.py:43
  5.9 5.6 %collective-permute-start.4 = (bf16[384,1024]{1,0:T(8,128)(2,1)}, bf16[384,1024]{1,0:T(8,128)(2,1)}, u32[]{:S(2)}, u32[]{:S(2)}) collective-permute-start(bf16[384,1024]{1,0:T(8,128)(2,1)} %param.1), channel_id=1, source_target_pairs={{0,129},{2,131},{4,133},{6,135},{8,137},{10,139},{12,141},{14,143}... | collective-permute-start | bytes 2359304 | tf_op jit(solution)/shard_map/ppermute | solution.py:43
  11.6 1.5 %collective-permute-start.3 = (bf16[384,1024]{1,0:T(8,128)(2,1)}, bf16[384,1024]{1,0:T(8,128)(2,1)}, u32[]{:S(2)}, u32[]{:S(2)}) collective-permute-start(bf16[384,1024]{1,0:T(8,128)(2,1)} %param.1), channel_id=1, source_target_pairs={{1,129},{3,131},{5,133},{7,135},{9,137},{11,139},{13,141},{15,143}... | collective-permute-start | bytes 2359304 | tf_op jit(solution)/shard_map/ppermute | solution.py:43
  13.1 1.3 convert_reduce_fusion.1
  15.2 5.2 %all-to-all-start = ((f32[16,16,128]{2,1,0:T(8,128)}), f32[16,16,128]{2,1,0:T(8,128)S(1)}, u32[]{:S(2)}, u32[]{:S(2)}) async-start(f32[16,16,128]{2,1,0:T(8,128)} %broadcast_in_dim.10), calls=%async_computation | async-start | bytes 262144 | tf_op jit(solution)/shard_map/all_to_all | solution.py:106
  20.4 10.7 %all-to-all-done = f32[16,16,128]{2,1,0:T(8,128)S(1)} async-done(((f32[16,16,128]{2,1,0:T(8,128)}), f32[16,16,128]{2,1,0:T(8,128)S(1)}, u32[]{:S(2)}, u32[]{:S(2)}) %all-to-all-start) | async-done | bytes 131104 | tf_op jit(solution)/shard_map/all_to_all | solution.py:106
  31.2 1.0 constant_dynamic-update-slice_fusion.1
  32.2 0.9 constant_dynamic-update-slice_fusion
  33.1 2.6 %collective-permute-start.6 = (bf16[768,1024]{1,0:T(8,128)(2,1)}, bf16[768,1024]{1,0:T(8,128)(2,1)}, u32[]{:S(2)}, u32[]{:S(2)}) collective-permute-start(bf16[768,1024]{1,0:T(8,128)(2,1)} %constant_dynamic-update-slice_fusion), channel_id=1, source_target_pairs={{0,129},{1,0},{2,131},{3,2},{4,133},{5,4},{6,135},{7,6},{8,137},{9... | collective-permute-start | bytes 4718600 | tf_op jit(solution)/shard_map/ppermute | solution.py:43
  35.6 3.0 %collective-permute-start.5 = (bf16[768,1024]{1,0:T(8,128)(2,1)}, bf16[768,1024]{1,0:T(8,128)(2,1)}, u32[]{:S(2)}, u32[]{:S(2)}) collective-permute-start(bf16[768,1024]{1,0:T(8,128)(2,1)} %constant_dynamic-update-slice_fusion), channel_id=1, source_target_pairs={{0,112},{1,17},{2,114},{3,19},{4,116},{5,21},{6,118},{7,23},{8,120... | collective-permute-start | bytes 4718600 | tf_op jit(solution)/shard_map/ppermute | solution.py:43
  39.1 2.3 %multiply_convert_fusion.7 = (bf16[384,1024]{1,0:T(8,128)(2,1)S(1)}, bf16[384,1024]{1,0:T(8,128)(2,1)S(1)}, bf16[384,1024]{1,0:T(8,128)(2,1)S(1)}, bf16[384,1024]{1,0:T(8,128)(2,1)S(1)}) fusion(bf16[384,1024]{1,0:T(8,128)(2,1)S(1)} %collective-permute-done.2, f32[1024]{0:T(1024)S(1)} %bitcast.81, bf16[384,1024]{1,0:T(8,128)(2,1)} %collective-permute-done.4, ...), kind=kLoop, calls=%fused_computation.27 | loop fusion | flops 6291456 | bytes 6299648 | tf_op jit(solution)/shard_map/convert_element_type | solution.py:113
  42.0 1.0 fusion.4
  43.2 1.0 fusion.37
  46.2 1.0 concatenate.63.clone
  47.2 5.0 %all-to-all-start.1 = ((f16[16,24,896]{2,1,0:T(8,128)(2,1)}), f16[16,24,896]{2,1,0:T(8,128)(2,1)S(1)}, u32[]{:S(2)}, u32[]{:S(2)}) async-start(f16[16,24,896]{2,1,0:T(8,128)(2,1)} %bitcast.6), calls=%async_computation.1 | async-start | bytes 1376256 | tf_op jit(solution)/shard_map/all_to_all | solution.py:80
  52.1 10.1 %all-to-all-done.1 = f16[16,24,896]{2,1,0:T(8,128)(2,1)S(1)} async-done(((f16[16,24,896]{2,1,0:T(8,128)(2,1)}), f16[16,24,896]{2,1,0:T(8,128)(2,1)S(1)}, u32[]{:S(2)}, u32[]{:S(2)}) %all-to-all-start.1) | async-done | bytes 688160 | tf_op jit(solution)/shard_map/all_to_all | solution.py:80
  62.3 2.9 %multiply_convert_fusion.6 = (bf16[384,1024]{1,0:T(8,128)(2,1)S(1)}, bf16[384,1024]{1,0:T(8,128)(2,1)S(1)}, bf16[384,1024]{1,0:T(8,128)(2,1)S(1)}, bf16[384,1024]{1,0:T(8,128)(2,1)S(1)}) fusion(bf16[768,1024]{1,0:T(8,128)(2,1)} %collective-permute-done.6, f32[1024]{0:T(1024)S(1)} %bitcast.79, f32[1024]{0:T(1024)S(1)} %bitcast.82, ...), kind=kLoop, calls=%fused_computation.26 | loop fusion | flops 6291456 | bytes 6299648 | tf_op jit(solution)/shard_map/convert_element_type | solution.py:113
  65.2 1.0 fusion.35
  66.2 1.0 fusion.11
  67.2 1.0 fusion.10
  68.2 1.0 fusion.12
  69.3 0.9 copy-done.3
  70.2 0.8 abs_reduce_fusion
  71.7 1.7 %collective-permute-start.7 = (bf16[768,1024]{1,0:T(8,128)(2,1)}, bf16[768,1024]{1,0:T(8,128)(2,1)}, u32[]{:S(2)}, u32[]{:S(2)}) collective-permute-start(bf16[768,1024]{1,0:T(8,128)(2,1)} %collective-permute-done.5), channel_id=1, source_target_pairs={{0,129},{1,0},{2,131},{3,2},{4,133},{5,4},{6,135},{7,6},{8,137},{9... | collective-permute-start | bytes 4718600 | tf_op jit(solution)/shard_map/ppermute | solution.py:43
  73.4 2.5 %multiply_convert_fusion = f16[384,1536]{0,1:T(8,128)(2,1)} fusion(f32[384,384]{0,1:T(8,128)} %copy-done.2, f32[384,384]{0,1:T(8,128)S(1)} %fusion.11, f32[384,384]{0,1:T(8,128)S(1)} %fusion.35, f32[384,384]{0,1:T(8,128)} %copy-done.3, f32[]{:T(128)S(6)} %exp2.41), kind=kLoop, calls=%fused_computation.2 | loop fusion | flops 2949120 | bytes 3538948 | tf_op jit(solution)/shard_map/convert_element_type | solution.py:77
  75.9 2.1 %copy.31 = f16[384,1536]{1,0:T(8,128)(2,1)S(1)} copy(f16[384,1536]{0,1:T(8,128)(2,1)} %multiply_convert_fusion) | data formatting | bytes 2359296
  78.0 1.3 concatenate.68.clone
  79.3 4.9 %all-to-all-start.2 = ((f16[16,24,1664]{2,1,0:T(8,128)(2,1)}), f16[16,24,1664]{2,1,0:T(8,128)(2,1)S(1)}, u32[]{:S(2)}, u32[]{:S(2)}) async-start(f16[16,24,1664]{2,1,0:T(8,128)(2,1)} %bitcast.75), calls=%async_computation.2 | async-start | bytes 2555904 | tf_op jit(solution)/shard_map/all_to_all | solution.py:80
  84.2 5.6 %copy.24 = f16[16,24,896]{0,2,1:T(8,128)(2,1)} copy(f16[16,24,896]{2,1,0:T(8,128)(2,1)S(1)} %all-to-all-done.1) | data formatting | bytes 1376256 | tf_op jit(solution)/shard_map/optimization_barrier | solution.py:140
  90.5 1.2 convert_multiply_fusion.2
  91.7 1.3 reduce_sum.57
  93.7 0.9 broadcast_in_dim.4
  96.4 8.9 %all-to-all-done.2 = f16[16,24,1664]{2,1,0:T(8,128)(2,1)S(1)} async-done(((f16[16,24,1664]{2,1,0:T(8,128)(2,1)}), f16[16,24,1664]{2,1,0:T(8,128)(2,1)S(1)}, u32[]{:S(2)}, u32[]{:S(2)}) %all-to-all-start.2) | async-done | bytes 1277984 | tf_op jit(solution)/shard_map/all_to_all | solution.py:80
  105.3 1.9 %multiply_convert_fusion.2 = (bf16[384,1024]{1,0:T(8,128)(2,1)S(1)}, bf16[384,1024]{1,0:T(8,128)(2,1)S(1)}) fusion(bf16[768,1024]{1,0:T(8,128)(2,1)} %collective-permute-done.7, f32[1024]{0:T(1024)S(1)} %bitcast.80, f32[1024]{0:T(1024)S(1)} %bitcast.83), kind=kLoop, calls=%fused_computation.22 | loop fusion | flops 3145728 | bytes 3153920 | tf_op jit(solution)/shard_map/convert_element_type | solution.py:113
  107.2 1.0 fusion.8
  108.2 1.0 fusion.9
  109.2 0.8 copy-done.1
  110.0 0.7 abs_reduce_fusion.1
  111.5 1.2 multiply_convert_fusion.11
  113.1 1.0 concatenate.71.clone
  114.1 6.5 %all-to-all-start.3 = ((f16[16,24,896]{2,1,0:T(8,128)(2,1)}), f16[16,24,896]{2,1,0:T(8,128)(2,1)S(1)}, u32[]{:S(2)}, u32[]{:S(2)}) async-start(f16[16,24,896]{2,1,0:T(8,128)(2,1)} %bitcast.18), calls=%async_computation.3 | async-start | bytes 1376256 | tf_op jit(solution)/shard_map/all_to_all | solution.py:80
  120.7 9.1 %copy.26 = f16[16,24,1664]{0,2,1:T(8,128)(2,1)} copy(f16[16,24,1664]{2,1,0:T(8,128)(2,1)S(1)} %all-to-all-done.2) | data formatting | bytes 2555904 | tf_op jit(solution)/shard_map/optimization_barrier | solution.py:146
  130.4 1.8 %convert_multiply_fusion = f32[16,24,1536]{2,1,0:T(8,128)} fusion(f32[16]{0:T(128)S(1)} %fusion.24, f16[16,24,1664]{2,1,0:T(8,128)(2,1)S(1)} %all-to-all-done.2), kind=kLoop, calls=%fused_computation.1 | loop fusion | flops 1179648 | bytes 3539008 | tf_op jit(solution)/shard_map/mul | solution.py:87
  132.2 1.8 %reduce_sum.58 = f32[2,24,1536]{2,1,0:T(8,128)S(1)} reduce(f32[8,2,24,1536]{3,2,1,0:T(8,128)} %bitcast.74, f32[]{:T(128)} %constant.20.clone.1), dimensions={0}, to_apply=%region_6.7 | reduce | flops 516096 | bytes 2654212 | tf_op jit(solution)/shard_map/reduce_sum | solution.py:88
  134.4 4.2 %collective-permute-start.11 = (f32[24,384]{1,0:T(8,128)S(1)}, f32[24,384]{1,0:T(8,128)S(1)}, u32[]{:S(2)}, u32[]{:S(2)}) collective-permute-start(f32[24,384]{1,0:T(8,128)S(1)} %get-tuple-element.32), channel_id=1, source_target_pairs={{0,112},{1,113},{2,114},{3,115},{4,116},{5,117},{6,118},{7,119},{8... | collective-permute-start | bytes 110600 | tf_op jit(solution)/shard_map/ppermute | solution.py:43
  138.6 1.9 %collective-permute-start.8 = (f32[24,768]{1,0:T(8,128)S(1)}, f32[24,768]{1,0:T(8,128)S(1)}, u32[]{:S(2)}, u32[]{:S(2)}) collective-permute-start(f32[24,768]{1,0:T(8,128)S(1)} %pad_maximum_fusion.12), channel_id=1, source_target_pairs={{0,128},{1,129},{2,130},{3,131},{4,132},{5,133},{6,134},{7,135},{8... | collective-permute-start | bytes 221192 | tf_op jit(solution)/shard_map/ppermute | solution.py:43
  142.8 4.1 %collective-permute-start.10 = (f32[24,768]{1,0:T(8,128)S(1)}, f32[24,768]{1,0:T(8,128)S(1)}, u32[]{:S(2)}, u32[]{:S(2)}) collective-permute-start(f32[24,768]{1,0:T(8,128)S(1)} %pad_maximum_fusion.14), channel_id=1, source_target_pairs={{0,96},{1,97},{2,98},{3,99},{4,100},{5,101},{6,102},{7,103},{8,104... | collective-permute-start | bytes 221192 | tf_op jit(solution)/shard_map/ppermute | solution.py:43
  (81 shorter events, 16.7 us)
Async XLA Ops:
  0.0 14.4 %collective-permute-start = (bf16[384,1024]{1,0:T(8,128)(2,1)}, bf16[384,1024]{1,0:T(8,128)(2,1)S(1)}, u32[]{:S(2)}, u32[]{:S(2)}) collective-permute-start(bf16[384,1024]{1,0:T(8,128)(2,1)} %param.1), channel_id=1, source_target_pairs={{0,1},{1,0},{2,3},{3,2},{4,5},{5,4},{6,7},{7,6},{8,9},{9,8},{10,11... | collective-permute-start | bytes 2359304 | tf_op jit(solution)/shard_map/ppermute | solution.py:43
  0.0 31.2 %collective-permute-start.2 = (bf16[384,1024]{1,0:T(8,128)(2,1)}, bf16[384,1024]{1,0:T(8,128)(2,1)S(1)}, u32[]{:S(2)}, u32[]{:S(2)}) collective-permute-start(bf16[384,1024]{1,0:T(8,128)(2,1)} %param.1), channel_id=1, source_target_pairs={{0,17},{1,112},{2,19},{3,114},{4,21},{5,116},{6,23},{7,118},{8,25}... | collective-permute-start | bytes 2359304 | tf_op jit(solution)/shard_map/ppermute | solution.py:43
  2.0 29.1 %collective-permute-start.1 = (bf16[384,1024]{1,0:T(8,128)(2,1)}, bf16[384,1024]{1,0:T(8,128)(2,1)S(1)}, u32[]{:S(2)}, u32[]{:S(2)}) collective-permute-start(bf16[384,1024]{1,0:T(8,128)(2,1)} %param.1), channel_id=1, source_target_pairs={{0,112},{1,17},{2,114},{3,19},{4,116},{5,21},{6,118},{7,23},{8,120... | collective-permute-start | bytes 2359304 | tf_op jit(solution)/shard_map/ppermute | solution.py:43
  5.9 25.2 %collective-permute-start.4 = (bf16[384,1024]{1,0:T(8,128)(2,1)}, bf16[384,1024]{1,0:T(8,128)(2,1)}, u32[]{:S(2)}, u32[]{:S(2)}) collective-permute-start(bf16[384,1024]{1,0:T(8,128)(2,1)} %param.1), channel_id=1, source_target_pairs={{0,129},{2,131},{4,133},{6,135},{8,137},{10,139},{12,141},{14,143}... | collective-permute-start | bytes 2359304 | tf_op jit(solution)/shard_map/ppermute | solution.py:43
  11.6 19.6 %collective-permute-start.3 = (bf16[384,1024]{1,0:T(8,128)(2,1)}, bf16[384,1024]{1,0:T(8,128)(2,1)}, u32[]{:S(2)}, u32[]{:S(2)}) collective-permute-start(bf16[384,1024]{1,0:T(8,128)(2,1)} %param.1), channel_id=1, source_target_pairs={{1,129},{3,131},{5,133},{7,135},{9,137},{11,139},{13,141},{15,143}... | collective-permute-start | bytes 2359304 | tf_op jit(solution)/shard_map/ppermute | solution.py:43
  15.2 15.9 %all-to-all-start = ((f32[16,16,128]{2,1,0:T(8,128)}), f32[16,16,128]{2,1,0:T(8,128)S(1)}, u32[]{:S(2)}, u32[]{:S(2)}) async-start(f32[16,16,128]{2,1,0:T(8,128)} %broadcast_in_dim.10), calls=%async_computation | async-start | bytes 262144 | tf_op jit(solution)/shard_map/all_to_all | solution.py:106
  31.1 7.5 %copy-start = (bf16[384,1024]{1,0:T(8,128)(2,1)S(1)}, bf16[384,1024]{1,0:T(8,128)(2,1)}, u32[]{:S(2)}) copy-start(bf16[384,1024]{1,0:T(8,128)(2,1)} %param.1) | copy-start | bytes 2359300
  33.1 29.2 %collective-permute-start.6 = (bf16[768,1024]{1,0:T(8,128)(2,1)}, bf16[768,1024]{1,0:T(8,128)(2,1)}, u32[]{:S(2)}, u32[]{:S(2)}) collective-permute-start(bf16[768,1024]{1,0:T(8,128)(2,1)} %constant_dynamic-update-slice_fusion), channel_id=1, source_target_pairs={{0,129},{1,0},{2,131},{3,2},{4,133},{5,4},{6,135},{7,6},{8,137},{9... | collective-permute-start | bytes 4718600 | tf_op jit(solution)/shard_map/ppermute | solution.py:43
  35.6 26.7 %collective-permute-start.5 = (bf16[768,1024]{1,0:T(8,128)(2,1)}, bf16[768,1024]{1,0:T(8,128)(2,1)}, u32[]{:S(2)}, u32[]{:S(2)}) collective-permute-start(bf16[768,1024]{1,0:T(8,128)(2,1)} %constant_dynamic-update-slice_fusion), channel_id=1, source_target_pairs={{0,112},{1,17},{2,114},{3,19},{4,116},{5,21},{6,118},{7,23},{8,120... | collective-permute-start | bytes 4718600 | tf_op jit(solution)/shard_map/ppermute | solution.py:43
  42.0 1.1 copy-start.4
  47.2 15.1 %all-to-all-start.1 = ((f16[16,24,896]{2,1,0:T(8,128)(2,1)}), f16[16,24,896]{2,1,0:T(8,128)(2,1)S(1)}, u32[]{:S(2)}, u32[]{:S(2)}) async-start(f16[16,24,896]{2,1,0:T(8,128)(2,1)} %bitcast.6), calls=%async_computation.1 | async-start | bytes 1376256 | tf_op jit(solution)/shard_map/all_to_all | solution.py:80
  62.3 2.9 %copy-start.5 = (bf16[384,2048]{1,0:T(8,128)(2,1)S(1)}, bf16[384,2048]{1,0:T(8,128)(2,1)}, u32[]{:S(2)}) copy-start(bf16[384,2048]{1,0:T(8,128)(2,1)} %copy-done.4) | copy-start | bytes 4718596
  65.2 2.0 %copy-start.6 = (bf16[384,1024]{1,0:T(8,128)(2,1)}, bf16[384,1024]{1,0:T(8,128)(2,1)S(1)}, u32[]{:S(2)}) copy-start(bf16[384,1024]{1,0:T(8,128)(2,1)S(1)} %get-tuple-element.38) | copy-start | bytes 2359300
  65.2 2.0 %copy-start.8 = (bf16[384,1024]{1,0:T(8,128)(2,1)}, bf16[384,1024]{1,0:T(8,128)(2,1)S(1)}, u32[]{:S(2)}) copy-start(bf16[384,1024]{1,0:T(8,128)(2,1)S(1)} %get-tuple-element.39) | copy-start | bytes 2359300
  68.2 1.0 copy-start.2
  69.3 0.9 copy-start.3
  71.7 33.6 %collective-permute-start.7 = (bf16[768,1024]{1,0:T(8,128)(2,1)}, bf16[768,1024]{1,0:T(8,128)(2,1)}, u32[]{:S(2)}, u32[]{:S(2)}) collective-permute-start(bf16[768,1024]{1,0:T(8,128)(2,1)} %collective-permute-done.5), channel_id=1, source_target_pairs={{0,129},{1,0},{2,131},{3,2},{4,133},{5,4},{6,135},{7,6},{8,137},{9... | collective-permute-start | bytes 4718600 | tf_op jit(solution)/shard_map/ppermute | solution.py:43
  79.3 26.0 %all-to-all-start.2 = ((f16[16,24,1664]{2,1,0:T(8,128)(2,1)}), f16[16,24,1664]{2,1,0:T(8,128)(2,1)S(1)}, u32[]{:S(2)}, u32[]{:S(2)}) async-start(f16[16,24,1664]{2,1,0:T(8,128)(2,1)} %bitcast.75), calls=%async_computation.2 | async-start | bytes 2555904 | tf_op jit(solution)/shard_map/all_to_all | solution.py:80
  105.3 1.9 %copy-start.7 = (bf16[384,1024]{1,0:T(8,128)(2,1)S(1)}, bf16[384,1024]{1,0:T(8,128)(2,1)}, u32[]{:S(2)}) copy-start(bf16[384,1024]{1,0:T(8,128)(2,1)} %copy-done.6) | copy-start | bytes 2359300
  105.3 1.9 %copy-start.9 = (bf16[384,1024]{1,0:T(8,128)(2,1)S(1)}, bf16[384,1024]{1,0:T(8,128)(2,1)}, u32[]{:S(2)}) copy-start(bf16[384,1024]{1,0:T(8,128)(2,1)} %copy-done.8) | copy-start | bytes 2359300
  109.2 0.8 copy-start.1
  114.1 28.2 %all-to-all-start.3 = ((f16[16,24,896]{2,1,0:T(8,128)(2,1)}), f16[16,24,896]{2,1,0:T(8,128)(2,1)S(1)}, u32[]{:S(2)}, u32[]{:S(2)}) async-start(f16[16,24,896]{2,1,0:T(8,128)(2,1)} %bitcast.18), calls=%async_computation.3 | async-start | bytes 1376256 | tf_op jit(solution)/shard_map/all_to_all | solution.py:80
  132.2 6.4 %copy-start.10 = (f32[24,384]{1,0:T(8,128)S(1)}, f32[24,384]{1,0:T(8,128)}, u32[]{:S(2)}) copy-start(f32[24,384]{1,0:T(8,128)} %slice_bitcast_fusion.7) | copy-start | bytes 110596
  134.1 18.4 %collective-permute-start.12 = (f32[24,384]{1,0:T(8,128)S(1)}, f32[24,384]{1,0:T(8,128)S(1)}, u32[]{:S(2)}, u32[]{:S(2)}) collective-permute-start(f32[24,384]{1,0:T(8,128)S(1)} %get-tuple-element.31), channel_id=1, source_target_pairs={{0,144},{1,145},{2,146},{3,147},{4,148},{5,149},{6,150},{7,151},{8... | collective-permute-start | bytes 110600 | tf_op jit(solution)/shard_map/ppermute | solution.py:43
  134.4 17.5 %collective-permute-start.11 = (f32[24,384]{1,0:T(8,128)S(1)}, f32[24,384]{1,0:T(8,128)S(1)}, u32[]{:S(2)}, u32[]{:S(2)}) collective-permute-start(f32[24,384]{1,0:T(8,128)S(1)} %get-tuple-element.32), channel_id=1, source_target_pairs={{0,112},{1,113},{2,114},{3,115},{4,116},{5,117},{6,118},{7,119},{8... | collective-permute-start | bytes 110600 | tf_op jit(solution)/shard_map/ppermute | solution.py:43
  138.6 9.6 %collective-permute-start.8 = (f32[24,768]{1,0:T(8,128)S(1)}, f32[24,768]{1,0:T(8,128)S(1)}, u32[]{:S(2)}, u32[]{:S(2)}) collective-permute-start(f32[24,768]{1,0:T(8,128)S(1)} %pad_maximum_fusion.12), channel_id=1, source_target_pairs={{0,128},{1,129},{2,130},{3,131},{4,132},{5,133},{6,134},{7,135},{8... | collective-permute-start | bytes 221192 | tf_op jit(solution)/shard_map/ppermute | solution.py:43
  142.7 6.7 %collective-permute-start.9 = (f32[24,768]{1,0:T(8,128)S(1)}, f32[24,768]{1,0:T(8,128)S(1)}, u32[]{:S(2)}, u32[]{:S(2)}) collective-permute-start(f32[24,768]{1,0:T(8,128)S(1)} %pad_maximum_fusion.13), channel_id=1, source_target_pairs={{0,32},{1,33},{2,34},{3,35},{4,36},{5,37},{6,38},{7,39},{8,40},{9,... | collective-permute-start | bytes 221192 | tf_op jit(solution)/shard_map/ppermute | solution.py:43
  142.8 7.8 %collective-permute-start.10 = (f32[24,768]{1,0:T(8,128)S(1)}, f32[24,768]{1,0:T(8,128)S(1)}, u32[]{:S(2)}, u32[]{:S(2)}) collective-permute-start(f32[24,768]{1,0:T(8,128)S(1)} %pad_maximum_fusion.14), channel_id=1, source_target_pairs={{0,96},{1,97},{2,98},{3,99},{4,100},{5,101},{6,102},{7,103},{8,104... | collective-permute-start | bytes 221192 | tf_op jit(solution)/shard_map/ppermute | solution.py:43

commit v2 on v0

v2 whole, which is shorter than its diff:
```python
import functools

import jax
import jax.numpy as jnp
import numpy as np
from jax import lax
from jax.experimental import pallas as pl
from jax.experimental.pallas import tpu as pltpu
from jax.sharding import Mesh, PartitionSpec as P

AXES = {"yh": 2, "z": 8, "x": 4, "yl": 2, "core": 2}
SAMP = ("yh", "z")
PAR = ("x", "yl", "core")
VMEM_MIB = 16

SLOTS = {
    "S0": ((0, 0), (0, 0)),
    "S1": ((0, 1), (0, -1)),
    "S2": ((0, 2), (0, -2)),
    "T1": ((0, 0), (1, 0)),
    "T3": ((0, -2), (1, 2)),
}
GROUPS = (
    ((("S0", "T1"),) * 2, (("S1", "T1"),) * 2, (("T1", "S1"),) * 2),
    ((("S0", "T3"),) * 2, (("T3", "S0"),) * 2, (("S1", "T3"),) * 2, (("T3", "S1"),) * 2),
    ((("T3", "S2"), ("S2", "T3")),),
)


def permute(value, route):
    sizes = tuple(AXES.values())

    def number(place):
        index = 0
        for coordinate, size in zip(place, sizes):
            index = index * size + coordinate % size
        return index

    places = [
        (y, z, x, l, c)
        for y in range(sizes[0])
        for z in range(sizes[1])
        for x in range(sizes[2])
        for l in range(sizes[3])
        for c in range(sizes[4])
    ]
    pairs = [(number(p), number(route(*p))) for p in places if route(*p) is not None]
    return lax.ppermute(value, tuple(AXES), pairs)


def along_z(y, z, x, l, c):
    return (y, z - 1 if c == 0 else z + 1, x, l, c)


def across_y(y, z, x, l, c):
    return (y + 1, z, x, l, 1) if c == 1 else None


def crossing(y, z, x, l, c):
    return (y + 1, z - 1, x, l, 1) if c == 0 else (y, z + 1, x, l, 0)


def other_core(y, z, x, l, c):
    return (y, z, x, l, 1 - c)


def to_offset(dy, dz):
    return lambda y, z, x, l, c: (y + dy, z + dz, x, l, c)


def multiply_kernel(raw, held, kept, group, scale, core_ref, mean_ref, *refs):
    raw_refs, refs = refs[: len(raw)], refs[len(raw) :]
    held_refs, kept_refs, out_ref = refs[: len(held)], refs[len(held) : -1], refs[-1]
    rows, width = raw_refs[0].shape[0] // 2, raw_refs[0].shape[1]
    cols = out_ref.shape[1] - 128
    on_core_1 = core_ref[0] == 1

    terms = [[] for _ in group]
    for half in range(2):
        across = slice(half * width, (half + 1) * width)
        mean = mean_ref[0:1, across]
        wide = {}
        for ref, (name, flip) in zip(raw_refs, raw):
            first = (1 - half if flip else half) * rows
            wide[name] = ref[first : first + rows, :].astype(jnp.float32)
        if "T1" in wide:
            wide["T1"] = jnp.where(on_core_1, wide["T1"], wide["S0"])
        blocks = {
            name: ((value - mean) * scale).astype(jnp.bfloat16) for name, value in wide.items()
        }
        for ref, name in zip(kept_refs, kept):
            ref[:, across] = blocks[name]
        for ref, name in zip(held_refs, held):
            blocks[name] = ref[:, across]
        for term, ((left, right), (left_1, right_1)) in zip(terms, group):
            left, right = blocks[left], blocks[right]
            if left_1 != left:
                left = jnp.where(on_core_1, blocks[left_1], left)
                right = jnp.where(on_core_1, blocks[right_1], right)
            term.append(
                lax.dot_general(
                    left, right, (((1,), (1,)), ((), ())), preferred_element_type=jnp.float32
                )
            )
    largest = jnp.zeros((1, 1), jnp.float32)
    for n, (first, second) in enumerate(terms):
        total = first + second
        out_ref[:, n * rows : (n + 1) * rows] = total
        largest = jnp.maximum(largest, jnp.max(jnp.abs(total), keepdims=True))
    exponent = jnp.clip(jnp.ceil(jnp.log2(largest)), -100.0, 20.0)
    out_ref[:, :cols] *= jnp.exp2(14.0 - exponent)
    out_ref[:, cols:] = jnp.broadcast_to(exponent, (rows, 128))


def multiply(core, mean, raw, held, kept, group, scale):
    first = next(iter(raw.values()))[0]
    rows, width = first.shape[0] // 2, 2 * first.shape[1]
    cols = len(group) * rows
    whole = pl.BlockSpec(memory_space=pltpu.VMEM)
    centred = jax.ShapeDtypeStruct((rows, width), jnp.bfloat16)
    names = tuple((name, flip) for name, (_, flip) in raw.items())
    *blocks, value = pl.pallas_call(
        functools.partial(multiply_kernel, names, tuple(held), kept, group, scale),
        in_specs=[pl.BlockSpec(memory_space=pltpu.SMEM)] + [whole] * (1 + len(raw) + len(held)),
        out_specs=[whole] * (len(kept) + 1),
        out_shape=[*(centred for _ in kept), jax.ShapeDtypeStruct((rows, cols + 128), jnp.float32)],
        compiler_params=pltpu.CompilerParams(vmem_limit_bytes=VMEM_MIB * 2**20),
        cost_estimate=pl.CostEstimate(flops=1, bytes_accessed=1, transcendentals=0),
    )(core, mean, *(block for block, _ in raw.values()), *held.values())
    return dict(zip(kept, blocks)), value


def scatter_over_par(value):
    rows, width = value.shape
    message = value.astype(jnp.float16).reshape(16, rows // 16, width)
    return lax.all_to_all(message, PAR, 0, 0)


def gather_sum(message):
    _, chunk, width = message.shape
    message = message.reshape(8, 2, chunk, width)
    factor = jnp.exp2(message[:, :, :1, width - 128 : width - 127].astype(jnp.float32) - 14.0)
    return jnp.sum(message[:, :, :, : width - 128].astype(jnp.float32) * factor, axis=0)


def place_kernel(pieces, place_ref, *refs):
    out_ref = refs[-1]
    for n, (source, index) in enumerate(pieces):
        value = refs[source][index]
        width = value.shape[1]
        out_ref[:, pl.ds(pl.multiple_of(place_ref[n] * width, 128), width)] = value


def local(block):
    rows = block.shape[0]
    chunk = rows // 16
    blocks = AXES["yh"] * AXES["z"]
    total_rows = rows * blocks
    sy, sz, core = (lax.axis_index(axis).astype(jnp.int32) for axis in ("yh", "z", "core"))
    core = core.reshape(1)

    own = jnp.concatenate([block, permute(block, other_core)], axis=0)
    near = permute(own, along_z)
    mate = permute(own, across_y)

    sums = [jnp.sum(part.astype(jnp.float32), axis=0) for part in (own[:rows], own[rows:])]
    sums = jnp.concatenate(sums).reshape(-1, 128)
    sums = lax.all_to_all(jnp.broadcast_to(sums, (blocks, *sums.shape)), SAMP, 0, 0)
    near, mate, sums = lax.optimization_barrier((near, mate, sums))
    crossed = permute(near, crossing)
    mean = jnp.sum(sums, axis=0).reshape(1, -1) / total_rows
    mean = jnp.broadcast_to(mean, (8, mean.shape[1]))
    scale = float(np.float32(1) / np.sqrt(np.float32(total_rows)))

    raw = {"S0": (own, False), "S1": (near, False), "T1": (mate, False)}
    held, value = multiply(core, mean, raw, {}, ("S0", "S1"), GROUPS[0], scale)
    messages = [scatter_over_par(value)]
    held, value = multiply(core, mean, {"T3": (crossed, True)}, held, ("T3",), GROUPS[1], scale)
    near, value = lax.optimization_barrier((near, value))
    far = permute(near, along_z)
    messages.append(scatter_over_par(value))
    _, value = multiply(core, mean, {"S2": (far, False)}, held, (), GROUPS[2], scale)
    messages[1], value = lax.optimization_barrier((messages[1], value))
    messages.append(scatter_over_par(value))

    sources, pieces, places = [], [], []

    def move(leads):
        for lead, items in leads.items():
            value = jnp.concatenate([value for _, value in items], axis=1)
            moved.append(permute(value, to_offset(*lead)))
            for n, (offset, _) in enumerate(items):
                across = slice(n * rows, (n + 1) * rows)
                pieces.append((len(sources) + len(moved) - 1, (slice(None), across)))
                places.append(offset)

    leads = {}
    for n, (group, message) in enumerate(zip(GROUPS, messages)):
        moved = []
        if n == len(GROUPS) - 1:
            move(leads)
            leads = {}
            *moved, message = lax.optimization_barrier((*moved, message))
            sources += moved
            moved = []
        done = gather_sum(message)
        sources.append(done)
        for k, pairs in enumerate(group):
            across = slice(k * rows, (k + 1) * rows)
            for c, (left, right) in enumerate(pairs):
                a, b = SLOTS[left][c], SLOTS[right][c]
                offset = (b[0] - a[0]) & 1, (b[1] - a[1]) & 7
                lead = a[0] & 1, a[1] & 7
                if lead == (0, 0):
                    pieces.append((len(sources) - 1, (c, slice(None), across)))
                    places.append(offset)
                else:
                    leads.setdefault(lead, []).append((offset, done[c, :, across]))
    move(leads)
    sources += moved
    place = jnp.stack([((sy + dy) & 1) * 8 + ((sz + dz) & 7) for dy, dz in places])
    whole = pl.BlockSpec(memory_space=pltpu.VMEM)
    return pl.pallas_call(
        functools.partial(place_kernel, tuple(pieces)),
        in_specs=[pl.BlockSpec(memory_space=pltpu.SMEM), *(whole for _ in sources)],
        out_specs=whole,
        out_shape=jax.ShapeDtypeStruct((chunk, total_rows), jnp.float32),
        compiler_params=pltpu.CompilerParams(vmem_limit_bytes=8 * 2**20),
    )(place, *sources)


def solution(mesh):
    fine = Mesh(mesh.devices.reshape(tuple(AXES.values())), tuple(AXES))
    return jax.shard_map(
        local,
        mesh=fine,
        in_specs=(P(SAMP, PAR),),
        out_specs=P(SAMP + PAR, None),
        check_vma=False,
    )
```

time: 358 us -> 128 us (0.36)
  waiting for transfers between devices: 277 us -> 27 us
  starting transfers between devices: 0.04 us -> 46.2 us
  blocking collectives: 45.1 us -> 20.7 us
  matrix products: 15.4 us -> 0 us
  local copies, waits for them, and re-layouts: 0 us -> 14.1 us
  between operations: 13.4 us -> 0.19 us
  Pallas kernels: 0 us -> 10.8 us
    all_gather x1 -> x0, waiting for transfers between devices: 173 us -> none  [local(): lax.all_gather(centered, 'samp', axis=0, tiled=True)]
    reduce_scatter x1 -> x0, waiting for transfers between devices: 104 us -> none  [local(): lax.psum_scatter(partial_value, 'par', scatter_dimension=0, tiled=True)]
    psum x1 -> x0, blocking collectives: 45.1 us -> none  [local(): lax.psum(jnp.sum(log_derivs.astype(jnp.float32), axis=0), 'samp')]
    ppermute x0 -> x11, starting transfers between devices: none -> 28 us  [permute(): return lax.ppermute(value, tuple(AXES), pairs)]
    ppermute x0 -> x11, waiting for transfers between devices: none -> 24.5 us  [permute(): return lax.ppermute(value, tuple(AXES), pairs)]
    all_to_all x0 -> x1, blocking collectives: none -> 20.7 us  [local(): lax.all_to_all(jnp.broadcast_to(sums, (blocks, *sums.shape)), SAMP, 0, 0)]
    all_to_all x0 -> x3, starting transfers between devices: none -> 18.2 us  [scatter_over_par(): return lax.all_to_all(message, PAR, 0, 0)]
    dot_general x1 -> x0, matrix products: 15.4 us -> none  [tile_product(): lax.dot_general(left, right, (((1,), (1,)), ((), ())), preferred_element_...]
  transfers between devices with their start and end apart: 2 -> 14, of which waited for: 2 -> 7; matrix products, arithmetic and copies ran while one was open for 0% -> 6% of each run, Pallas kernels for 0% -> 7%
where the time goes in v2:
time: 128 us; the launch traced here: 126 us
  starting transfers between devices  46.2 us (36%)
  waiting for transfers between devices  27 us (21%)
  blocking collectives  20.7 us (16%)
  local copies, waits for them, and re-layouts  14.1 us (11%)
  Pallas kernels  10.8 us (8%)
  other arithmetic  6.72 us (5%)
    ppermute x11, starting transfers between devices, permute(): return lax.ppermute(value, tuple(AXES), pairs)  28 us
    ppermute x11, waiting for transfers between devices, permute(): return lax.ppermute(value, tuple(AXES), pairs)  24.5 us
    all_to_all x1, blocking collectives, local(): lax.all_to_all(jnp.broadcast_to(sums, (blocks, *sums.shape)), SAMP, 0, 0)  20.7 us
    all_to_all x3, starting transfers between devices, scatter_over_par(): return lax.all_to_all(message, PAR, 0, 0)  18.2 us
    unnamed x26, local copies, waits for them, and re-layouts  12.1 us
    pallas_call x3, Pallas kernels, multiply(): pl.pallas_call(functools.partial(multiply_kernel, names, tuple(held), kep...  9.42 us
    reduce_sum x3, other arithmetic, gather_sum(): jnp.sum(message[:, :, :, :width - 128].astype(jnp.float32) * factor, axis=0)  3.21 us
    convert_element_type x3, other arithmetic, scatter_over_par(): message = value.astype(jnp.float16).reshape(16, rows // 16, width)  3.14 us
  transfers between devices with their start and end apart: 14, of which 7 were waited for; matrix products, arithmetic and copies ran while one was open for 6% of the time, Pallas kernels for 7%

profile of v2, /device:TPU:2, one launch (start us, length us, event | category | flops | bytes accessed | tf_op | source)
XLA Modules:
  0.0 125.7 jit_solution(4620643017235141405)
XLA Ops:
  0.0 1.3 constant_dynamic-update-slice_fusion.1
  1.3 1.2 collective-permute-done
  2.6 5.9 %collective-permute-start.1 = (bf16[768,1024]{1,0:T(8,128)(2,1)S(1)}, bf16[768,1024]{1,0:T(8,128)(2,1)S(1)}, u32[]{:S(2)}, u32[]{:S(2)}) collective-permute-start(bf16[768,1024]{1,0:T(8,128)(2,1)S(1)} %constant_dynamic-update-slice_fusion.refs_0_), channel_id=1, source_target_pairs={{0,112},{1,17},{2,114},{3,19},{4,116},{5,21},{6,118},{7,23},{8,120... | collective-permute-start | bytes 4718600 | tf_op jit(solution)/shard_map/ppermute | solution.py:48
  8.5 0.7 collective-permute-start.2
  9.3 0.1 convert_reduce_fusion.1
  9.4 0.1 convert_reduce_fusion
  9.6 20.7 %all_to_all.20 = f32[16,16,128]{2,1,0:T(8,128)S(1)} all-to-all(f32[16,16,128]{2,1,0:T(8,128)S(1)} %broadcast_in_dim.8), channel_id=1, replica_groups=mesh['yh'=2,'z'=8,'x'=4,'yl'=2,'core'=2] {'yh','z'}, dimensions={0} | all-to-all | bytes 262144 | tf_op jit(solution)/shard_map/all_to_all | solution.py:168
  30.2 1.1 copy-done
  31.4 4.9 %collective-permute-start.3 = (bf16[768,1024]{1,0:T(8,128)(2,1)S(1)}, bf16[768,1024]{1,0:T(8,128)(2,1)}, u32[]{:S(2)}, u32[]{:S(2)}) collective-permute-start(bf16[768,1024]{1,0:T(8,128)(2,1)S(1)} %collective-permute-done.1.refs_1_), channel_id=1, source_target_pairs={{0,241},{1,16},{2,243},{3,18},{4,245},{5,20},{6,247},{7,22},{8,249... | collective-permute-start | bytes 4718600 | tf_op jit(solution)/shard_map/ppermute | solution.py:48
  36.3 1.4 %copy-done.1 = bf16[768,1024]{1,0:T(8,128)(2,1)S(1)} copy-done((bf16[768,1024]{1,0:T(8,128)(2,1)S(1)}, bf16[768,1024]{1,0:T(8,128)(2,1)}, u32[]{:S(2)}) %copy-start.1) | copy-done | bytes 1572888
  37.7 3.1 %shard_map.17 = (bf16[384,2048]{1,0:T(8,128)(2,1)S(1)}, bf16[384,2048]{1,0:T(8,128)(2,1)S(1)}, f32[384,1280]{1,0:T(8,128)S(1)}) custom-call(s32[1]{0:T(128)} %bitcast.16.core_ref, f32[8,2048]{1,0:T(8,128)S(1)} %broadcast_in_dim.9.mean_ref, bf16[768,1024]{1,0:T(8,128)(2,1)S(1)} %constant_dynamic-update-slice_fusion.refs_0_, ...), custom_call_target="tpu_custom_call" | custom-call | flops 1 | bytes 1 | tf_op jit(solution)/shard_map/pallas_call | solution.py:122
  40.8 1.1 copy-done.4
  41.9 1.2 convert_element_type.35
  43.1 0.3 copy-done.2
  43.4 5.1 %all-to-all-start.1 = ((f16[16,24,1280]{2,1,0:T(8,128)(2,1)}), f16[16,24,1280]{2,1,0:T(8,128)(2,1)}, u32[]{:S(2)}, u32[]{:S(2)}) async-start(f16[16,24,1280]{2,1,0:T(8,128)(2,1)} %bitcast.56), calls=%async_computation.1 | async-start | bytes 1966080 | tf_op jit(solution)/shard_map/all_to_all | solution.py:136
  48.6 8.1 %collective-permute-done.3.refs_0_ = bf16[768,1024]{1,0:T(8,128)(2,1)} collective-permute-done((bf16[768,1024]{1,0:T(8,128)(2,1)S(1)}, bf16[768,1024]{1,0:T(8,128)(2,1)}, u32[]{:S(2)}, u32[]{:S(2)}) %collective-permute-start.3) | collective-permute-done | bytes 1572896 | tf_op jit(solution)/shard_map/ppermute | solution.py:48
  56.6 1.4 %copy-done.5 = bf16[384,2048]{1,0:T(8,128)(2,1)S(1)} copy-done((bf16[384,2048]{1,0:T(8,128)(2,1)S(1)}, bf16[384,2048]{1,0:T(8,128)(2,1)}, u32[]{:S(2)}) %copy-start.5) | copy-done | bytes 1572888
  58.0 5.1 %shard_map.18 = (bf16[384,2048]{1,0:T(8,128)(2,1)S(1)}, f32[384,1664]{1,0:T(8,128)S(1)}) custom-call(s32[1]{0:T(128)} %bitcast.16.core_ref, f32[8,2048]{1,0:T(8,128)S(1)} %broadcast_in_dim.9.mean_ref, bf16[768,1024]{1,0:T(8,128)(2,1)} %collective-permute-done.3.refs_0_, bf16[384,2048]{1,0:T(8,128)(2,1)S(1)} %copy-done.3, bf16[384,2048]{1,0:T(8,128)(2,1)S(1)} %copy-done.5), custom_call_target="tpu_custom_call" | custom-call | flops 1 | bytes 1 | tf_op jit(solution)/shard_map/pallas_call | solution.py:122
  63.2 1.2 copy-done.6
  64.4 3.3 %collective-permute-start.4 = (bf16[768,1024]{1,0:T(8,128)(2,1)S(1)}, bf16[768,1024]{1,0:T(8,128)(2,1)S(1)}, u32[]{:S(2)}, u32[]{:S(2)}) collective-permute-start(bf16[768,1024]{1,0:T(8,128)(2,1)S(1)} %collective-permute-done.1.refs_1_), channel_id=1, source_target_pairs={{0,112},{1,17},{2,114},{3,19},{4,116},{5,21},{6,118},{7,23},{8,120... | collective-permute-start | bytes 4718600 | tf_op jit(solution)/shard_map/ppermute | solution.py:48
  67.7 1.2 convert_element_type.38
  68.9 7.4 %all-to-all-start.2 = ((f16[16,24,1664]{2,1,0:T(8,128)(2,1)}), f16[16,24,1664]{2,1,0:T(8,128)(2,1)}, u32[]{:S(2)}, u32[]{:S(2)}) async-start(f16[16,24,1664]{2,1,0:T(8,128)(2,1)} %bitcast.55), calls=%async_computation.2 | async-start | bytes 2555904 | tf_op jit(solution)/shard_map/all_to_all | solution.py:136
  76.2 0.8 slice.69
  77.0 0.1 copy.14
  77.2 1.5 %multiply_reduce_fusion.1.refs_0_ = f32[2,24,1152]{2,1,0:T(8,128)S(1)} fusion(f16[8,2,24,1280]{3,2,1,0:T(8,128)(2,1)} %bitcast.21, f32[8,2]{1,0:T(8,128)S(1)} %copy.9), kind=kLoop, calls=%fused_computation.1 | loop fusion | flops 1271808 | bytes 1105984 | tf_op jit(solution)/shard_map/reduce_sum | solution.py:143
  78.7 6.9 %collective-permute-done.4.refs_0_ = bf16[768,1024]{1,0:T(8,128)(2,1)S(1)} collective-permute-done((bf16[768,1024]{1,0:T(8,128)(2,1)S(1)}, bf16[768,1024]{1,0:T(8,128)(2,1)S(1)}, u32[]{:S(2)}, u32[]{:S(2)}) %collective-permute-start.4) | collective-permute-done | bytes 1572896 | tf_op jit(solution)/shard_map/ppermute | solution.py:48
  85.6 1.1 copy-done.8
  86.7 1.4 %copy-done.7 = bf16[384,2048]{1,0:T(8,128)(2,1)S(1)} copy-done((bf16[384,2048]{1,0:T(8,128)(2,1)S(1)}, bf16[384,2048]{1,0:T(8,128)(2,1)}, u32[]{:S(2)}) %copy-start.7) | copy-done | bytes 1572888
  88.1 1.4 %copy-done.9 = bf16[768,1024]{1,0:T(8,128)(2,1)S(1)} copy-done((bf16[768,1024]{1,0:T(8,128)(2,1)S(1)}, bf16[768,1024]{1,0:T(8,128)(2,1)}, u32[]{:S(2)}) %copy-start.9) | copy-done | bytes 1572888
  89.6 1.2 shard_map.19
  90.8 2.4 %all-to-all-done.2 = f16[16,24,1664]{2,1,0:T(8,128)(2,1)} async-done(((f16[16,24,1664]{2,1,0:T(8,128)(2,1)}), f16[16,24,1664]{2,1,0:T(8,128)(2,1)}, u32[]{:S(2)}, u32[]{:S(2)}) %all-to-all-start.2) | async-done | bytes 1277984 | tf_op jit(solution)/shard_map/all_to_all | solution.py:136
  93.2 0.8 slice.71
  94.0 0.1 copy.15
  94.2 1.6 %multiply_reduce_fusion.refs_1_ = f32[2,24,1536]{2,1,0:T(8,128)S(1)} fusion(f16[8,2,24,1664]{3,2,1,0:T(8,128)(2,1)} %bitcast.24, f32[8,2]{1,0:T(8,128)S(1)} %copy.11), kind=kLoop, calls=%fused_computation | loop fusion | flops 1695744 | bytes 1474624 | tf_op jit(solution)/shard_map/reduce_sum | solution.py:143
  95.9 1.9 %collective-permute-start.5 = (f32[24,768]{1,0:T(8,128)S(1)}, f32[24,768]{1,0:T(8,128)S(1)}, u32[]{:S(2)}, u32[]{:S(2)}) collective-permute-start(f32[24,768]{1,0:T(8,128)S(1)} %pad_maximum_fusion), channel_id=1, source_target_pairs={{0,16},{1,17},{2,18},{3,19},{4,20},{5,21},{6,22},{7,23},{8,24},{9,... | collective-permute-start | bytes 221192 | tf_op jit(solution)/shard_map/ppermute | solution.py:48
  97.8 0.8 convert_element_type.41
  98.6 5.7 %all-to-all-start.3 = ((f16[16,24,512]{2,1,0:T(8,128)(2,1)}), f16[16,24,512]{2,1,0:T(8,128)(2,1)S(1)}, u32[]{:S(2)}, u32[]{:S(2)}) async-start(f16[16,24,512]{2,1,0:T(8,128)(2,1)} %bitcast.35), calls=%async_computation.3 | async-start | bytes 786432 | tf_op jit(solution)/shard_map/all_to_all | solution.py:136
  104.3 2.9 %collective-permute-start.6 = (f32[24,768]{1,0:T(8,128)S(1)}, f32[24,768]{1,0:T(8,128)S(1)}, u32[]{:S(2)}, u32[]{:S(2)}) collective-permute-start(f32[24,768]{1,0:T(8,128)S(1)} %pad_maximum_fusion.1), channel_id=1, source_target_pairs={{0,112},{1,113},{2,114},{3,115},{4,116},{5,117},{6,118},{7,119},{8... | collective-permute-start | bytes 221192 | tf_op jit(solution)/shard_map/ppermute | solution.py:48
  107.2 2.0 %collective-permute-start.8 = (f32[24,768]{1,0:T(8,128)S(1)}, f32[24,768]{1,0:T(8,128)S(1)}, u32[]{:S(2)}, u32[]{:S(2)}) collective-permute-start(f32[24,768]{1,0:T(8,128)S(1)} %pad_maximum_fusion.2), channel_id=1, source_target_pairs={{0,96},{1,97},{2,98},{3,99},{4,100},{5,101},{6,102},{7,103},{8,104... | collective-permute-start | bytes 221192 | tf_op jit(solution)/shard_map/ppermute | solution.py:48
  109.2 2.6 %collective-permute-start.9 = (f32[24,768]{1,0:T(8,128)S(1)}, f32[24,768]{1,0:T(8,128)S(1)}, u32[]{:S(2)}, u32[]{:S(2)}) collective-permute-start(f32[24,768]{1,0:T(8,128)S(1)} %pad_maximum_fusion.3), channel_id=1, source_target_pairs={{0,160},{1,161},{2,162},{3,163},{4,164},{5,165},{6,166},{7,167},{8... | collective-permute-start | bytes 221192 | tf_op jit(solution)/shard_map/ppermute | solution.py:48
  111.8 1.3 collective-permute-start.7
  113.1 4.2 %collective-permute-done.7.refs_4_ = f32[24,384]{1,0:T(8,128)S(1)} collective-permute-done((f32[24,384]{1,0:T(8,128)S(1)}, f32[24,384]{1,0:T(8,128)S(1)}, u32[]{:S(2)}, u32[]{:S(2)}) %collective-permute-start.7) | collective-permute-done | bytes 36896 | tf_op jit(solution)/shard_map/ppermute | solution.py:48
  117.3 1.1 collective-permute-done.9.refs_6_
  118.4 0.1 copy.16
  118.6 0.1 multiply_reduce_fusion.2.refs_7_
  118.8 2.5 %collective-permute-start.10 = (f32[24,768]{1,0:T(8,128)S(1)}, f32[24,768]{1,0:T(8,128)S(1)}, u32[]{:S(2)}, u32[]{:S(2)}) collective-permute-start(f32[24,768]{1,0:T(8,128)S(1)} %pad_maximum_fusion.4), channel_id=1, source_target_pairs={{0,96},{1,97},{2,98},{3,99},{4,100},{5,101},{6,102},{7,103},{8,104... | collective-permute-start | bytes 221192 | tf_op jit(solution)/shard_map/ppermute | solution.py:48
  121.4 3.0 %collective-permute-done.10.refs_8_ = f32[24,768]{1,0:T(8,128)S(1)} collective-permute-done((f32[24,768]{1,0:T(8,128)S(1)}, f32[24,768]{1,0:T(8,128)S(1)}, u32[]{:S(2)}, u32[]{:S(2)}) %collective-permute-start.10) | collective-permute-done | bytes 73760 | tf_op jit(solution)/shard_map/ppermute | solution.py:48
  124.3 1.4 %shard_map.20 = f32[24,6144]{1,0:T(8,128)} custom-call(s32[16]{0:T(128)S(1)} %stack.67.place_ref, f32[2,24,1152]{2,1,0:T(8,128)S(1)} %multiply_reduce_fusion.1.refs_0_, f32[2,24,1536]{2,1,0:T(8,128)S(1)} %multiply_reduce_fusion.refs_1_, f32[24,768]{1,0:T(8,128)S(1)} %collective-permute-done.5.refs_2_, f32[24,768]{1,0:T(8,128)S(1)} %collective-permute-done.6.refs_3_, ...), custom_call_target="tpu_custom_call" | custom-call | tf_op jit(solution)/shard_map/pallas_call | solution.py:223
  (42 shorter events, 0.6 us)
Async XLA Ops:
  0.0 9.2 %copy-start.10 = (bf16[384,1024]{1,0:T(8,128)(2,1)S(1)}, bf16[384,1024]{1,0:T(8,128)(2,1)}, u32[]{:S(2)}) copy-start(bf16[384,1024]{1,0:T(8,128)(2,1)} %param.1) | copy-start | bytes 2359300
  0.0 2.5 %collective-permute-start = (bf16[384,1024]{1,0:T(8,128)(2,1)}, bf16[384,1024]{1,0:T(8,128)(2,1)S(1)}, u32[]{:S(2)}, u32[]{:S(2)}) collective-permute-start(bf16[384,1024]{1,0:T(8,128)(2,1)} %param.1), channel_id=1, source_target_pairs={{0,1},{1,0},{2,3},{3,2},{4,5},{5,4},{6,7},{7,6},{8,9},{9,8},{10,11... | collective-permute-start | bytes 2359304 | tf_op jit(solution)/shard_map/ppermute | solution.py:48
  2.6 27.7 %collective-permute-start.1 = (bf16[768,1024]{1,0:T(8,128)(2,1)S(1)}, bf16[768,1024]{1,0:T(8,128)(2,1)S(1)}, u32[]{:S(2)}, u32[]{:S(2)}) collective-permute-start(bf16[768,1024]{1,0:T(8,128)(2,1)S(1)} %constant_dynamic-update-slice_fusion.refs_0_), channel_id=1, source_target_pairs={{0,112},{1,17},{2,114},{3,19},{4,116},{5,21},{6,118},{7,23},{8,120... | collective-permute-start | bytes 4718600 | tf_op jit(solution)/shard_map/ppermute | solution.py:48
  8.5 21.7 %collective-permute-start.2 = (bf16[768,1024]{1,0:T(8,128)(2,1)S(1)}, bf16[768,1024]{1,0:T(8,128)(2,1)S(1)}, u32[]{:S(2)}, u32[]{:S(2)}) collective-permute-start(bf16[768,1024]{1,0:T(8,128)(2,1)S(1)} %constant_dynamic-update-slice_fusion.refs_0_), channel_id=1, source_target_pairs={{1,129},{3,131},{5,133},{7,135},{9,137},{11,139},{13,141},{15,143}... | collective-permute-start | bytes 4718600 | tf_op jit(solution)/shard_map/ppermute | solution.py:48
  30.2 1.1 copy-start
  31.4 25.2 %collective-permute-start.3 = (bf16[768,1024]{1,0:T(8,128)(2,1)S(1)}, bf16[768,1024]{1,0:T(8,128)(2,1)}, u32[]{:S(2)}, u32[]{:S(2)}) collective-permute-start(bf16[768,1024]{1,0:T(8,128)(2,1)S(1)} %collective-permute-done.1.refs_1_), channel_id=1, source_target_pairs={{0,241},{1,16},{2,243},{3,18},{4,245},{5,20},{6,247},{7,22},{8,249... | collective-permute-start | bytes 4718600 | tf_op jit(solution)/shard_map/ppermute | solution.py:48
  36.3 1.4 %copy-start.1 = (bf16[768,1024]{1,0:T(8,128)(2,1)S(1)}, bf16[768,1024]{1,0:T(8,128)(2,1)}, u32[]{:S(2)}) copy-start(bf16[768,1024]{1,0:T(8,128)(2,1)} %copy-done) | copy-start | bytes 4718596
  40.8 1.1 copy-start.4
  41.9 1.5 %copy-start.2 = (bf16[384,2048]{1,0:T(8,128)(2,1)}, bf16[384,2048]{1,0:T(8,128)(2,1)S(1)}, u32[]{:S(2)}) copy-start(bf16[384,2048]{1,0:T(8,128)(2,1)S(1)} %get-tuple-element.27.refs_1_) | copy-start | bytes 4718596
  43.4 13.2 %copy-start.3 = (bf16[384,2048]{1,0:T(8,128)(2,1)S(1)}, bf16[384,2048]{1,0:T(8,128)(2,1)}, u32[]{:S(2)}) copy-start(bf16[384,2048]{1,0:T(8,128)(2,1)} %copy-done.2) | copy-start | bytes 4718596
  43.4 25.4 %all-to-all-start.1 = ((f16[16,24,1280]{2,1,0:T(8,128)(2,1)}), f16[16,24,1280]{2,1,0:T(8,128)(2,1)}, u32[]{:S(2)}, u32[]{:S(2)}) async-start(f16[16,24,1280]{2,1,0:T(8,128)(2,1)} %bitcast.56), calls=%async_computation.1 | async-start | bytes 1966080 | tf_op jit(solution)/shard_map/all_to_all | solution.py:136
  56.6 1.4 %copy-start.5 = (bf16[384,2048]{1,0:T(8,128)(2,1)S(1)}, bf16[384,2048]{1,0:T(8,128)(2,1)}, u32[]{:S(2)}) copy-start(bf16[384,2048]{1,0:T(8,128)(2,1)} %copy-done.4) | copy-start | bytes 4718596
  63.2 1.2 copy-start.6
  64.4 21.2 %collective-permute-start.4 = (bf16[768,1024]{1,0:T(8,128)(2,1)S(1)}, bf16[768,1024]{1,0:T(8,128)(2,1)S(1)}, u32[]{:S(2)}, u32[]{:S(2)}) collective-permute-start(bf16[768,1024]{1,0:T(8,128)(2,1)S(1)} %collective-permute-done.1.refs_1_), channel_id=1, source_target_pairs={{0,112},{1,17},{2,114},{3,19},{4,116},{5,21},{6,118},{7,23},{8,120... | collective-permute-start | bytes 4718600 | tf_op jit(solution)/shard_map/ppermute | solution.py:48
  68.9 24.3 %all-to-all-start.2 = ((f16[16,24,1664]{2,1,0:T(8,128)(2,1)}), f16[16,24,1664]{2,1,0:T(8,128)(2,1)}, u32[]{:S(2)}, u32[]{:S(2)}) async-start(f16[16,24,1664]{2,1,0:T(8,128)(2,1)} %bitcast.55), calls=%async_computation.2 | async-start | bytes 2555904 | tf_op jit(solution)/shard_map/all_to_all | solution.py:136
  85.6 1.1 copy-start.8
  86.7 1.4 %copy-start.7 = (bf16[384,2048]{1,0:T(8,128)(2,1)S(1)}, bf16[384,2048]{1,0:T(8,128)(2,1)}, u32[]{:S(2)}) copy-start(bf16[384,2048]{1,0:T(8,128)(2,1)} %copy-done.6) | copy-start | bytes 4718596
  88.1 1.4 %copy-start.9 = (bf16[768,1024]{1,0:T(8,128)(2,1)S(1)}, bf16[768,1024]{1,0:T(8,128)(2,1)}, u32[]{:S(2)}) copy-start(bf16[768,1024]{1,0:T(8,128)(2,1)} %copy-done.8) | copy-start | bytes 4718596
  95.9 21.4 %collective-permute-start.5 = (f32[24,768]{1,0:T(8,128)S(1)}, f32[24,768]{1,0:T(8,128)S(1)}, u32[]{:S(2)}, u32[]{:S(2)}) collective-permute-start(f32[24,768]{1,0:T(8,128)S(1)} %pad_maximum_fusion), channel_id=1, source_target_pairs={{0,16},{1,17},{2,18},{3,19},{4,20},{5,21},{6,22},{7,23},{8,24},{9,... | collective-permute-start | bytes 221192 | tf_op jit(solution)/shard_map/ppermute | solution.py:48
  98.6 19.9 %all-to-all-start.3 = ((f16[16,24,512]{2,1,0:T(8,128)(2,1)}), f16[16,24,512]{2,1,0:T(8,128)(2,1)S(1)}, u32[]{:S(2)}, u32[]{:S(2)}) async-start(f16[16,24,512]{2,1,0:T(8,128)(2,1)} %bitcast.35), calls=%async_computation.3 | async-start | bytes 786432 | tf_op jit(solution)/shard_map/all_to_all | solution.py:136
  104.3 13.0 %collective-permute-start.6 = (f32[24,768]{1,0:T(8,128)S(1)}, f32[24,768]{1,0:T(8,128)S(1)}, u32[]{:S(2)}, u32[]{:S(2)}) collective-permute-start(f32[24,768]{1,0:T(8,128)S(1)} %pad_maximum_fusion.1), channel_id=1, source_target_pairs={{0,112},{1,113},{2,114},{3,115},{4,116},{5,117},{6,118},{7,119},{8... | collective-permute-start | bytes 221192 | tf_op jit(solution)/shard_map/ppermute | solution.py:48
  107.2 10.1 %collective-permute-start.8 = (f32[24,768]{1,0:T(8,128)S(1)}, f32[24,768]{1,0:T(8,128)S(1)}, u32[]{:S(2)}, u32[]{:S(2)}) collective-permute-start(f32[24,768]{1,0:T(8,128)S(1)} %pad_maximum_fusion.2), channel_id=1, source_target_pairs={{0,96},{1,97},{2,98},{3,99},{4,100},{5,101},{6,102},{7,103},{8,104... | collective-permute-start | bytes 221192 | tf_op jit(solution)/shard_map/ppermute | solution.py:48
  109.2 9.2 %collective-permute-start.9 = (f32[24,768]{1,0:T(8,128)S(1)}, f32[24,768]{1,0:T(8,128)S(1)}, u32[]{:S(2)}, u32[]{:S(2)}) collective-permute-start(f32[24,768]{1,0:T(8,128)S(1)} %pad_maximum_fusion.3), channel_id=1, source_target_pairs={{0,160},{1,161},{2,162},{3,163},{4,164},{5,165},{6,166},{7,167},{8... | collective-permute-start | bytes 221192 | tf_op jit(solution)/shard_map/ppermute | solution.py:48
  111.8 5.5 %collective-permute-start.7 = (f32[24,384]{1,0:T(8,128)S(1)}, f32[24,384]{1,0:T(8,128)S(1)}, u32[]{:S(2)}, u32[]{:S(2)}) collective-permute-start(f32[24,384]{1,0:T(8,128)S(1)} %get-tuple-element.54), channel_id=1, source_target_pairs={{0,128},{1,129},{2,130},{3,131},{4,132},{5,133},{6,134},{7,135},{8... | collective-permute-start | bytes 110600 | tf_op jit(solution)/shard_map/ppermute | solution.py:48
  118.8 5.5 %collective-permute-start.10 = (f32[24,768]{1,0:T(8,128)S(1)}, f32[24,768]{1,0:T(8,128)S(1)}, u32[]{:S(2)}, u32[]{:S(2)}) collective-permute-start(f32[24,768]{1,0:T(8,128)S(1)} %pad_maximum_fusion.4), channel_id=1, source_target_pairs={{0,96},{1,97},{2,98},{3,99},{4,100},{5,101},{6,102},{7,103},{8,104... | collective-permute-start | bytes 221192 | tf_op jit(solution)/shard_map/ppermute | solution.py:48

commit v3 on v2

--- a/solution.py
+++ b/solution.py
@@ -22,8 +22,8 @@
 }
 GROUPS = (
     ((("S0", "T1"),) * 2, (("S1", "T1"),) * 2, (("T1", "S1"),) * 2),
-    ((("S0", "T3"),) * 2, (("T3", "S0"),) * 2, (("S1", "T3"),) * 2, (("T3", "S1"),) * 2),
-    ((("T3", "S2"), ("S2", "T3")),),
+    ((("T3", "S0"),) * 2, (("S1", "T3"),) * 2, (("T3", "S1"),) * 2),
+    ((("S0", "T3"),) * 2, (("T3", "S2"), ("S2", "T3"))),
 )
 
 
@@ -130,9 +130,12 @@
     return dict(zip(kept, blocks)), value
 
 
-def scatter_over_par(value):
+def message_of(value):
     rows, width = value.shape
-    message = value.astype(jnp.float16).reshape(16, rows // 16, width)
+    return value.astype(jnp.float16).reshape(16, rows // 16, width)
+
+
+def scatter_over_par(message):
     return lax.all_to_all(message, PAR, 0, 0)
 
 
@@ -174,37 +177,23 @@
 
     raw = {"S0": (own, False), "S1": (near, False), "T1": (mate, False)}
     held, value = multiply(core, mean, raw, {}, ("S0", "S1"), GROUPS[0], scale)
-    messages = [scatter_over_par(value)]
-    held, value = multiply(core, mean, {"T3": (crossed, True)}, held, ("T3",), GROUPS[1], scale)
-    near, value = lax.optimization_barrier((near, value))
+    messages = [scatter_over_par(message_of(value))]
+    near, held["S1"] = lax.optimization_barrier((near, held["S1"]))
     far = permute(near, along_z)
-    messages.append(scatter_over_par(value))
-    _, value = multiply(core, mean, {"S2": (far, False)}, held, (), GROUPS[2], scale)
-    messages[1], value = lax.optimization_barrier((messages[1], value))
-    messages.append(scatter_over_par(value))
+    _, value = multiply(core, mean, {"T3": (crossed, True)}, held, (), GROUPS[1], scale)
+    messages.append(scatter_over_par(message_of(value)))
+    far, crossed, _ = lax.optimization_barrier((far, crossed, value))
+    raw = {"S2": (far, False), "T3": (crossed, True)}
+    _, value = multiply(core, mean, raw, {"S0": held["S0"]}, (), GROUPS[2], scale)
+    messages[1], message = lax.optimization_barrier((messages[1], message_of(value)))
+    messages.append(scatter_over_par(message))
 
     sources, pieces, places = [], [], []
-
-    def move(leads):
-        for lead, items in leads.items():
-            value = jnp.concatenate([value for _, value in items], axis=1)
-            moved.append(permute(value, to_offset(*lead)))
-            for n, (offset, _) in enumerate(items):
-                across = slice(n * rows, (n + 1) * rows)
-                pieces.append((len(sources) + len(moved) - 1, (slice(None), across)))
-                places.append(offset)
-
-    leads = {}
-    for n, (group, message) in enumerate(zip(GROUPS, messages)):
-        moved = []
-        if n == len(GROUPS) - 1:
-            move(leads)
-            leads = {}
-            *moved, message = lax.optimization_barrier((*moved, message))
-            sources += moved
-            moved = []
+    for group, message in zip(GROUPS, messages):
+        *sources, message = lax.optimization_barrier((*sources, message))
         done = gather_sum(message)
         sources.append(done)
+        leads = {}
         for k, pairs in enumerate(group):
             across = slice(k * rows, (k + 1) * rows)
             for c, (left, right) in enumerate(pairs):
@@ -216,8 +205,13 @@
                     places.append(offset)
                 else:
                     leads.setdefault(lead, []).append((offset, done[c, :, across]))
-    move(leads)
-    sources += moved
+        for lead, items in leads.items():
+            value = jnp.concatenate([value for _, value in items], axis=1)
+            sources.append(permute(value, to_offset(*lead)))
+            for n, (offset, _) in enumerate(items):
+                across = slice(n * rows, (n + 1) * rows)
+                pieces.append((len(sources) - 1, (slice(None), across)))
+                places.append(offset)
     place = jnp.stack([((sy + dy) & 1) * 8 + ((sz + dz) & 7) for dy, dz in places])
     whole = pl.BlockSpec(memory_space=pltpu.VMEM)
     return pl.pallas_call(

time: 128 us -> 116 us (0.906); the launches traced: 126 us -> 116 us
  waiting for transfers between devices: 27 us -> 20.1 us
  local copies, waits for them, and re-layouts: 14.1 us -> 9.79 us
  Pallas kernels: 10.8 us -> 12.2 us
    ppermute x11 -> x13, waiting for transfers between devices: 24.5 us -> 15.6 us  [permute(): return lax.ppermute(value, tuple(AXES), pairs)]
    unnamed x26 -> x18, local copies, waits for them, and re-layouts: 12.1 us -> 7.16 us
    all_to_all x3, waiting for transfers between devices: 2.44 us -> 4.51 us  [scatter_over_par(): return lax.all_to_all(message, PAR, 0, 0)]
    all_to_all x3, starting transfers between devices: 18.2 us -> 16.3 us  [scatter_over_par(): return lax.all_to_all(message, PAR, 0, 0)]
    ppermute x11 -> x13, starting transfers between devices: 28 us -> 29.6 us  [permute(): return lax.ppermute(value, tuple(AXES), pairs)]
    pallas_call x3, Pallas kernels: 9.42 us -> 10.8 us  [multiply(): pl.pallas_call(functools.partial(multiply_kernel, names, tuple(held), kep...]
  transfers between devices with their start and end apart: 14 -> 16, of which waited for: 7 -> 8; matrix products, arithmetic and copies ran while one was open for 6% -> 8% of each run, Pallas kernels for 7% -> 9%
where the time goes in v3:
time: 116 us
  starting transfers between devices  46 us (40%)
  blocking collectives  20.7 us (18%)
  waiting for transfers between devices  20.1 us (17%)
  Pallas kernels  12.2 us (11%)
  local copies, waits for them, and re-layouts  9.79 us (8%)
  other arithmetic  6.72 us (6%)
    ppermute x13, starting transfers between devices, permute(): return lax.ppermute(value, tuple(AXES), pairs)  29.6 us
    all_to_all x1, blocking collectives, local(): lax.all_to_all(jnp.broadcast_to(sums, (blocks, *sums.shape)), SAMP, 0, 0)  20.7 us
    all_to_all x3, starting transfers between devices, scatter_over_par(): return lax.all_to_all(message, PAR, 0, 0)  16.3 us
    ppermute x13, waiting for transfers between devices, permute(): return lax.ppermute(value, tuple(AXES), pairs)  15.6 us
    pallas_call x3, Pallas kernels, multiply(): pl.pallas_call(functools.partial(multiply_kernel, names, tuple(held), kep...  10.8 us
    unnamed x18, local copies, waits for them, and re-layouts  7.16 us
    all_to_all x3, waiting for transfers between devices, scatter_over_par(): return lax.all_to_all(message, PAR, 0, 0)  4.51 us
    convert_element_type x3, other arithmetic, message_of(): return value.astype(jnp.float16).reshape(16, rows // 16, width)  3.21 us
  transfers between devices with their start and end apart: 16, of which 8 were waited for; matrix products, arithmetic and copies ran while one was open for 8% of the time, Pallas kernels for 9%

profile of v3, /device:TPU:2, one launch (start us, length us, event | category | flops | bytes accessed | tf_op | source)
XLA Modules:
  0.0 115.6 jit_solution(13497569053944217718)
XLA Ops:
  0.0 1.3 %constant_dynamic-update-slice_fusion.1 = bf16[768,1024]{1,0:T(8,128)(2,1)S(1)} fusion(bf16[384,1024]{1,0:T(8,128)(2,1)} %param.1), kind=kLoop, calls=%fused_computation.22 | loop fusion | bytes 1572864
  1.3 1.2 %collective-permute-done = bf16[384,1024]{1,0:T(8,128)(2,1)S(1)} collective-permute-done((bf16[384,1024]{1,0:T(8,128)(2,1)}, bf16[384,1024]{1,0:T(8,128)(2,1)S(1)}, u32[]{:S(2)}, u32[]{:S(2)}) %collective-permute-start) | collective-permute-done | bytes 786464 | tf_op jit(solution)/shard_map/ppermute | solution.py:48
  2.6 5.9 %collective-permute-start.1 = (bf16[768,1024]{1,0:T(8,128)(2,1)S(1)}, bf16[768,1024]{1,0:T(8,128)(2,1)}, u32[]{:S(2)}, u32[]{:S(2)}) collective-permute-start(bf16[768,1024]{1,0:T(8,128)(2,1)S(1)} %constant_dynamic-update-slice_fusion.refs_0_), channel_id=1, source_target_pairs={{0,112},{1,17},{2,114},{3,19},{4,116},{5,21},{6,118},{7,23},{8,120... | collective-permute-start | bytes 4718600 | tf_op jit(solution)/shard_map/ppermute | solution.py:48
  8.5 0.7 collective-permute-start.2
  9.3 0.1 convert_reduce_fusion.1
  9.4 0.1 convert_reduce_fusion
  9.6 20.7 %all_to_all.20 = f32[16,16,128]{2,1,0:T(8,128)S(1)} all-to-all(f32[16,16,128]{2,1,0:T(8,128)S(1)} %broadcast_in_dim.8), channel_id=1, replica_groups=mesh['yh'=2,'z'=8,'x'=4,'yl'=2,'core'=2] {'yh','z'}, dimensions={0} | all-to-all | bytes 262144 | tf_op jit(solution)/shard_map/all_to_all | solution.py:171
  30.3 1.1 copy-done.2
  31.4 4.9 %collective-permute-start.6 = (bf16[768,1024]{1,0:T(8,128)(2,1)}, bf16[768,1024]{1,0:T(8,128)(2,1)S(1)}, u32[]{:S(2)}, u32[]{:S(2)}) collective-permute-start(bf16[768,1024]{1,0:T(8,128)(2,1)} %collective-permute-done.1.refs_1_), channel_id=1, source_target_pairs={{0,241},{1,16},{2,243},{3,18},{4,245},{5,20},{6,247},{7,22},{8,249... | collective-permute-start | bytes 4718600 | tf_op jit(solution)/shard_map/ppermute | solution.py:48
  36.3 1.4 %copy-done.1 = bf16[768,1024]{1,0:T(8,128)(2,1)S(1)} copy-done((bf16[768,1024]{1,0:T(8,128)(2,1)S(1)}, bf16[768,1024]{1,0:T(8,128)(2,1)}, u32[]{:S(2)}) %copy-start.1) | copy-done | bytes 1572888
  37.7 1.4 %copy-done.3 = bf16[768,1024]{1,0:T(8,128)(2,1)S(1)} copy-done((bf16[768,1024]{1,0:T(8,128)(2,1)S(1)}, bf16[768,1024]{1,0:T(8,128)(2,1)}, u32[]{:S(2)}) %copy-start.3) | copy-done | bytes 1572888
  39.1 4.5 %shard_map.17 = (bf16[384,2048]{1,0:T(8,128)(2,1)S(1)}, bf16[384,2048]{1,0:T(8,128)(2,1)S(1)}, f32[384,1280]{1,0:T(8,128)S(1)}) custom-call(s32[1]{0:T(128)} %bitcast.16.core_ref, f32[8,2048]{1,0:T(8,128)S(1)} %broadcast_in_dim.9.mean_ref, bf16[768,1024]{1,0:T(8,128)(2,1)S(1)} %copy-done.1, bf16[768,1024]{1,0:T(8,128)(2,1)} %collective-permute-done.1.refs_1_, ...), custom_call_target="tpu_custom_call" | custom-call | flops 1 | bytes 1 | tf_op jit(solution)/shard_map/pallas_call | solution.py:122
  43.6 1.2 %convert_element_type.35 = f16[384,1280]{1,0:T(8,128)(2,1)} convert(f32[384,1280]{1,0:T(8,128)S(1)} %get-tuple-element.35) | non-fusion elementwise | flops 491520 | bytes 2949120 | tf_op jit(solution)/shard_map/convert_element_type | solution.py:135
  44.8 0.2 copy-done.4
  45.1 5.0 %all-to-all-start.1 = ((f16[16,24,1280]{2,1,0:T(8,128)(2,1)}), f16[16,24,1280]{2,1,0:T(8,128)(2,1)}, u32[]{:S(2)}, u32[]{:S(2)}) async-start(f16[16,24,1280]{2,1,0:T(8,128)(2,1)} %bitcast.56), calls=%async_computation.1 | async-start | bytes 1966080 | tf_op jit(solution)/shard_map/all_to_all | solution.py:139
  50.1 1.6 %collective-permute-start.7 = (bf16[768,1024]{1,0:T(8,128)(2,1)}, bf16[768,1024]{1,0:T(8,128)(2,1)}, u32[]{:S(2)}, u32[]{:S(2)}) collective-permute-start(bf16[768,1024]{1,0:T(8,128)(2,1)} %collective-permute-done.1.refs_1_), channel_id=1, source_target_pairs={{0,112},{1,17},{2,114},{3,19},{4,116},{5,21},{6,118},{7,23},{8,120... | collective-permute-start | bytes 4718600 | tf_op jit(solution)/shard_map/ppermute | solution.py:48
  51.7 4.0 %collective-permute-done.6.refs_0_.refs_1_ = bf16[768,1024]{1,0:T(8,128)(2,1)S(1)} collective-permute-done((bf16[768,1024]{1,0:T(8,128)(2,1)}, bf16[768,1024]{1,0:T(8,128)(2,1)S(1)}, u32[]{:S(2)}, u32[]{:S(2)}) %collective-permute-start.6) | collective-permute-done | bytes 1572896 | tf_op jit(solution)/shard_map/ppermute | solution.py:48
  55.7 1.4 %copy-done.5 = bf16[384,2048]{1,0:T(8,128)(2,1)S(1)} copy-done((bf16[384,2048]{1,0:T(8,128)(2,1)S(1)}, bf16[384,2048]{1,0:T(8,128)(2,1)}, u32[]{:S(2)}) %copy-start.5) | copy-done | bytes 1572888
  57.1 2.9 %shard_map.18 = f32[384,1280]{1,0:T(8,128)S(1)} custom-call(s32[1]{0:T(128)} %bitcast.16.core_ref, f32[8,2048]{1,0:T(8,128)S(1)} %broadcast_in_dim.9.mean_ref, bf16[768,1024]{1,0:T(8,128)(2,1)S(1)} %collective-permute-done.6.refs_0_.refs_1_, bf16[384,2048]{1,0:T(8,128)(2,1)S(1)} %get-tuple-element.36.refs_1_.refs_2_, bf16[384,2048]{1,0:T(8,128)(2,1)S(1)} %copy-done.5), custom_call_target="tpu_custom_call" | custom-call | flops 1 | bytes 1 | tf_op jit(solution)/shard_map/pallas_call | solution.py:122
  60.0 1.1 convert_element_type.38
  61.1 4.2 %all-to-all-done.1 = f16[16,24,1280]{2,1,0:T(8,128)(2,1)} async-done(((f16[16,24,1280]{2,1,0:T(8,128)(2,1)}), f16[16,24,1280]{2,1,0:T(8,128)(2,1)}, u32[]{:S(2)}, u32[]{:S(2)}) %all-to-all-start.1) | async-done | bytes 983072 | tf_op jit(solution)/shard_map/all_to_all | solution.py:139
  65.3 5.2 %all-to-all-start.2 = ((f16[16,24,1280]{2,1,0:T(8,128)(2,1)}), f16[16,24,1280]{2,1,0:T(8,128)(2,1)}, u32[]{:S(2)}, u32[]{:S(2)}) async-start(f16[16,24,1280]{2,1,0:T(8,128)(2,1)} %bitcast.55), calls=%async_computation.2 | async-start | bytes 1966080 | tf_op jit(solution)/shard_map/all_to_all | solution.py:139
  70.5 0.8 slice.69
  71.3 0.1 copy.14
  71.5 1.5 %multiply_reduce_fusion.1.refs_0_ = f32[2,24,1152]{2,1,0:T(8,128)S(1)} fusion(f16[8,2,24,1280]{3,2,1,0:T(8,128)(2,1)} %bitcast.21, f32[8,2]{1,0:T(8,128)S(1)} %copy.9), kind=kLoop, calls=%fused_computation.1 | loop fusion | flops 1271808 | bytes 1105984 | tf_op jit(solution)/shard_map/reduce_sum | solution.py:146
  73.0 0.6 slice_bitcast_fusion.8
  73.6 1.2 %collective-permute-start.3 = (f32[24,384]{1,0:T(8,128)}, f32[24,384]{1,0:T(8,128)S(1)}, u32[]{:S(2)}, u32[]{:S(2)}) collective-permute-start(f32[24,384]{1,0:T(8,128)} %get-tuple-element.67), channel_id=1, source_target_pairs={{0,16},{1,17},{2,18},{3,19},{4,20},{5,21},{6,22},{7,23},{8,24},{9,... | collective-permute-start | bytes 110600 | tf_op jit(solution)/shard_map/ppermute | solution.py:48
  74.8 2.8 %collective-permute-start.4 = (f32[24,384]{1,0:T(8,128)}, f32[24,384]{1,0:T(8,128)S(1)}, u32[]{:S(2)}, u32[]{:S(2)}) collective-permute-start(f32[24,384]{1,0:T(8,128)} %get-tuple-element.66), channel_id=1, source_target_pairs={{0,112},{1,113},{2,114},{3,115},{4,116},{5,117},{6,118},{7,119},{8... | collective-permute-start | bytes 110600 | tf_op jit(solution)/shard_map/ppermute | solution.py:48
  77.6 2.0 %collective-permute-start.5 = (f32[24,384]{1,0:T(8,128)}, f32[24,384]{1,0:T(8,128)S(1)}, u32[]{:S(2)}, u32[]{:S(2)}) collective-permute-start(f32[24,384]{1,0:T(8,128)} %get-tuple-element.65), channel_id=1, source_target_pairs={{0,128},{1,129},{2,130},{3,131},{4,132},{5,133},{6,134},{7,135},{8... | collective-permute-start | bytes 110600 | tf_op jit(solution)/shard_map/ppermute | solution.py:48
  79.6 3.4 %shard_map.19 = f32[384,896]{1,0:T(8,128)S(1)} custom-call(s32[1]{0:T(128)} %bitcast.16.core_ref, f32[8,2048]{1,0:T(8,128)S(1)} %broadcast_in_dim.9.mean_ref, bf16[768,1024]{1,0:T(8,128)(2,1)} %collective-permute-done.7.refs_0_, bf16[768,1024]{1,0:T(8,128)(2,1)S(1)} %collective-permute-done.6.refs_0_.refs_1_, ...), custom_call_target="tpu_custom_call" | custom-call | flops 1 | bytes 1 | tf_op jit(solution)/shard_map/pallas_call | solution.py:122
  83.0 0.9 convert_element_type.39
  84.0 0.3 all-to-all-done.2
  84.3 0.5 collective-permute-done.5.refs_3_
  84.8 0.8 slice.74
  85.6 0.1 copy.15
  85.8 6.1 %all-to-all-start.3 = ((f16[16,24,896]{2,1,0:T(8,128)(2,1)}), f16[16,24,896]{2,1,0:T(8,128)(2,1)S(1)}, u32[]{:S(2)}, u32[]{:S(2)}) async-start(f16[16,24,896]{2,1,0:T(8,128)(2,1)} %bitcast.27), calls=%async_computation.3 | async-start | bytes 1376256 | tf_op jit(solution)/shard_map/all_to_all | solution.py:139
  91.9 1.4 %multiply_reduce_fusion.refs_4_ = f32[2,24,1152]{2,1,0:T(8,128)S(1)} fusion(f16[8,2,24,1280]{3,2,1,0:T(8,128)(2,1)} %bitcast.28, f32[8,2]{1,0:T(8,128)S(1)} %copy.11), kind=kLoop, calls=%fused_computation | loop fusion | flops 1271808 | bytes 1105984 | tf_op jit(solution)/shard_map/reduce_sum | solution.py:146
  93.4 4.0 %collective-permute-start.8 = (f32[24,768]{1,0:T(8,128)S(1)}, f32[24,768]{1,0:T(8,128)S(1)}, u32[]{:S(2)}, u32[]{:S(2)}) collective-permute-start(f32[24,768]{1,0:T(8,128)S(1)} %pad_maximum_fusion), channel_id=1, source_target_pairs={{0,96},{1,97},{2,98},{3,99},{4,100},{5,101},{6,102},{7,103},{8,104... | collective-permute-start | bytes 221192 | tf_op jit(solution)/shard_map/ppermute | solution.py:48
  97.4 0.4 collective-permute-start.9
  97.8 3.4 %collective-permute-start.10 = (f32[24,384]{1,0:T(8,128)S(1)}, f32[24,384]{1,0:T(8,128)S(1)}, u32[]{:S(2)}, u32[]{:S(2)}) collective-permute-start(f32[24,384]{1,0:T(8,128)S(1)} %get-tuple-element.60), channel_id=1, source_target_pairs={{0,16},{1,17},{2,18},{3,19},{4,20},{5,21},{6,22},{7,23},{8,24},{9,... | collective-permute-start | bytes 110600 | tf_op jit(solution)/shard_map/ppermute | solution.py:48
  101.2 1.8 %collective-permute-start.11 = (f32[24,384]{1,0:T(8,128)S(1)}, f32[24,384]{1,0:T(8,128)S(1)}, u32[]{:S(2)}, u32[]{:S(2)}) collective-permute-start(f32[24,384]{1,0:T(8,128)S(1)} %get-tuple-element.59), channel_id=1, source_target_pairs={{0,112},{1,113},{2,114},{3,115},{4,116},{5,117},{6,118},{7,119},{8... | collective-permute-start | bytes 110600 | tf_op jit(solution)/shard_map/ppermute | solution.py:48
  103.0 4.4 %collective-permute-done.10.refs_7_ = f32[24,384]{1,0:T(8,128)S(1)} collective-permute-done((f32[24,384]{1,0:T(8,128)S(1)}, f32[24,384]{1,0:T(8,128)S(1)}, u32[]{:S(2)}, u32[]{:S(2)}) %collective-permute-start.10) | collective-permute-done | bytes 36896 | tf_op jit(solution)/shard_map/ppermute | solution.py:48
  107.4 0.3 collective-permute-done.9.refs_6_
  107.7 0.1 copy.16
  107.9 0.2 multiply_reduce_fusion.2.refs_9_
  108.2 0.9 collective-permute-start.12
  109.1 5.1 %collective-permute-done.12.refs_10_ = f32[24,768]{1,0:T(8,128)S(1)} collective-permute-done((f32[24,768]{1,0:T(8,128)S(1)}, f32[24,768]{1,0:T(8,128)S(1)}, u32[]{:S(2)}, u32[]{:S(2)}) %collective-permute-start.12) | collective-permute-done | bytes 73760 | tf_op jit(solution)/shard_map/ppermute | solution.py:48
  114.2 1.4 %shard_map.20 = f32[24,6144]{1,0:T(8,128)} custom-call(s32[16]{0:T(128)S(1)} %stack.67.place_ref, f32[2,24,1152]{2,1,0:T(8,128)S(1)} %multiply_reduce_fusion.1.refs_0_, f32[24,384]{1,0:T(8,128)S(1)} %collective-permute-done.3.refs_1_, f32[24,384]{1,0:T(8,128)S(1)} %collective-permute-done.4.refs_2_, f32[24,384]{1,0:T(8,128)S(1)} %collective-permute-done.5.refs_3_, ...), custom_call_target="tpu_custom_call" | custom-call | tf_op jit(solution)/shard_map/pallas_call | solution.py:217
  (37 shorter events, 0.6 us)
Async XLA Ops:
  0.0 9.3 %copy-start.6 = (bf16[384,1024]{1,0:T(8,128)(2,1)S(1)}, bf16[384,1024]{1,0:T(8,128)(2,1)}, u32[]{:S(2)}) copy-start(bf16[384,1024]{1,0:T(8,128)(2,1)} %param.1) | copy-start | bytes 2359300
  0.0 2.5 %collective-permute-start = (bf16[384,1024]{1,0:T(8,128)(2,1)}, bf16[384,1024]{1,0:T(8,128)(2,1)S(1)}, u32[]{:S(2)}, u32[]{:S(2)}) collective-permute-start(bf16[384,1024]{1,0:T(8,128)(2,1)} %param.1), channel_id=1, source_target_pairs={{0,1},{1,0},{2,3},{3,2},{4,5},{5,4},{6,7},{7,6},{8,9},{9,8},{10,11... | collective-permute-start | bytes 2359304 | tf_op jit(solution)/shard_map/ppermute | solution.py:48
  2.6 27.7 %copy-start = (bf16[768,1024]{1,0:T(8,128)(2,1)}, bf16[768,1024]{1,0:T(8,128)(2,1)S(1)}, u32[]{:S(2)}) copy-start(bf16[768,1024]{1,0:T(8,128)(2,1)S(1)} %constant_dynamic-update-slice_fusion.refs_0_) | copy-start | bytes 4718596
  2.6 27.7 %collective-permute-start.1 = (bf16[768,1024]{1,0:T(8,128)(2,1)S(1)}, bf16[768,1024]{1,0:T(8,128)(2,1)}, u32[]{:S(2)}, u32[]{:S(2)}) collective-permute-start(bf16[768,1024]{1,0:T(8,128)(2,1)S(1)} %constant_dynamic-update-slice_fusion.refs_0_), channel_id=1, source_target_pairs={{0,112},{1,17},{2,114},{3,19},{4,116},{5,21},{6,118},{7,23},{8,120... | collective-permute-start | bytes 4718600 | tf_op jit(solution)/shard_map/ppermute | solution.py:48
  8.5 21.8 %collective-permute-start.2 = (bf16[768,1024]{1,0:T(8,128)(2,1)S(1)}, bf16[768,1024]{1,0:T(8,128)(2,1)S(1)}, u32[]{:S(2)}, u32[]{:S(2)}) collective-permute-start(bf16[768,1024]{1,0:T(8,128)(2,1)S(1)} %constant_dynamic-update-slice_fusion.refs_0_), channel_id=1, source_target_pairs={{1,129},{3,131},{5,133},{7,135},{9,137},{11,139},{13,141},{15,143}... | collective-permute-start | bytes 4718600 | tf_op jit(solution)/shard_map/ppermute | solution.py:48
  30.3 1.1 copy-start.2
  31.4 24.3 %collective-permute-start.6 = (bf16[768,1024]{1,0:T(8,128)(2,1)}, bf16[768,1024]{1,0:T(8,128)(2,1)S(1)}, u32[]{:S(2)}, u32[]{:S(2)}) collective-permute-start(bf16[768,1024]{1,0:T(8,128)(2,1)} %collective-permute-done.1.refs_1_), channel_id=1, source_target_pairs={{0,241},{1,16},{2,243},{3,18},{4,245},{5,20},{6,247},{7,22},{8,249... | collective-permute-start | bytes 4718600 | tf_op jit(solution)/shard_map/ppermute | solution.py:48
  36.3 1.4 %copy-start.1 = (bf16[768,1024]{1,0:T(8,128)(2,1)S(1)}, bf16[768,1024]{1,0:T(8,128)(2,1)}, u32[]{:S(2)}) copy-start(bf16[768,1024]{1,0:T(8,128)(2,1)} %copy-done) | copy-start | bytes 4718596
  37.7 1.4 %copy-start.3 = (bf16[768,1024]{1,0:T(8,128)(2,1)S(1)}, bf16[768,1024]{1,0:T(8,128)(2,1)}, u32[]{:S(2)}) copy-start(bf16[768,1024]{1,0:T(8,128)(2,1)} %copy-done.2) | copy-start | bytes 4718596
  43.6 1.4 %copy-start.4 = (bf16[384,2048]{1,0:T(8,128)(2,1)}, bf16[384,2048]{1,0:T(8,128)(2,1)S(1)}, u32[]{:S(2)}) copy-start(bf16[384,2048]{1,0:T(8,128)(2,1)S(1)} %get-tuple-element.38.refs_2_) | copy-start | bytes 4718596
  45.1 20.2 %all-to-all-start.1 = ((f16[16,24,1280]{2,1,0:T(8,128)(2,1)}), f16[16,24,1280]{2,1,0:T(8,128)(2,1)}, u32[]{:S(2)}, u32[]{:S(2)}) async-start(f16[16,24,1280]{2,1,0:T(8,128)(2,1)} %bitcast.56), calls=%async_computation.1 | async-start | bytes 1966080 | tf_op jit(solution)/shard_map/all_to_all | solution.py:139
  50.1 29.5 %collective-permute-start.7 = (bf16[768,1024]{1,0:T(8,128)(2,1)}, bf16[768,1024]{1,0:T(8,128)(2,1)}, u32[]{:S(2)}, u32[]{:S(2)}) collective-permute-start(bf16[768,1024]{1,0:T(8,128)(2,1)} %collective-permute-done.1.refs_1_), channel_id=1, source_target_pairs={{0,112},{1,17},{2,114},{3,19},{4,116},{5,21},{6,118},{7,23},{8,120... | collective-permute-start | bytes 4718600 | tf_op jit(solution)/shard_map/ppermute | solution.py:48
  55.7 1.4 %copy-start.5 = (bf16[384,2048]{1,0:T(8,128)(2,1)S(1)}, bf16[384,2048]{1,0:T(8,128)(2,1)}, u32[]{:S(2)}) copy-start(bf16[384,2048]{1,0:T(8,128)(2,1)} %copy-done.4) | copy-start | bytes 4718596
  65.3 19.0 %all-to-all-start.2 = ((f16[16,24,1280]{2,1,0:T(8,128)(2,1)}), f16[16,24,1280]{2,1,0:T(8,128)(2,1)}, u32[]{:S(2)}, u32[]{:S(2)}) async-start(f16[16,24,1280]{2,1,0:T(8,128)(2,1)} %bitcast.55), calls=%async_computation.2 | async-start | bytes 1966080 | tf_op jit(solution)/shard_map/all_to_all | solution.py:139
  73.6 10.7 %collective-permute-start.3 = (f32[24,384]{1,0:T(8,128)}, f32[24,384]{1,0:T(8,128)S(1)}, u32[]{:S(2)}, u32[]{:S(2)}) collective-permute-start(f32[24,384]{1,0:T(8,128)} %get-tuple-element.67), channel_id=1, source_target_pairs={{0,16},{1,17},{2,18},{3,19},{4,20},{5,21},{6,22},{7,23},{8,24},{9,... | collective-permute-start | bytes 110600 | tf_op jit(solution)/shard_map/ppermute | solution.py:48
  74.8 9.5 %collective-permute-start.4 = (f32[24,384]{1,0:T(8,128)}, f32[24,384]{1,0:T(8,128)S(1)}, u32[]{:S(2)}, u32[]{:S(2)}) collective-permute-start(f32[24,384]{1,0:T(8,128)} %get-tuple-element.66), channel_id=1, source_target_pairs={{0,112},{1,113},{2,114},{3,115},{4,116},{5,117},{6,118},{7,119},{8... | collective-permute-start | bytes 110600 | tf_op jit(solution)/shard_map/ppermute | solution.py:48
  77.6 7.3 %collective-permute-start.5 = (f32[24,384]{1,0:T(8,128)}, f32[24,384]{1,0:T(8,128)S(1)}, u32[]{:S(2)}, u32[]{:S(2)}) collective-permute-start(f32[24,384]{1,0:T(8,128)} %get-tuple-element.65), channel_id=1, source_target_pairs={{0,128},{1,129},{2,130},{3,131},{4,132},{5,133},{6,134},{7,135},{8... | collective-permute-start | bytes 110600 | tf_op jit(solution)/shard_map/ppermute | solution.py:48
  85.8 21.9 %all-to-all-start.3 = ((f16[16,24,896]{2,1,0:T(8,128)(2,1)}), f16[16,24,896]{2,1,0:T(8,128)(2,1)S(1)}, u32[]{:S(2)}, u32[]{:S(2)}) async-start(f16[16,24,896]{2,1,0:T(8,128)(2,1)} %bitcast.27), calls=%async_computation.3 | async-start | bytes 1376256 | tf_op jit(solution)/shard_map/all_to_all | solution.py:139
  93.4 14.0 %collective-permute-start.8 = (f32[24,768]{1,0:T(8,128)S(1)}, f32[24,768]{1,0:T(8,128)S(1)}, u32[]{:S(2)}, u32[]{:S(2)}) collective-permute-start(f32[24,768]{1,0:T(8,128)S(1)} %pad_maximum_fusion), channel_id=1, source_target_pairs={{0,96},{1,97},{2,98},{3,99},{4,100},{5,101},{6,102},{7,103},{8,104... | collective-permute-start | bytes 221192 | tf_op jit(solution)/shard_map/ppermute | solution.py:48
  97.4 10.3 %collective-permute-start.9 = (f32[24,768]{1,0:T(8,128)S(1)}, f32[24,768]{1,0:T(8,128)S(1)}, u32[]{:S(2)}, u32[]{:S(2)}) collective-permute-start(f32[24,768]{1,0:T(8,128)S(1)} %pad_maximum_fusion.1), channel_id=1, source_target_pairs={{0,160},{1,161},{2,162},{3,163},{4,164},{5,165},{6,166},{7,167},{8... | collective-permute-start | bytes 221192 | tf_op jit(solution)/shard_map/ppermute | solution.py:48
  97.8 9.6 %collective-permute-start.10 = (f32[24,384]{1,0:T(8,128)S(1)}, f32[24,384]{1,0:T(8,128)S(1)}, u32[]{:S(2)}, u32[]{:S(2)}) collective-permute-start(f32[24,384]{1,0:T(8,128)S(1)} %get-tuple-element.60), channel_id=1, source_target_pairs={{0,16},{1,17},{2,18},{3,19},{4,20},{5,21},{6,22},{7,23},{8,24},{9,... | collective-permute-start | bytes 110600 | tf_op jit(solution)/shard_map/ppermute | solution.py:48
  101.2 6.1 %collective-permute-start.11 = (f32[24,384]{1,0:T(8,128)S(1)}, f32[24,384]{1,0:T(8,128)S(1)}, u32[]{:S(2)}, u32[]{:S(2)}) collective-permute-start(f32[24,384]{1,0:T(8,128)S(1)} %get-tuple-element.59), channel_id=1, source_target_pairs={{0,112},{1,113},{2,114},{3,115},{4,116},{5,117},{6,118},{7,119},{8... | collective-permute-start | bytes 110600 | tf_op jit(solution)/shard_map/ppermute | solution.py:48
  108.2 6.1 %collective-permute-start.12 = (f32[24,768]{1,0:T(8,128)S(1)}, f32[24,768]{1,0:T(8,128)S(1)}, u32[]{:S(2)}, u32[]{:S(2)}) collective-permute-start(f32[24,768]{1,0:T(8,128)S(1)} %pad_maximum_fusion.2), channel_id=1, source_target_pairs={{0,96},{1,97},{2,98},{3,99},{4,100},{5,101},{6,102},{7,103},{8,104... | collective-permute-start | bytes 221192 | tf_op jit(solution)/shard_map/ppermute | solution.py:48

commit v4 on v3

--- a/solution.py
+++ b/solution.py
@@ -72,7 +72,6 @@
     raw_refs, refs = refs[: len(raw)], refs[len(raw) :]
     held_refs, kept_refs, out_ref = refs[: len(held)], refs[len(held) : -1], refs[-1]
     rows, width = raw_refs[0].shape[0] // 2, raw_refs[0].shape[1]
-    cols = out_ref.shape[1] - 128
     on_core_1 = core_ref[0] == 1
 
     terms = [[] for _ in group]
@@ -102,20 +101,26 @@
                     left, right, (((1,), (1,)), ((), ())), preferred_element_type=jnp.float32
                 )
             )
+    totals = [first + second for first, second in terms]
     largest = jnp.zeros((1, 1), jnp.float32)
-    for n, (first, second) in enumerate(terms):
-        total = first + second
-        out_ref[:, n * rows : (n + 1) * rows] = total
+    for total in totals:
         largest = jnp.maximum(largest, jnp.max(jnp.abs(total), keepdims=True))
     exponent = jnp.clip(jnp.ceil(jnp.log2(largest)), -100.0, 20.0)
-    out_ref[:, :cols] *= jnp.exp2(14.0 - exponent)
-    out_ref[:, cols:] = jnp.broadcast_to(exponent, (rows, 128))
+    factor = jnp.exp2(14.0 - exponent)
+    tile = 0
+    for total in totals:
+        scaled = (total * factor).reshape(16, rows // 128, 8, rows)
+        for deep in range(rows // 128):
+            for begin in range(0, rows, 128):
+                out_ref[:, tile] = scaled[:, deep, :, begin : begin + 128]
+                tile += 1
+    out_ref[:, tile] = jnp.broadcast_to(exponent.reshape(1, 1, 1), (16, 8, 128))
 
 
 def multiply(core, mean, raw, held, kept, group, scale):
     first = next(iter(raw.values()))[0]
     rows, width = first.shape[0] // 2, 2 * first.shape[1]
-    cols = len(group) * rows
+    tiles = len(group) * (rows // 128) ** 2 + 1
     whole = pl.BlockSpec(memory_space=pltpu.VMEM)
     centred = jax.ShapeDtypeStruct((rows, width), jnp.bfloat16)
     names = tuple((name, flip) for name, (_, flip) in raw.items())
@@ -123,35 +128,33 @@
         functools.partial(multiply_kernel, names, tuple(held), kept, group, scale),
         in_specs=[pl.BlockSpec(memory_space=pltpu.SMEM)] + [whole] * (1 + len(raw) + len(held)),
         out_specs=[whole] * (len(kept) + 1),
-        out_shape=[*(centred for _ in kept), jax.ShapeDtypeStruct((rows, cols + 128), jnp.float32)],
+        out_shape=[*(centred for _ in kept), jax.ShapeDtypeStruct((16, tiles, 8, 128), jnp.float32)],
         compiler_params=pltpu.CompilerParams(vmem_limit_bytes=VMEM_MIB * 2**20),
         cost_estimate=pl.CostEstimate(flops=1, bytes_accessed=1, transcendentals=0),
     )(core, mean, *(block for block, _ in raw.values()), *held.values())
     return dict(zip(kept, blocks)), value
 
 
-def message_of(value):
-    rows, width = value.shape
-    return value.astype(jnp.float16).reshape(16, rows // 16, width)
-
-
 def scatter_over_par(message):
     return lax.all_to_all(message, PAR, 0, 0)
 
 
 def gather_sum(message):
-    _, chunk, width = message.shape
-    message = message.reshape(8, 2, chunk, width)
-    factor = jnp.exp2(message[:, :, :1, width - 128 : width - 127].astype(jnp.float32) - 14.0)
-    return jnp.sum(message[:, :, :, : width - 128].astype(jnp.float32) * factor, axis=0)
+    message = message.reshape(8, 2, *message.shape[1:])
+    factor = jnp.exp2(message[:, :, -1:].astype(jnp.float32) - 14.0)
+    return jnp.sum(message[:, :, :-1].astype(jnp.float32) * factor, axis=0)
 
 
 def place_kernel(pieces, place_ref, *refs):
     out_ref = refs[-1]
-    for n, (source, index) in enumerate(pieces):
-        value = refs[source][index]
-        width = value.shape[1]
-        out_ref[:, pl.ds(pl.multiple_of(place_ref[n] * width, 128), width)] = value
+    for n, (source, index, count) in enumerate(pieces):
+        side = round(count**0.5)
+        start = place_ref[n] * (side * 128)
+        for tile in range(count):
+            deep, along = divmod(tile, side)
+            column = pl.multiple_of(start + along * 128, 128)
+            value = refs[source][(*index[:-1], index[-1] + tile)]
+            out_ref[deep * 8 : deep * 8 + 8, pl.ds(column, 128)] = value
 
 
 def local(block):
@@ -177,17 +180,18 @@
 
     raw = {"S0": (own, False), "S1": (near, False), "T1": (mate, False)}
     held, value = multiply(core, mean, raw, {}, ("S0", "S1"), GROUPS[0], scale)
-    messages = [scatter_over_par(message_of(value))]
+    messages = [scatter_over_par(value.astype(jnp.float16))]
     near, held["S1"] = lax.optimization_barrier((near, held["S1"]))
     far = permute(near, along_z)
     _, value = multiply(core, mean, {"T3": (crossed, True)}, held, (), GROUPS[1], scale)
-    messages.append(scatter_over_par(message_of(value)))
+    messages.append(scatter_over_par(value.astype(jnp.float16)))
     far, crossed, _ = lax.optimization_barrier((far, crossed, value))
     raw = {"S2": (far, False), "T3": (crossed, True)}
     _, value = multiply(core, mean, raw, {"S0": held["S0"]}, (), GROUPS[2], scale)
-    messages[1], message = lax.optimization_barrier((messages[1], message_of(value)))
+    messages[1], message = lax.optimization_barrier((messages[1], value.astype(jnp.float16)))
     messages.append(scatter_over_par(message))
 
+    tiles = (rows // 128) ** 2
     sources, pieces, places = [], [], []
     for group, message in zip(GROUPS, messages):
         *sources, message = lax.optimization_barrier((*sources, message))
@@ -195,22 +199,21 @@
         sources.append(done)
         leads = {}
         for k, pairs in enumerate(group):
-            across = slice(k * rows, (k + 1) * rows)
             for c, (left, right) in enumerate(pairs):
                 a, b = SLOTS[left][c], SLOTS[right][c]
                 offset = (b[0] - a[0]) & 1, (b[1] - a[1]) & 7
                 lead = a[0] & 1, a[1] & 7
                 if lead == (0, 0):
-                    pieces.append((len(sources) - 1, (c, slice(None), across)))
+                    pieces.append((len(sources) - 1, (c, k * tiles), tiles))
                     places.append(offset)
                 else:
-                    leads.setdefault(lead, []).append((offset, done[c, :, across]))
+                    value = done[c, k * tiles : (k + 1) * tiles]
+                    leads.setdefault(lead, []).append((offset, value))
         for lead, items in leads.items():
-            value = jnp.concatenate([value for _, value in items], axis=1)
+            value = jnp.concatenate([value for _, value in items], axis=0)
             sources.append(permute(value, to_offset(*lead)))
             for n, (offset, _) in enumerate(items):
-                across = slice(n * rows, (n + 1) * rows)
-                pieces.append((len(sources) - 1, (slice(None), across)))
+                pieces.append((len(sources) - 1, (n * tiles,), tiles))
                 places.append(offset)
     place = jnp.stack([((sy + dy) & 1) * 8 + ((sz + dz) & 7) for dy, dz in places])
     whole = pl.BlockSpec(memory_space=pltpu.VMEM)

time: 116 us -> 114 us (0.983)
  waiting for transfers between devices: 20.1 us -> 17.9 us
  local copies, waits for them, and re-layouts: 9.79 us -> 8.59 us
    ppermute x13, waiting for transfers between devices: 15.6 us -> 13.7 us  [permute(): return lax.ppermute(value, tuple(AXES), pairs)]
    slice x3 -> x0, local copies, waits for them, and re-layouts: 1.54 us -> none  [gather_sum(): message[:, :, :1, width - 128:width - 127].astype(jnp.float32) - 14.0]
    mul x3, other arithmetic: 0.03 us -> 1.58 us  [gather_sum(): return jnp.sum(message[:, :, :-1].astype(jnp.float32) * factor, axis=0)]
    unnamed x18 -> x15, local copies, waits for them, and re-layouts: 7.16 us -> 7.76 us
  transfers between devices with their start and end apart: 16 -> 16, of which waited for: 8 -> 7; matrix products, arithmetic and copies ran while one was open for 8% -> 8% of each run, Pallas kernels for 9% -> 9%
where the time goes in v4:
time: 114 us; the launch traced here: 113 us
  starting transfers between devices  46.1 us (40%)
  blocking collectives  20.7 us (18%)
  waiting for transfers between devices  17.9 us (16%)
  Pallas kernels  12.2 us (11%)
  local copies, waits for them, and re-layouts  8.59 us (8%)
  other arithmetic  7.83 us (7%)
    ppermute x13, starting transfers between devices, permute(): return lax.ppermute(value, tuple(AXES), pairs)  29.4 us
    all_to_all x1, blocking collectives, local(): lax.all_to_all(jnp.broadcast_to(sums, (blocks, *sums.shape)), SAMP, 0, 0)  20.7 us
    all_to_all x3, starting transfers between devices, scatter_over_par(): return lax.all_to_all(message, PAR, 0, 0)  16.7 us
    ppermute x13, waiting for transfers between devices, permute(): return lax.ppermute(value, tuple(AXES), pairs)  13.7 us
    pallas_call x3, Pallas kernels, multiply(): pl.pallas_call(functools.partial(multiply_kernel, names, tuple(held), kep...  10.8 us
    unnamed x15, local copies, waits for them, and re-layouts  7.76 us
    all_to_all x3, waiting for transfers between devices, scatter_over_par(): return lax.all_to_all(message, PAR, 0, 0)  4.17 us
    reduce_sum x3, other arithmetic, gather_sum(): return jnp.sum(message[:, :, :-1].astype(jnp.float32) * factor, axis=0)  2.88 us
  transfers between devices with their start and end apart: 16, of which 7 were waited for; matrix products, arithmetic and copies ran while one was open for 8% of the time, Pallas kernels for 9%

profile of v4, /device:TPU:2, one launch (start us, length us, event | category | flops | bytes accessed | tf_op | source)
XLA Modules:
  0.0 113.5 jit_solution(5704913531130129533)
XLA Ops:
  0.0 1.3 %constant_dynamic-update-slice_fusion.1 = bf16[768,1024]{1,0:T(8,128)(2,1)S(1)} fusion(bf16[384,1024]{1,0:T(8,128)(2,1)} %param.1), kind=kLoop, calls=%fused_computation.25 | loop fusion | bytes 1572864
  1.3 1.2 %collective-permute-done = bf16[384,1024]{1,0:T(8,128)(2,1)S(1)} collective-permute-done((bf16[384,1024]{1,0:T(8,128)(2,1)}, bf16[384,1024]{1,0:T(8,128)(2,1)S(1)}, u32[]{:S(2)}, u32[]{:S(2)}) %collective-permute-start) | collective-permute-done | bytes 786464 | tf_op jit(solution)/shard_map/ppermute | solution.py:48
  2.5 0.1 constant_dynamic-update-slice_fusion.refs_0_
  2.6 5.9 %collective-permute-start.1 = (bf16[768,1024]{1,0:T(8,128)(2,1)S(1)}, bf16[768,1024]{1,0:T(8,128)(2,1)}, u32[]{:S(2)}, u32[]{:S(2)}) collective-permute-start(bf16[768,1024]{1,0:T(8,128)(2,1)S(1)} %constant_dynamic-update-slice_fusion.refs_0_), channel_id=1, source_target_pairs={{0,112},{1,17},{2,114},{3,19},{4,116},{5,21},{6,118},{7,23},{8,120... | collective-permute-start | bytes 4718600 | tf_op jit(solution)/shard_map/ppermute | solution.py:48
  8.5 0.7 collective-permute-start.2
  9.3 0.1 convert_reduce_fusion.1
  9.4 0.1 convert_reduce_fusion
  9.6 20.7 %all_to_all.20 = f32[16,16,128]{2,1,0:T(8,128)S(1)} all-to-all(f32[16,16,128]{2,1,0:T(8,128)S(1)} %broadcast_in_dim.8), channel_id=1, replica_groups=mesh['yh'=2,'z'=8,'x'=4,'yl'=2,'core'=2] {'yh','z'}, dimensions={0} | all-to-all | bytes 262144 | tf_op jit(solution)/shard_map/all_to_all | solution.py:174
  30.2 0.0 collective-permute-done.1.refs_1_
  30.3 1.1 %copy-done.2 = bf16[768,1024]{1,0:T(8,128)(2,1)} copy-done((bf16[768,1024]{1,0:T(8,128)(2,1)}, bf16[768,1024]{1,0:T(8,128)(2,1)S(1)}, u32[]{:S(2)}) %copy-start.2) | copy-done | bytes 1572888
  31.4 4.9 %collective-permute-start.6 = (bf16[768,1024]{1,0:T(8,128)(2,1)}, bf16[768,1024]{1,0:T(8,128)(2,1)S(1)}, u32[]{:S(2)}, u32[]{:S(2)}) collective-permute-start(bf16[768,1024]{1,0:T(8,128)(2,1)} %collective-permute-done.1.refs_1_), channel_id=1, source_target_pairs={{0,241},{1,16},{2,243},{3,18},{4,245},{5,20},{6,247},{7,22},{8,249... | collective-permute-start | bytes 4718600 | tf_op jit(solution)/shard_map/ppermute | solution.py:48
  36.3 1.4 %copy-done.1 = bf16[768,1024]{1,0:T(8,128)(2,1)S(1)} copy-done((bf16[768,1024]{1,0:T(8,128)(2,1)S(1)}, bf16[768,1024]{1,0:T(8,128)(2,1)}, u32[]{:S(2)}) %copy-start.1) | copy-done | bytes 1572888
  37.7 1.4 %copy-done.3 = bf16[768,1024]{1,0:T(8,128)(2,1)S(1)} copy-done((bf16[768,1024]{1,0:T(8,128)(2,1)S(1)}, bf16[768,1024]{1,0:T(8,128)(2,1)}, u32[]{:S(2)}) %copy-start.3) | copy-done | bytes 1572888
  39.1 4.5 %shard_map.17 = (bf16[384,2048]{1,0:T(8,128)(2,1)S(1)}, bf16[384,2048]{1,0:T(8,128)(2,1)S(1)}, f32[16,28,8,128]{3,2,1,0:T(8,128)S(1)}) custom-call(s32[1]{0:T(128)} %bitcast.16.core_ref, f32[8,2048]{1,0:T(8,128)S(1)} %broadcast_in_dim.9.mean_ref, bf16[768,1024]{1,0:T(8,128)(2,1)S(1)} %copy-done.1, bf16[768,1024]{1,0:T(8,128)(2,1)} %collective-permute-done.1.refs_1_, ...), custom_call_target="tpu_custom_call" | custom-call | flops 1 | bytes 1 | tf_op jit(solution)/shard_map/pallas_call | solution.py:127
  43.6 1.1 %copy-done.4 = bf16[384,2048]{1,0:T(8,128)(2,1)} copy-done((bf16[384,2048]{1,0:T(8,128)(2,1)}, bf16[384,2048]{1,0:T(8,128)(2,1)S(1)}, u32[]{:S(2)}) %copy-start.4) | copy-done | bytes 1572888
  44.8 1.1 convert_element_type.35
  45.8 5.0 %all-to-all-start.1 = ((f16[16,28,8,128]{3,2,1,0:T(8,128)(2,1)}), f16[16,28,8,128]{3,2,1,0:T(8,128)(2,1)}, u32[]{:S(2)}, u32[]{:S(2)}) async-start(f16[16,28,8,128]{3,2,1,0:T(8,128)(2,1)} %convert_element_type.35), calls=%async_computation.1 | async-start | bytes 1835008 | tf_op jit(solution)/shard_map/all_to_all | solution.py:139
  50.8 1.6 %collective-permute-start.7 = (bf16[768,1024]{1,0:T(8,128)(2,1)}, bf16[768,1024]{1,0:T(8,128)(2,1)}, u32[]{:S(2)}, u32[]{:S(2)}) collective-permute-start(bf16[768,1024]{1,0:T(8,128)(2,1)} %collective-permute-done.1.refs_1_), channel_id=1, source_target_pairs={{0,112},{1,17},{2,114},{3,19},{4,116},{5,21},{6,118},{7,23},{8,120... | collective-permute-start | bytes 4718600 | tf_op jit(solution)/shard_map/ppermute | solution.py:48
  52.5 2.8 %collective-permute-done.6.refs_0_.refs_1_ = bf16[768,1024]{1,0:T(8,128)(2,1)S(1)} collective-permute-done((bf16[768,1024]{1,0:T(8,128)(2,1)}, bf16[768,1024]{1,0:T(8,128)(2,1)S(1)}, u32[]{:S(2)}, u32[]{:S(2)}) %collective-permute-start.6) | collective-permute-done | bytes 1572896 | tf_op jit(solution)/shard_map/ppermute | solution.py:48
  55.2 1.4 %copy-done.5 = bf16[384,2048]{1,0:T(8,128)(2,1)S(1)} copy-done((bf16[384,2048]{1,0:T(8,128)(2,1)S(1)}, bf16[384,2048]{1,0:T(8,128)(2,1)}, u32[]{:S(2)}) %copy-start.5) | copy-done | bytes 1572888
  56.6 2.9 %shard_map.18 = f32[16,28,8,128]{3,2,1,0:T(8,128)S(1)} custom-call(s32[1]{0:T(128)} %bitcast.16.core_ref, f32[8,2048]{1,0:T(8,128)S(1)} %broadcast_in_dim.9.mean_ref, bf16[768,1024]{1,0:T(8,128)(2,1)S(1)} %collective-permute-done.6.refs_0_.refs_1_, bf16[384,2048]{1,0:T(8,128)(2,1)S(1)} %get-tuple-element.36.refs_1_.refs_2_, bf16[384,2048]{1,0:T(8,128)(2,1)S(1)} %copy-done.5), custom_call_target="tpu_custom_call" | custom-call | flops 1 | bytes 1 | tf_op jit(solution)/shard_map/pallas_call | solution.py:127
  59.5 1.1 convert_element_type.38
  60.6 4.0 %all-to-all-done.1 = f16[16,28,8,128]{3,2,1,0:T(8,128)(2,1)} async-done(((f16[16,28,8,128]{3,2,1,0:T(8,128)(2,1)}), f16[16,28,8,128]{3,2,1,0:T(8,128)(2,1)}, u32[]{:S(2)}, u32[]{:S(2)}) %all-to-all-start.1) | async-done | bytes 917536 | tf_op jit(solution)/shard_map/all_to_all | solution.py:139
  64.6 5.6 %all-to-all-start.2 = ((f16[16,28,8,128]{3,2,1,0:T(8,128)(2,1)}), f16[16,28,8,128]{3,2,1,0:T(8,128)(2,1)}, u32[]{:S(2)}, u32[]{:S(2)}) async-start(f16[16,28,8,128]{3,2,1,0:T(8,128)(2,1)} %convert_element_type.38), calls=%async_computation.2 | async-start | bytes 1835008 | tf_op jit(solution)/shard_map/all_to_all | solution.py:139
  70.2 0.8 exponential_bitcast_fusion.2
  71.0 1.4 %multiply_reduce_fusion.1.refs_0_ = f32[2,27,8,128]{3,2,1,0:T(8,128)S(1)} fusion(f16[8,2,28,8,128]{4,3,2,1,0:T(8,128)(2,1)} %bitcast.20, f32[8,2,8,128]{3,2,1,0:T(8,128)S(1)} %exponential_bitcast_fusion.2), kind=kLoop, calls=%fused_computation.1 | loop fusion | flops 1271808 | bytes 1171456 | tf_op jit(solution)/shard_map/reduce_sum | solution.py:145
  72.4 0.6 slice_bitcast_fusion.8
  73.0 0.8 collective-permute-start.3
  73.8 2.8 %collective-permute-start.4 = (f32[9,8,128]{2,1,0:T(8,128)}, f32[9,8,128]{2,1,0:T(8,128)S(1)}, u32[]{:S(2)}, u32[]{:S(2)}) collective-permute-start(f32[9,8,128]{2,1,0:T(8,128)} %get-tuple-element.66), channel_id=1, source_target_pairs={{0,112},{1,113},{2,114},{3,115},{4,116},{5,117},{6,118},{7,119},{8... | collective-permute-start | bytes 110600 | tf_op jit(solution)/shard_map/ppermute | solution.py:48
  76.6 2.0 %collective-permute-start.5 = (f32[9,8,128]{2,1,0:T(8,128)}, f32[9,8,128]{2,1,0:T(8,128)S(1)}, u32[]{:S(2)}, u32[]{:S(2)}) collective-permute-start(f32[9,8,128]{2,1,0:T(8,128)} %get-tuple-element.65), channel_id=1, source_target_pairs={{0,128},{1,129},{2,130},{3,131},{4,132},{5,133},{6,134},{7,135},{8... | collective-permute-start | bytes 110600 | tf_op jit(solution)/shard_map/ppermute | solution.py:48
  78.6 3.4 %shard_map.19 = f32[16,19,8,128]{3,2,1,0:T(8,128)S(1)} custom-call(s32[1]{0:T(128)} %bitcast.16.core_ref, f32[8,2048]{1,0:T(8,128)S(1)} %broadcast_in_dim.9.mean_ref, bf16[768,1024]{1,0:T(8,128)(2,1)} %collective-permute-done.7.refs_0_, bf16[768,1024]{1,0:T(8,128)(2,1)S(1)} %collective-permute-done.6.refs_0_.refs_1_, ...), custom_call_target="tpu_custom_call" | custom-call | flops 1 | bytes 1 | tf_op jit(solution)/shard_map/pallas_call | solution.py:127
  82.1 0.9 convert_element_type.39
  83.0 0.2 all-to-all-done.2
  83.2 0.0 collective-permute-done.3.refs_1_
  83.2 0.3 collective-permute-done.5.refs_3_
  83.5 0.8 exponential_bitcast_fusion.1
  84.3 6.1 %all-to-all-start.3 = ((f16[16,19,8,128]{3,2,1,0:T(8,128)(2,1)}), f16[16,19,8,128]{3,2,1,0:T(8,128)(2,1)S(1)}, u32[]{:S(2)}, u32[]{:S(2)}) async-start(f16[16,19,8,128]{3,2,1,0:T(8,128)(2,1)} %convert_element_type.39), calls=%async_computation.3 | async-start | bytes 1245184 | tf_op jit(solution)/shard_map/all_to_all | solution.py:139
  90.4 1.4 %multiply_reduce_fusion.refs_4_ = f32[2,27,8,128]{3,2,1,0:T(8,128)S(1)} fusion(f16[8,2,28,8,128]{4,3,2,1,0:T(8,128)(2,1)} %bitcast.25, f32[8,2,8,128]{3,2,1,0:T(8,128)S(1)} %exponential_bitcast_fusion.1), kind=kLoop, calls=%fused_computation | loop fusion | flops 1271808 | bytes 1171456 | tf_op jit(solution)/shard_map/reduce_sum | solution.py:145
  91.8 3.3 %collective-permute-start.8 = (f32[18,8,128]{2,1,0:T(8,128)S(1)}, f32[18,8,128]{2,1,0:T(8,128)S(1)}, u32[]{:S(2)}, u32[]{:S(2)}) collective-permute-start(f32[18,8,128]{2,1,0:T(8,128)S(1)} %pad_maximum_fusion), channel_id=1, source_target_pairs={{0,96},{1,97},{2,98},{3,99},{4,100},{5,101},{6,102},{7,103},{8,104... | collective-permute-start | bytes 221192 | tf_op jit(solution)/shard_map/ppermute | solution.py:48
  95.1 1.5 %collective-permute-start.9 = (f32[18,8,128]{2,1,0:T(8,128)S(1)}, f32[18,8,128]{2,1,0:T(8,128)S(1)}, u32[]{:S(2)}, u32[]{:S(2)}) collective-permute-start(f32[18,8,128]{2,1,0:T(8,128)S(1)} %pad_maximum_fusion.1), channel_id=1, source_target_pairs={{0,160},{1,161},{2,162},{3,163},{4,164},{5,165},{6,166},{7,167},{8... | collective-permute-start | bytes 221192 | tf_op jit(solution)/shard_map/ppermute | solution.py:48
  96.6 3.0 %collective-permute-start.10 = (f32[9,8,128]{2,1,0:T(8,128)S(1)}, f32[9,8,128]{2,1,0:T(8,128)S(1)}, u32[]{:S(2)}, u32[]{:S(2)}) collective-permute-start(f32[9,8,128]{2,1,0:T(8,128)S(1)} %get-tuple-element.60), channel_id=1, source_target_pairs={{0,16},{1,17},{2,18},{3,19},{4,20},{5,21},{6,22},{7,23},{8,24},{9,... | collective-permute-start | bytes 110600 | tf_op jit(solution)/shard_map/ppermute | solution.py:48
  99.5 1.8 %collective-permute-start.11 = (f32[9,8,128]{2,1,0:T(8,128)S(1)}, f32[9,8,128]{2,1,0:T(8,128)S(1)}, u32[]{:S(2)}, u32[]{:S(2)}) collective-permute-start(f32[9,8,128]{2,1,0:T(8,128)S(1)} %get-tuple-element.59), channel_id=1, source_target_pairs={{0,112},{1,113},{2,114},{3,115},{4,116},{5,117},{6,118},{7,119},{8... | collective-permute-start | bytes 110600 | tf_op jit(solution)/shard_map/ppermute | solution.py:48
  101.3 4.4 %collective-permute-done.10.refs_7_ = f32[9,8,128]{2,1,0:T(8,128)S(1)} collective-permute-done((f32[9,8,128]{2,1,0:T(8,128)S(1)}, f32[9,8,128]{2,1,0:T(8,128)S(1)}, u32[]{:S(2)}, u32[]{:S(2)}) %collective-permute-start.10) | collective-permute-done | bytes 36896 | tf_op jit(solution)/shard_map/ppermute | solution.py:48
  105.8 0.1 multiply_reduce_fusion.2.refs_9_
  105.9 1.1 collective-permute-start.12
  107.0 0.1 stack.67.place_ref
  107.1 4.9 %collective-permute-done.12.refs_10_ = f32[18,8,128]{2,1,0:T(8,128)S(1)} collective-permute-done((f32[18,8,128]{2,1,0:T(8,128)S(1)}, f32[18,8,128]{2,1,0:T(8,128)S(1)}, u32[]{:S(2)}, u32[]{:S(2)}) %collective-permute-start.12) | collective-permute-done | bytes 73760 | tf_op jit(solution)/shard_map/ppermute | solution.py:48
  112.1 1.4 %shard_map.20 = f32[24,6144]{1,0:T(8,128)} custom-call(s32[16]{0:T(128)S(1)} %stack.67.place_ref, f32[2,27,8,128]{3,2,1,0:T(8,128)S(1)} %multiply_reduce_fusion.1.refs_0_, f32[9,8,128]{2,1,0:T(8,128)S(1)} %collective-permute-done.3.refs_1_, f32[9,8,128]{2,1,0:T(8,128)S(1)} %collective-permute-done.4.refs_2_, ...), custom_call_target="tpu_custom_call" | custom-call | tf_op jit(solution)/shard_map/pallas_call | solution.py:220
  (28 shorter events, 0.2 us)
Async XLA Ops:
  0.0 9.3 %copy-start.6 = (bf16[384,1024]{1,0:T(8,128)(2,1)S(1)}, bf16[384,1024]{1,0:T(8,128)(2,1)}, u32[]{:S(2)}) copy-start(bf16[384,1024]{1,0:T(8,128)(2,1)} %param.1) | copy-start | bytes 2359300
  0.0 2.5 %collective-permute-start = (bf16[384,1024]{1,0:T(8,128)(2,1)}, bf16[384,1024]{1,0:T(8,128)(2,1)S(1)}, u32[]{:S(2)}, u32[]{:S(2)}) collective-permute-start(bf16[384,1024]{1,0:T(8,128)(2,1)} %param.1), channel_id=1, source_target_pairs={{0,1},{1,0},{2,3},{3,2},{4,5},{5,4},{6,7},{7,6},{8,9},{9,8},{10,11... | collective-permute-start | bytes 2359304 | tf_op jit(solution)/shard_map/ppermute | solution.py:48
  2.6 27.7 %copy-start = (bf16[768,1024]{1,0:T(8,128)(2,1)}, bf16[768,1024]{1,0:T(8,128)(2,1)S(1)}, u32[]{:S(2)}) copy-start(bf16[768,1024]{1,0:T(8,128)(2,1)S(1)} %constant_dynamic-update-slice_fusion.refs_0_) | copy-start | bytes 4718596
  2.6 27.7 %collective-permute-start.1 = (bf16[768,1024]{1,0:T(8,128)(2,1)S(1)}, bf16[768,1024]{1,0:T(8,128)(2,1)}, u32[]{:S(2)}, u32[]{:S(2)}) collective-permute-start(bf16[768,1024]{1,0:T(8,128)(2,1)S(1)} %constant_dynamic-update-slice_fusion.refs_0_), channel_id=1, source_target_pairs={{0,112},{1,17},{2,114},{3,19},{4,116},{5,21},{6,118},{7,23},{8,120... | collective-permute-start | bytes 4718600 | tf_op jit(solution)/shard_map/ppermute | solution.py:48
  8.5 21.8 %collective-permute-start.2 = (bf16[768,1024]{1,0:T(8,128)(2,1)S(1)}, bf16[768,1024]{1,0:T(8,128)(2,1)S(1)}, u32[]{:S(2)}, u32[]{:S(2)}) collective-permute-start(bf16[768,1024]{1,0:T(8,128)(2,1)S(1)} %constant_dynamic-update-slice_fusion.refs_0_), channel_id=1, source_target_pairs={{1,129},{3,131},{5,133},{7,135},{9,137},{11,139},{13,141},{15,143}... | collective-permute-start | bytes 4718600 | tf_op jit(solution)/shard_map/ppermute | solution.py:48
  30.3 1.1 %copy-start.2 = (bf16[768,1024]{1,0:T(8,128)(2,1)}, bf16[768,1024]{1,0:T(8,128)(2,1)S(1)}, u32[]{:S(2)}) copy-start(bf16[768,1024]{1,0:T(8,128)(2,1)S(1)} %collective-permute-done.2.refs_2_) | copy-start | bytes 4718596
  31.4 23.8 %collective-permute-start.6 = (bf16[768,1024]{1,0:T(8,128)(2,1)}, bf16[768,1024]{1,0:T(8,128)(2,1)S(1)}, u32[]{:S(2)}, u32[]{:S(2)}) collective-permute-start(bf16[768,1024]{1,0:T(8,128)(2,1)} %collective-permute-done.1.refs_1_), channel_id=1, source_target_pairs={{0,241},{1,16},{2,243},{3,18},{4,245},{5,20},{6,247},{7,22},{8,249... | collective-permute-start | bytes 4718600 | tf_op jit(solution)/shard_map/ppermute | solution.py:48
  36.3 1.4 %copy-start.1 = (bf16[768,1024]{1,0:T(8,128)(2,1)S(1)}, bf16[768,1024]{1,0:T(8,128)(2,1)}, u32[]{:S(2)}) copy-start(bf16[768,1024]{1,0:T(8,128)(2,1)} %copy-done) | copy-start | bytes 4718596
  37.7 1.4 %copy-start.3 = (bf16[768,1024]{1,0:T(8,128)(2,1)S(1)}, bf16[768,1024]{1,0:T(8,128)(2,1)}, u32[]{:S(2)}) copy-start(bf16[768,1024]{1,0:T(8,128)(2,1)} %copy-done.2) | copy-start | bytes 4718596
  43.6 1.1 %copy-start.4 = (bf16[384,2048]{1,0:T(8,128)(2,1)}, bf16[384,2048]{1,0:T(8,128)(2,1)S(1)}, u32[]{:S(2)}) copy-start(bf16[384,2048]{1,0:T(8,128)(2,1)S(1)} %get-tuple-element.38.refs_2_) | copy-start | bytes 4718596
  45.8 18.8 %all-to-all-start.1 = ((f16[16,28,8,128]{3,2,1,0:T(8,128)(2,1)}), f16[16,28,8,128]{3,2,1,0:T(8,128)(2,1)}, u32[]{:S(2)}, u32[]{:S(2)}) async-start(f16[16,28,8,128]{3,2,1,0:T(8,128)(2,1)} %convert_element_type.35), calls=%async_computation.1 | async-start | bytes 1835008 | tf_op jit(solution)/shard_map/all_to_all | solution.py:139
  50.8 27.8 %collective-permute-start.7 = (bf16[768,1024]{1,0:T(8,128)(2,1)}, bf16[768,1024]{1,0:T(8,128)(2,1)}, u32[]{:S(2)}, u32[]{:S(2)}) collective-permute-start(bf16[768,1024]{1,0:T(8,128)(2,1)} %collective-permute-done.1.refs_1_), channel_id=1, source_target_pairs={{0,112},{1,17},{2,114},{3,19},{4,116},{5,21},{6,118},{7,23},{8,120... | collective-permute-start | bytes 4718600 | tf_op jit(solution)/shard_map/ppermute | solution.py:48
  55.2 1.4 %copy-start.5 = (bf16[384,2048]{1,0:T(8,128)(2,1)S(1)}, bf16[384,2048]{1,0:T(8,128)(2,1)}, u32[]{:S(2)}) copy-start(bf16[384,2048]{1,0:T(8,128)(2,1)} %copy-done.4) | copy-start | bytes 4718596
  64.6 18.6 %all-to-all-start.2 = ((f16[16,28,8,128]{3,2,1,0:T(8,128)(2,1)}), f16[16,28,8,128]{3,2,1,0:T(8,128)(2,1)}, u32[]{:S(2)}, u32[]{:S(2)}) async-start(f16[16,28,8,128]{3,2,1,0:T(8,128)(2,1)} %convert_element_type.38), calls=%async_computation.2 | async-start | bytes 1835008 | tf_op jit(solution)/shard_map/all_to_all | solution.py:139
  73.0 10.2 %collective-permute-start.3 = (f32[9,8,128]{2,1,0:T(8,128)}, f32[9,8,128]{2,1,0:T(8,128)S(1)}, u32[]{:S(2)}, u32[]{:S(2)}) collective-permute-start(f32[9,8,128]{2,1,0:T(8,128)} %get-tuple-element.67), channel_id=1, source_target_pairs={{0,16},{1,17},{2,18},{3,19},{4,20},{5,21},{6,22},{7,23},{8,24},{9,... | collective-permute-start | bytes 110600 | tf_op jit(solution)/shard_map/ppermute | solution.py:48
  73.8 9.4 %collective-permute-start.4 = (f32[9,8,128]{2,1,0:T(8,128)}, f32[9,8,128]{2,1,0:T(8,128)S(1)}, u32[]{:S(2)}, u32[]{:S(2)}) collective-permute-start(f32[9,8,128]{2,1,0:T(8,128)} %get-tuple-element.66), channel_id=1, source_target_pairs={{0,112},{1,113},{2,114},{3,115},{4,116},{5,117},{6,118},{7,119},{8... | collective-permute-start | bytes 110600 | tf_op jit(solution)/shard_map/ppermute | solution.py:48
  76.6 6.9 %collective-permute-start.5 = (f32[9,8,128]{2,1,0:T(8,128)}, f32[9,8,128]{2,1,0:T(8,128)S(1)}, u32[]{:S(2)}, u32[]{:S(2)}) collective-permute-start(f32[9,8,128]{2,1,0:T(8,128)} %get-tuple-element.65), channel_id=1, source_target_pairs={{0,128},{1,129},{2,130},{3,131},{4,132},{5,133},{6,134},{7,135},{8... | collective-permute-start | bytes 110600 | tf_op jit(solution)/shard_map/ppermute | solution.py:48
  84.3 21.5 %all-to-all-start.3 = ((f16[16,19,8,128]{3,2,1,0:T(8,128)(2,1)}), f16[16,19,8,128]{3,2,1,0:T(8,128)(2,1)S(1)}, u32[]{:S(2)}, u32[]{:S(2)}) async-start(f16[16,19,8,128]{3,2,1,0:T(8,128)(2,1)} %convert_element_type.39), calls=%async_computation.3 | async-start | bytes 1245184 | tf_op jit(solution)/shard_map/all_to_all | solution.py:139
  91.8 13.9 %collective-permute-start.8 = (f32[18,8,128]{2,1,0:T(8,128)S(1)}, f32[18,8,128]{2,1,0:T(8,128)S(1)}, u32[]{:S(2)}, u32[]{:S(2)}) collective-permute-start(f32[18,8,128]{2,1,0:T(8,128)S(1)} %pad_maximum_fusion), channel_id=1, source_target_pairs={{0,96},{1,97},{2,98},{3,99},{4,100},{5,101},{6,102},{7,103},{8,104... | collective-permute-start | bytes 221192 | tf_op jit(solution)/shard_map/ppermute | solution.py:48
  95.1 10.6 %collective-permute-start.9 = (f32[18,8,128]{2,1,0:T(8,128)S(1)}, f32[18,8,128]{2,1,0:T(8,128)S(1)}, u32[]{:S(2)}, u32[]{:S(2)}) collective-permute-start(f32[18,8,128]{2,1,0:T(8,128)S(1)} %pad_maximum_fusion.1), channel_id=1, source_target_pairs={{0,160},{1,161},{2,162},{3,163},{4,164},{5,165},{6,166},{7,167},{8... | collective-permute-start | bytes 221192 | tf_op jit(solution)/shard_map/ppermute | solution.py:48
  96.6 9.2 %collective-permute-start.10 = (f32[9,8,128]{2,1,0:T(8,128)S(1)}, f32[9,8,128]{2,1,0:T(8,128)S(1)}, u32[]{:S(2)}, u32[]{:S(2)}) collective-permute-start(f32[9,8,128]{2,1,0:T(8,128)S(1)} %get-tuple-element.60), channel_id=1, source_target_pairs={{0,16},{1,17},{2,18},{3,19},{4,20},{5,21},{6,22},{7,23},{8,24},{9,... | collective-permute-start | bytes 110600 | tf_op jit(solution)/shard_map/ppermute | solution.py:48
  99.5 6.2 %collective-permute-start.11 = (f32[9,8,128]{2,1,0:T(8,128)S(1)}, f32[9,8,128]{2,1,0:T(8,128)S(1)}, u32[]{:S(2)}, u32[]{:S(2)}) collective-permute-start(f32[9,8,128]{2,1,0:T(8,128)S(1)} %get-tuple-element.59), channel_id=1, source_target_pairs={{0,112},{1,113},{2,114},{3,115},{4,116},{5,117},{6,118},{7,119},{8... | collective-permute-start | bytes 110600 | tf_op jit(solution)/shard_map/ppermute | solution.py:48
  105.9 6.1 %collective-permute-start.12 = (f32[18,8,128]{2,1,0:T(8,128)S(1)}, f32[18,8,128]{2,1,0:T(8,128)S(1)}, u32[]{:S(2)}, u32[]{:S(2)}) collective-permute-start(f32[18,8,128]{2,1,0:T(8,128)S(1)} %pad_maximum_fusion.2), channel_id=1, source_target_pairs={{0,96},{1,97},{2,98},{3,99},{4,100},{5,101},{6,102},{7,103},{8,104... | collective-permute-start | bytes 221192 | tf_op jit(solution)/shard_map/ppermute | solution.py:48

commit v5 on v4

--- a/solution.py
+++ b/solution.py
@@ -12,6 +12,7 @@
 SAMP = ("yh", "z")
 PAR = ("x", "yl", "core")
 VMEM_MIB = 16
+FLOPS = 5 * 10**10
 
 SLOTS = {
     "S0": ((0, 0), (0, 0)),
@@ -71,13 +72,20 @@
 def multiply_kernel(raw, held, kept, group, scale, core_ref, mean_ref, *refs):
     raw_refs, refs = refs[: len(raw)], refs[len(raw) :]
     held_refs, kept_refs, out_ref = refs[: len(held)], refs[len(held) : -1], refs[-1]
+    if mean_ref.ndim == 3:
+        total = jnp.sum(mean_ref[...], axis=0) * (1.0 / (mean_ref.shape[0] * (raw_refs[0].shape[0] // 2)))
+        means = jnp.concatenate([total[n : n + 1] for n in range(total.shape[0])], axis=1)
+        kept_refs, (mean_out_ref,) = kept_refs[:-1], kept_refs[-1:]
+        mean_out_ref[...] = jnp.broadcast_to(means, mean_out_ref.shape)
+    else:
+        means = mean_ref[0:1]
     rows, width = raw_refs[0].shape[0] // 2, raw_refs[0].shape[1]
     on_core_1 = core_ref[0] == 1
 
     terms = [[] for _ in group]
     for half in range(2):
         across = slice(half * width, (half + 1) * width)
-        mean = mean_ref[0:1, across]
+        mean = means[:, across]
         wide = {}
         for ref, (name, flip) in zip(raw_refs, raw):
             first = (1 - half if flip else half) * rows
@@ -117,20 +125,24 @@
     out_ref[:, tile] = jnp.broadcast_to(exponent.reshape(1, 1, 1), (16, 8, 128))
 
 
-def multiply(core, mean, raw, held, kept, group, scale):
+def multiply(core, mean, raw, held, kept, group, scale, flops=1):
     first = next(iter(raw.values()))[0]
     rows, width = first.shape[0] // 2, 2 * first.shape[1]
     tiles = len(group) * (rows // 128) ** 2 + 1
     whole = pl.BlockSpec(memory_space=pltpu.VMEM)
     centred = jax.ShapeDtypeStruct((rows, width), jnp.bfloat16)
     names = tuple((name, flip) for name, (_, flip) in raw.items())
+    first_round = mean.ndim == 3
+    if first_round:
+        kept = (*kept, "mean")
+    outs = [jax.ShapeDtypeStruct((8, width), jnp.float32) if n == "mean" else centred for n in kept]
     *blocks, value = pl.pallas_call(
-        functools.partial(multiply_kernel, names, tuple(held), kept, group, scale),
+        functools.partial(multiply_kernel, names, tuple(held), kept[: len(kept) - first_round], group, scale),
         in_specs=[pl.BlockSpec(memory_space=pltpu.SMEM)] + [whole] * (1 + len(raw) + len(held)),
         out_specs=[whole] * (len(kept) + 1),
-        out_shape=[*(centred for _ in kept), jax.ShapeDtypeStruct((16, tiles, 8, 128), jnp.float32)],
+        out_shape=[*outs, jax.ShapeDtypeStruct((16, tiles, 8, 128), jnp.float32)],
         compiler_params=pltpu.CompilerParams(vmem_limit_bytes=VMEM_MIB * 2**20),
-        cost_estimate=pl.CostEstimate(flops=1, bytes_accessed=1, transcendentals=0),
+        cost_estimate=pl.CostEstimate(flops=flops, bytes_accessed=1, transcendentals=0),
     )(core, mean, *(block for block, _ in raw.values()), *held.values())
     return dict(zip(kept, blocks)), value
 
@@ -172,14 +184,12 @@
     sums = [jnp.sum(part.astype(jnp.float32), axis=0) for part in (own[:rows], own[rows:])]
     sums = jnp.concatenate(sums).reshape(-1, 128)
     sums = lax.all_to_all(jnp.broadcast_to(sums, (blocks, *sums.shape)), SAMP, 0, 0)
-    near, mate, sums = lax.optimization_barrier((near, mate, sums))
     crossed = permute(near, crossing)
-    mean = jnp.sum(sums, axis=0).reshape(1, -1) / total_rows
-    mean = jnp.broadcast_to(mean, (8, mean.shape[1]))
     scale = float(np.float32(1) / np.sqrt(np.float32(total_rows)))
 
     raw = {"S0": (own, False), "S1": (near, False), "T1": (mate, False)}
-    held, value = multiply(core, mean, raw, {}, ("S0", "S1"), GROUPS[0], scale)
+    held, value = multiply(core, sums, raw, {}, ("S0", "S1"), GROUPS[0], scale, FLOPS)
+    mean = held.pop("mean")
     messages = [scatter_over_par(value.astype(jnp.float16))]
     near, held["S1"] = lax.optimization_barrier((near, held["S1"]))
     far = permute(near, along_z)

time: 114 us -> 110 us (0.965)
  blocking collectives: 20.7 us -> 0 us
  waiting for transfers between devices: 17.9 us -> 28.6 us
  starting transfers between devices: 46.1 us -> 53.2 us
  local copies, waits for them, and re-layouts: 8.59 us -> 6.7 us
    all_to_all x1 -> x0, blocking collectives: 20.7 us -> none  [local(): lax.all_to_all(jnp.broadcast_to(sums, (blocks, *sums.shape)), SAMP, 0, 0)]
    ppermute x13, waiting for transfers between devices: 13.7 us -> 21.8 us  [permute(): return lax.ppermute(value, tuple(AXES), pairs)]
    all_to_all x0 -> x1, starting transfers between devices: none -> 5.91 us  [local(): lax.all_to_all(jnp.broadcast_to(sums, (blocks, *sums.shape)), SAMP, 0, 0)]
    all_to_all x3, waiting for transfers between devices: 4.17 us -> 6.74 us  [scatter_over_par(): return lax.all_to_all(message, PAR, 0, 0)]
    unnamed x15 -> x11, local copies, waits for them, and re-layouts: 7.76 us -> 5.21 us
    ppermute x13, starting transfers between devices: 29.4 us -> 30.8 us  [permute(): return lax.ppermute(value, tuple(AXES), pairs)]
  transfers between devices with their start and end apart: 16 -> 17, of which waited for: 7 -> 7; matrix products, arithmetic and copies ran while one was open for 8% -> 9% of each run, Pallas kernels for 9% -> 10%
where the time goes in v5:
time: 110 us; the launch traced here: 109 us
  starting transfers between devices  53.2 us (48%)
  waiting for transfers between devices  28.6 us (26%)
  Pallas kernels  12.7 us (12%)
  other arithmetic  7.78 us (7%)
  local copies, waits for them, and re-layouts  6.7 us (6%)
    ppermute x13, starting transfers between devices, permute(): return lax.ppermute(value, tuple(AXES), pairs)  30.8 us
    ppermute x13, waiting for transfers between devices, permute(): return lax.ppermute(value, tuple(AXES), pairs)  21.8 us
    all_to_all x3, starting transfers between devices, scatter_over_par(): return lax.all_to_all(message, PAR, 0, 0)  16.5 us
    pallas_call x3, Pallas kernels, multiply(): pl.pallas_call(functools.partial(multiply_kernel, names, tuple(held), kep...  11.2 us
    all_to_all x3, waiting for transfers between devices, scatter_over_par(): return lax.all_to_all(message, PAR, 0, 0)  6.74 us
    all_to_all x1, starting transfers between devices, local(): lax.all_to_all(jnp.broadcast_to(sums, (blocks, *sums.shape)), SAMP, 0, 0)  5.91 us
    unnamed x11, local copies, waits for them, and re-layouts  5.21 us
    reduce_sum x3, other arithmetic, gather_sum(): return jnp.sum(message[:, :, :-1].astype(jnp.float32) * factor, axis=0)  2.88 us
  transfers between devices with their start and end apart: 17, of which 7 were waited for; matrix products, arithmetic and copies ran while one was open for 9% of the time, Pallas kernels for 10%

profile of v5, /device:TPU:2, one launch (start us, length us, event | category | flops | bytes accessed | tf_op | source)
XLA Modules:
  0.0 109.1 jit_solution(5921897503034385437)
XLA Ops:
  0.0 0.0 collective-permute-start
  0.0 1.3 %constant_dynamic-update-slice_fusion.1 = bf16[768,1024]{1,0:T(8,128)(2,1)S(1)} fusion(bf16[384,1024]{1,0:T(8,128)(2,1)} %param.1), kind=kLoop, calls=%fused_computation.24 | loop fusion | bytes 1572864
  1.3 1.2 %collective-permute-done = bf16[384,1024]{1,0:T(8,128)(2,1)S(1)} collective-permute-done((bf16[384,1024]{1,0:T(8,128)(2,1)}, bf16[384,1024]{1,0:T(8,128)(2,1)S(1)}, u32[]{:S(2)}, u32[]{:S(2)}) %collective-permute-start) | collective-permute-done | bytes 786464 | tf_op jit(solution)/shard_map/ppermute | solution.py:49
  2.5 0.1 constant_dynamic-update-slice_fusion.refs_0_
  2.6 5.9 %collective-permute-start.1 = (bf16[768,1024]{1,0:T(8,128)(2,1)S(1)}, bf16[768,1024]{1,0:T(8,128)(2,1)}, u32[]{:S(2)}, u32[]{:S(2)}) collective-permute-start(bf16[768,1024]{1,0:T(8,128)(2,1)S(1)} %constant_dynamic-update-slice_fusion.refs_0_), channel_id=1, source_target_pairs={{0,112},{1,17},{2,114},{3,19},{4,116},{5,21},{6,118},{7,23},{8,120... | collective-permute-start | bytes 4718600 | tf_op jit(solution)/shard_map/ppermute | solution.py:49
  8.5 1.8 %collective-permute-start.2 = (bf16[768,1024]{1,0:T(8,128)(2,1)S(1)}, bf16[768,1024]{1,0:T(8,128)(2,1)}, u32[]{:S(2)}, u32[]{:S(2)}) collective-permute-start(bf16[768,1024]{1,0:T(8,128)(2,1)S(1)} %constant_dynamic-update-slice_fusion.refs_0_), channel_id=1, source_target_pairs={{1,129},{3,131},{5,133},{7,135},{9,137},{11,139},{13,141},{15,143}... | collective-permute-start | bytes 4718600 | tf_op jit(solution)/shard_map/ppermute | solution.py:49
  10.3 0.1 convert_reduce_fusion.1
  10.4 0.1 convert_reduce_fusion
  10.6 0.7 broadcast_in_dim.3
  11.3 5.9 %all-to-all-start = ((f32[16,16,128]{2,1,0:T(8,128)}), f32[16,16,128]{2,1,0:T(8,128)S(1)}, u32[]{:S(2)}, u32[]{:S(2)}) async-start(f32[16,16,128]{2,1,0:T(8,128)} %broadcast_in_dim.3), calls=%async_computation | async-start | bytes 262144 | tf_op jit(solution)/shard_map/all_to_all | solution.py:186
  17.2 11.5 %collective-permute-done.1.refs_1_ = bf16[768,1024]{1,0:T(8,128)(2,1)} collective-permute-done((bf16[768,1024]{1,0:T(8,128)(2,1)S(1)}, bf16[768,1024]{1,0:T(8,128)(2,1)}, u32[]{:S(2)}, u32[]{:S(2)}) %collective-permute-start.1) | collective-permute-done | bytes 1572896 | tf_op jit(solution)/shard_map/ppermute | solution.py:49
  28.7 3.2 %collective-permute-start.6 = (bf16[768,1024]{1,0:T(8,128)(2,1)}, bf16[768,1024]{1,0:T(8,128)(2,1)S(1)}, u32[]{:S(2)}, u32[]{:S(2)}) collective-permute-start(bf16[768,1024]{1,0:T(8,128)(2,1)} %collective-permute-done.1.refs_1_), channel_id=1, source_target_pairs={{0,241},{1,16},{2,243},{3,18},{4,245},{5,20},{6,247},{7,22},{8,249... | collective-permute-start | bytes 4718600 | tf_op jit(solution)/shard_map/ppermute | solution.py:49
  31.9 0.0 all-to-all-done.mean_ref
  32.0 1.4 %copy-done.3 = bf16[768,1024]{1,0:T(8,128)(2,1)S(1)} copy-done((bf16[768,1024]{1,0:T(8,128)(2,1)S(1)}, bf16[768,1024]{1,0:T(8,128)(2,1)}, u32[]{:S(2)}) %copy-start.3) | copy-done | bytes 1572888
  33.4 4.9 %shard_map.17 = (bf16[384,2048]{1,0:T(8,128)(2,1)S(1)}, bf16[384,2048]{1,0:T(8,128)(2,1)S(1)}, f32[8,2048]{1,0:T(8,128)S(1)}, f32[16,28,8,128]{3,2,1,0:T(8,128)S(1)}) custom-call(s32[1]{0:T(128)} %bitcast.16.core_ref, f32[16,16,128]{2,1,0:T(8,128)S(1)} %all-to-all-done.mean_ref, bf16[768,1024]{1,0:T(8,128)(2,1)S(1)} %copy-done.3, ...), custom_call_target="tpu_custom_call" | custom-call | flops 49999998976 | bytes 1 | tf_op jit(solution)/shard_map/pallas_call | solution.py:139
  38.3 1.1 %copy-done = bf16[384,2048]{1,0:T(8,128)(2,1)} copy-done((bf16[384,2048]{1,0:T(8,128)(2,1)}, bf16[384,2048]{1,0:T(8,128)(2,1)S(1)}, u32[]{:S(2)}) %copy-start) | copy-done | bytes 1572888
  39.4 1.0 convert_element_type.35
  40.5 5.1 %all-to-all-start.1 = ((f16[16,28,8,128]{3,2,1,0:T(8,128)(2,1)}), f16[16,28,8,128]{3,2,1,0:T(8,128)(2,1)}, u32[]{:S(2)}, u32[]{:S(2)}) async-start(f16[16,28,8,128]{3,2,1,0:T(8,128)(2,1)} %convert_element_type.35), calls=%async_computation.1 | async-start | bytes 1835008 | tf_op jit(solution)/shard_map/all_to_all | solution.py:151
  45.6 3.4 %collective-permute-start.7 = (bf16[768,1024]{1,0:T(8,128)(2,1)}, bf16[768,1024]{1,0:T(8,128)(2,1)}, u32[]{:S(2)}, u32[]{:S(2)}) collective-permute-start(bf16[768,1024]{1,0:T(8,128)(2,1)} %collective-permute-done.1.refs_1_), channel_id=1, source_target_pairs={{0,112},{1,17},{2,114},{3,19},{4,116},{5,21},{6,118},{7,23},{8,120... | collective-permute-start | bytes 4718600 | tf_op jit(solution)/shard_map/ppermute | solution.py:49
  49.1 1.1 %collective-permute-done.6.refs_0_.refs_1_ = bf16[768,1024]{1,0:T(8,128)(2,1)S(1)} collective-permute-done((bf16[768,1024]{1,0:T(8,128)(2,1)}, bf16[768,1024]{1,0:T(8,128)(2,1)S(1)}, u32[]{:S(2)}, u32[]{:S(2)}) %collective-permute-start.6) | collective-permute-done | bytes 1572896 | tf_op jit(solution)/shard_map/ppermute | solution.py:49
  50.2 1.4 %copy-done.1 = bf16[384,2048]{1,0:T(8,128)(2,1)S(1)} copy-done((bf16[384,2048]{1,0:T(8,128)(2,1)S(1)}, bf16[384,2048]{1,0:T(8,128)(2,1)}, u32[]{:S(2)}) %copy-start.1) | copy-done | bytes 1572888
  51.6 2.9 %shard_map.18 = f32[16,28,8,128]{3,2,1,0:T(8,128)S(1)} custom-call(s32[1]{0:T(128)} %bitcast.16.core_ref, f32[8,2048]{1,0:T(8,128)S(1)} %get-tuple-element.31.mean_ref, bf16[768,1024]{1,0:T(8,128)(2,1)S(1)} %collective-permute-done.6.refs_0_.refs_1_, bf16[384,2048]{1,0:T(8,128)(2,1)S(1)} %get-tuple-element.32.refs_1_.refs_2_, bf16[384,2048]{1,0:T(8,128)(2,1)S(1)} %copy-done.1), custom_call_target="tpu_custom_call" | custom-call | flops 1 | bytes 1 | tf_op jit(solution)/shard_map/pallas_call | solution.py:139
  54.5 1.1 convert_element_type.38
  55.6 5.2 %all-to-all-done.1 = f16[16,28,8,128]{3,2,1,0:T(8,128)(2,1)} async-done(((f16[16,28,8,128]{3,2,1,0:T(8,128)(2,1)}), f16[16,28,8,128]{3,2,1,0:T(8,128)(2,1)}, u32[]{:S(2)}, u32[]{:S(2)}) %all-to-all-start.1) | async-done | bytes 917536 | tf_op jit(solution)/shard_map/all_to_all | solution.py:151
  60.7 5.7 %all-to-all-start.2 = ((f16[16,28,8,128]{3,2,1,0:T(8,128)(2,1)}), f16[16,28,8,128]{3,2,1,0:T(8,128)(2,1)}, u32[]{:S(2)}, u32[]{:S(2)}) async-start(f16[16,28,8,128]{3,2,1,0:T(8,128)(2,1)} %convert_element_type.38), calls=%async_computation.2 | async-start | bytes 1835008 | tf_op jit(solution)/shard_map/all_to_all | solution.py:151
  66.4 0.8 exponential_bitcast_fusion.2
  67.2 1.4 %multiply_reduce_fusion.1.refs_0_ = f32[2,27,8,128]{3,2,1,0:T(8,128)S(1)} fusion(f16[8,2,28,8,128]{4,3,2,1,0:T(8,128)(2,1)} %bitcast.19, f32[8,2,8,128]{3,2,1,0:T(8,128)S(1)} %exponential_bitcast_fusion.2), kind=kLoop, calls=%fused_computation.1 | loop fusion | flops 1271808 | bytes 1171456 | tf_op jit(solution)/shard_map/reduce_sum | solution.py:157
  68.6 0.7 slice_bitcast_fusion.8
  69.2 1.0 collective-permute-start.3
  70.2 2.3 %collective-permute-start.4 = (f32[9,8,128]{2,1,0:T(8,128)}, f32[9,8,128]{2,1,0:T(8,128)S(1)}, u32[]{:S(2)}, u32[]{:S(2)}) collective-permute-start(f32[9,8,128]{2,1,0:T(8,128)} %get-tuple-element.62), channel_id=1, source_target_pairs={{0,112},{1,113},{2,114},{3,115},{4,116},{5,117},{6,118},{7,119},{8... | collective-permute-start | bytes 110600 | tf_op jit(solution)/shard_map/ppermute | solution.py:49
  72.5 1.0 collective-permute-start.5
  73.5 3.4 %shard_map.19 = f32[16,19,8,128]{3,2,1,0:T(8,128)S(1)} custom-call(s32[1]{0:T(128)} %bitcast.16.core_ref, f32[8,2048]{1,0:T(8,128)S(1)} %get-tuple-element.31.mean_ref, bf16[768,1024]{1,0:T(8,128)(2,1)} %collective-permute-done.7.refs_0_, bf16[768,1024]{1,0:T(8,128)(2,1)S(1)} %collective-permute-done.6.refs_0_.refs_1_, ...), custom_call_target="tpu_custom_call" | custom-call | flops 1 | bytes 1 | tf_op jit(solution)/shard_map/pallas_call | solution.py:139
  76.9 0.9 convert_element_type.39
  77.8 1.6 %all-to-all-done.2 = f16[16,28,8,128]{3,2,1,0:T(8,128)(2,1)} async-done(((f16[16,28,8,128]{3,2,1,0:T(8,128)(2,1)}), f16[16,28,8,128]{3,2,1,0:T(8,128)(2,1)}, u32[]{:S(2)}, u32[]{:S(2)}) %all-to-all-start.2) | async-done | bytes 917536 | tf_op jit(solution)/shard_map/all_to_all | solution.py:151
  79.4 0.0 collective-permute-done.5.refs_3_
  79.4 0.8 exponential_bitcast_fusion.1
  80.2 5.7 %all-to-all-start.3 = ((f16[16,19,8,128]{3,2,1,0:T(8,128)(2,1)}), f16[16,19,8,128]{3,2,1,0:T(8,128)(2,1)S(1)}, u32[]{:S(2)}, u32[]{:S(2)}) async-start(f16[16,19,8,128]{3,2,1,0:T(8,128)(2,1)} %convert_element_type.39), calls=%async_computation.3 | async-start | bytes 1245184 | tf_op jit(solution)/shard_map/all_to_all | solution.py:151
  85.9 1.4 %multiply_reduce_fusion.refs_4_ = f32[2,27,8,128]{3,2,1,0:T(8,128)S(1)} fusion(f16[8,2,28,8,128]{4,3,2,1,0:T(8,128)(2,1)} %bitcast.24, f32[8,2,8,128]{3,2,1,0:T(8,128)S(1)} %exponential_bitcast_fusion.1), kind=kLoop, calls=%fused_computation | loop fusion | flops 1271808 | bytes 1171456 | tf_op jit(solution)/shard_map/reduce_sum | solution.py:157
  87.3 3.4 %collective-permute-start.8 = (f32[18,8,128]{2,1,0:T(8,128)S(1)}, f32[18,8,128]{2,1,0:T(8,128)S(1)}, u32[]{:S(2)}, u32[]{:S(2)}) collective-permute-start(f32[18,8,128]{2,1,0:T(8,128)S(1)} %pad_maximum_fusion), channel_id=1, source_target_pairs={{0,96},{1,97},{2,98},{3,99},{4,100},{5,101},{6,102},{7,103},{8,104... | collective-permute-start | bytes 221192 | tf_op jit(solution)/shard_map/ppermute | solution.py:49
  90.7 2.1 %collective-permute-start.9 = (f32[18,8,128]{2,1,0:T(8,128)S(1)}, f32[18,8,128]{2,1,0:T(8,128)S(1)}, u32[]{:S(2)}, u32[]{:S(2)}) collective-permute-start(f32[18,8,128]{2,1,0:T(8,128)S(1)} %pad_maximum_fusion.1), channel_id=1, source_target_pairs={{0,160},{1,161},{2,162},{3,163},{4,164},{5,165},{6,166},{7,167},{8... | collective-permute-start | bytes 221192 | tf_op jit(solution)/shard_map/ppermute | solution.py:49
  92.7 1.0 collective-permute-start.10
  93.8 3.2 %collective-permute-start.11 = (f32[9,8,128]{2,1,0:T(8,128)S(1)}, f32[9,8,128]{2,1,0:T(8,128)S(1)}, u32[]{:S(2)}, u32[]{:S(2)}) collective-permute-start(f32[9,8,128]{2,1,0:T(8,128)S(1)} %get-tuple-element.55), channel_id=1, source_target_pairs={{0,112},{1,113},{2,114},{3,115},{4,116},{5,117},{6,118},{7,119},{8... | collective-permute-start | bytes 110600 | tf_op jit(solution)/shard_map/ppermute | solution.py:49
  97.0 4.3 %collective-permute-done.10.refs_7_ = f32[9,8,128]{2,1,0:T(8,128)S(1)} collective-permute-done((f32[9,8,128]{2,1,0:T(8,128)S(1)}, f32[9,8,128]{2,1,0:T(8,128)S(1)}, u32[]{:S(2)}, u32[]{:S(2)}) %collective-permute-start.10) | collective-permute-done | bytes 36896 | tf_op jit(solution)/shard_map/ppermute | solution.py:49
  101.4 0.1 multiply_reduce_fusion.2.refs_9_
  101.6 2.5 %collective-permute-start.12 = (f32[18,8,128]{2,1,0:T(8,128)S(1)}, f32[18,8,128]{2,1,0:T(8,128)S(1)}, u32[]{:S(2)}, u32[]{:S(2)}) collective-permute-start(f32[18,8,128]{2,1,0:T(8,128)S(1)} %pad_maximum_fusion.2), channel_id=1, source_target_pairs={{0,96},{1,97},{2,98},{3,99},{4,100},{5,101},{6,102},{7,103},{8,104... | collective-permute-start | bytes 221192 | tf_op jit(solution)/shard_map/ppermute | solution.py:49
  104.0 0.1 stack.67.place_ref
  104.1 3.5 %collective-permute-done.12.refs_10_ = f32[18,8,128]{2,1,0:T(8,128)S(1)} collective-permute-done((f32[18,8,128]{2,1,0:T(8,128)S(1)}, f32[18,8,128]{2,1,0:T(8,128)S(1)}, u32[]{:S(2)}, u32[]{:S(2)}) %collective-permute-start.12) | collective-permute-done | bytes 73760 | tf_op jit(solution)/shard_map/ppermute | solution.py:49
  107.7 1.4 %shard_map.20 = f32[24,6144]{1,0:T(8,128)} custom-call(s32[16]{0:T(128)S(1)} %stack.67.place_ref, f32[2,27,8,128]{3,2,1,0:T(8,128)S(1)} %multiply_reduce_fusion.1.refs_0_, f32[9,8,128]{2,1,0:T(8,128)S(1)} %collective-permute-done.3.refs_1_, f32[9,8,128]{2,1,0:T(8,128)S(1)} %collective-permute-done.4.refs_2_, ...), custom_call_target="tpu_custom_call" | custom-call | tf_op jit(solution)/shard_map/pallas_call | solution.py:230
  (22 shorter events, 0.1 us)
Async XLA Ops:
  0.0 10.3 %copy-start.4 = (bf16[384,1024]{1,0:T(8,128)(2,1)S(1)}, bf16[384,1024]{1,0:T(8,128)(2,1)}, u32[]{:S(2)}) copy-start(bf16[384,1024]{1,0:T(8,128)(2,1)} %param.1) | copy-start | bytes 2359300
  0.0 2.5 %collective-permute-start = (bf16[384,1024]{1,0:T(8,128)(2,1)}, bf16[384,1024]{1,0:T(8,128)(2,1)S(1)}, u32[]{:S(2)}, u32[]{:S(2)}) collective-permute-start(bf16[384,1024]{1,0:T(8,128)(2,1)} %param.1), channel_id=1, source_target_pairs={{0,1},{1,0},{2,3},{3,2},{4,5},{5,4},{6,7},{7,6},{8,9},{9,8},{10,11... | collective-permute-start | bytes 2359304 | tf_op jit(solution)/shard_map/ppermute | solution.py:49
  2.6 29.4 %copy-start.2 = (bf16[768,1024]{1,0:T(8,128)(2,1)}, bf16[768,1024]{1,0:T(8,128)(2,1)S(1)}, u32[]{:S(2)}) copy-start(bf16[768,1024]{1,0:T(8,128)(2,1)S(1)} %constant_dynamic-update-slice_fusion.refs_0_) | copy-start | bytes 4718596
  2.6 26.2 %collective-permute-start.1 = (bf16[768,1024]{1,0:T(8,128)(2,1)S(1)}, bf16[768,1024]{1,0:T(8,128)(2,1)}, u32[]{:S(2)}, u32[]{:S(2)}) collective-permute-start(bf16[768,1024]{1,0:T(8,128)(2,1)S(1)} %constant_dynamic-update-slice_fusion.refs_0_), channel_id=1, source_target_pairs={{0,112},{1,17},{2,114},{3,19},{4,116},{5,21},{6,118},{7,23},{8,120... | collective-permute-start | bytes 4718600 | tf_op jit(solution)/shard_map/ppermute | solution.py:49
  8.5 23.4 %collective-permute-start.2 = (bf16[768,1024]{1,0:T(8,128)(2,1)S(1)}, bf16[768,1024]{1,0:T(8,128)(2,1)}, u32[]{:S(2)}, u32[]{:S(2)}) collective-permute-start(bf16[768,1024]{1,0:T(8,128)(2,1)S(1)} %constant_dynamic-update-slice_fusion.refs_0_), channel_id=1, source_target_pairs={{1,129},{3,131},{5,133},{7,135},{9,137},{11,139},{13,141},{15,143}... | collective-permute-start | bytes 4718600 | tf_op jit(solution)/shard_map/ppermute | solution.py:49
  11.3 20.7 %all-to-all-start = ((f32[16,16,128]{2,1,0:T(8,128)}), f32[16,16,128]{2,1,0:T(8,128)S(1)}, u32[]{:S(2)}, u32[]{:S(2)}) async-start(f32[16,16,128]{2,1,0:T(8,128)} %broadcast_in_dim.3), calls=%async_computation | async-start | bytes 262144 | tf_op jit(solution)/shard_map/all_to_all | solution.py:186
  28.7 21.5 %collective-permute-start.6 = (bf16[768,1024]{1,0:T(8,128)(2,1)}, bf16[768,1024]{1,0:T(8,128)(2,1)S(1)}, u32[]{:S(2)}, u32[]{:S(2)}) collective-permute-start(bf16[768,1024]{1,0:T(8,128)(2,1)} %collective-permute-done.1.refs_1_), channel_id=1, source_target_pairs={{0,241},{1,16},{2,243},{3,18},{4,245},{5,20},{6,247},{7,22},{8,249... | collective-permute-start | bytes 4718600 | tf_op jit(solution)/shard_map/ppermute | solution.py:49
  32.0 1.4 %copy-start.3 = (bf16[768,1024]{1,0:T(8,128)(2,1)S(1)}, bf16[768,1024]{1,0:T(8,128)(2,1)}, u32[]{:S(2)}) copy-start(bf16[768,1024]{1,0:T(8,128)(2,1)} %copy-done.2) | copy-start | bytes 4718596
  38.3 1.1 %copy-start = (bf16[384,2048]{1,0:T(8,128)(2,1)}, bf16[384,2048]{1,0:T(8,128)(2,1)S(1)}, u32[]{:S(2)}) copy-start(bf16[384,2048]{1,0:T(8,128)(2,1)S(1)} %get-tuple-element.34.refs_2_) | copy-start | bytes 4718596
  40.5 20.2 %all-to-all-start.1 = ((f16[16,28,8,128]{3,2,1,0:T(8,128)(2,1)}), f16[16,28,8,128]{3,2,1,0:T(8,128)(2,1)}, u32[]{:S(2)}, u32[]{:S(2)}) async-start(f16[16,28,8,128]{3,2,1,0:T(8,128)(2,1)} %convert_element_type.35), calls=%async_computation.1 | async-start | bytes 1835008 | tf_op jit(solution)/shard_map/all_to_all | solution.py:151
  45.6 27.8 %collective-permute-start.7 = (bf16[768,1024]{1,0:T(8,128)(2,1)}, bf16[768,1024]{1,0:T(8,128)(2,1)}, u32[]{:S(2)}, u32[]{:S(2)}) collective-permute-start(bf16[768,1024]{1,0:T(8,128)(2,1)} %collective-permute-done.1.refs_1_), channel_id=1, source_target_pairs={{0,112},{1,17},{2,114},{3,19},{4,116},{5,21},{6,118},{7,23},{8,120... | collective-permute-start | bytes 4718600 | tf_op jit(solution)/shard_map/ppermute | solution.py:49
  50.2 1.4 %copy-start.1 = (bf16[384,2048]{1,0:T(8,128)(2,1)S(1)}, bf16[384,2048]{1,0:T(8,128)(2,1)}, u32[]{:S(2)}) copy-start(bf16[384,2048]{1,0:T(8,128)(2,1)} %copy-done) | copy-start | bytes 4718596
  60.7 18.7 %all-to-all-start.2 = ((f16[16,28,8,128]{3,2,1,0:T(8,128)(2,1)}), f16[16,28,8,128]{3,2,1,0:T(8,128)(2,1)}, u32[]{:S(2)}, u32[]{:S(2)}) async-start(f16[16,28,8,128]{3,2,1,0:T(8,128)(2,1)} %convert_element_type.38), calls=%async_computation.2 | async-start | bytes 1835008 | tf_op jit(solution)/shard_map/all_to_all | solution.py:151
  69.2 10.2 %collective-permute-start.3 = (f32[9,8,128]{2,1,0:T(8,128)}, f32[9,8,128]{2,1,0:T(8,128)S(1)}, u32[]{:S(2)}, u32[]{:S(2)}) collective-permute-start(f32[9,8,128]{2,1,0:T(8,128)} %get-tuple-element.63), channel_id=1, source_target_pairs={{0,16},{1,17},{2,18},{3,19},{4,20},{5,21},{6,22},{7,23},{8,24},{9,... | collective-permute-start | bytes 110600 | tf_op jit(solution)/shard_map/ppermute | solution.py:49
  70.2 9.2 %collective-permute-start.4 = (f32[9,8,128]{2,1,0:T(8,128)}, f32[9,8,128]{2,1,0:T(8,128)S(1)}, u32[]{:S(2)}, u32[]{:S(2)}) collective-permute-start(f32[9,8,128]{2,1,0:T(8,128)} %get-tuple-element.62), channel_id=1, source_target_pairs={{0,112},{1,113},{2,114},{3,115},{4,116},{5,117},{6,118},{7,119},{8... | collective-permute-start | bytes 110600 | tf_op jit(solution)/shard_map/ppermute | solution.py:49
  72.5 7.0 %collective-permute-start.5 = (f32[9,8,128]{2,1,0:T(8,128)}, f32[9,8,128]{2,1,0:T(8,128)S(1)}, u32[]{:S(2)}, u32[]{:S(2)}) collective-permute-start(f32[9,8,128]{2,1,0:T(8,128)} %get-tuple-element.61), channel_id=1, source_target_pairs={{0,128},{1,129},{2,130},{3,131},{4,132},{5,133},{6,134},{7,135},{8... | collective-permute-start | bytes 110600 | tf_op jit(solution)/shard_map/ppermute | solution.py:49
  80.2 21.1 %all-to-all-start.3 = ((f16[16,19,8,128]{3,2,1,0:T(8,128)(2,1)}), f16[16,19,8,128]{3,2,1,0:T(8,128)(2,1)S(1)}, u32[]{:S(2)}, u32[]{:S(2)}) async-start(f16[16,19,8,128]{3,2,1,0:T(8,128)(2,1)} %convert_element_type.39), calls=%async_computation.3 | async-start | bytes 1245184 | tf_op jit(solution)/shard_map/all_to_all | solution.py:151
  87.3 14.1 %collective-permute-start.8 = (f32[18,8,128]{2,1,0:T(8,128)S(1)}, f32[18,8,128]{2,1,0:T(8,128)S(1)}, u32[]{:S(2)}, u32[]{:S(2)}) collective-permute-start(f32[18,8,128]{2,1,0:T(8,128)S(1)} %pad_maximum_fusion), channel_id=1, source_target_pairs={{0,96},{1,97},{2,98},{3,99},{4,100},{5,101},{6,102},{7,103},{8,104... | collective-permute-start | bytes 221192 | tf_op jit(solution)/shard_map/ppermute | solution.py:49
  90.7 10.7 %collective-permute-start.9 = (f32[18,8,128]{2,1,0:T(8,128)S(1)}, f32[18,8,128]{2,1,0:T(8,128)S(1)}, u32[]{:S(2)}, u32[]{:S(2)}) collective-permute-start(f32[18,8,128]{2,1,0:T(8,128)S(1)} %pad_maximum_fusion.1), channel_id=1, source_target_pairs={{0,160},{1,161},{2,162},{3,163},{4,164},{5,165},{6,166},{7,167},{8... | collective-permute-start | bytes 221192 | tf_op jit(solution)/shard_map/ppermute | solution.py:49
  92.7 8.6 %collective-permute-start.10 = (f32[9,8,128]{2,1,0:T(8,128)S(1)}, f32[9,8,128]{2,1,0:T(8,128)S(1)}, u32[]{:S(2)}, u32[]{:S(2)}) collective-permute-start(f32[9,8,128]{2,1,0:T(8,128)S(1)} %get-tuple-element.56), channel_id=1, source_target_pairs={{0,16},{1,17},{2,18},{3,19},{4,20},{5,21},{6,22},{7,23},{8,24},{9,... | collective-permute-start | bytes 110600 | tf_op jit(solution)/shard_map/ppermute | solution.py:49
  93.8 7.6 %collective-permute-start.11 = (f32[9,8,128]{2,1,0:T(8,128)S(1)}, f32[9,8,128]{2,1,0:T(8,128)S(1)}, u32[]{:S(2)}, u32[]{:S(2)}) collective-permute-start(f32[9,8,128]{2,1,0:T(8,128)S(1)} %get-tuple-element.55), channel_id=1, source_target_pairs={{0,112},{1,113},{2,114},{3,115},{4,116},{5,117},{6,118},{7,119},{8... | collective-permute-start | bytes 110600 | tf_op jit(solution)/shard_map/ppermute | solution.py:49
  101.6 6.1 %collective-permute-start.12 = (f32[18,8,128]{2,1,0:T(8,128)S(1)}, f32[18,8,128]{2,1,0:T(8,128)S(1)}, u32[]{:S(2)}, u32[]{:S(2)}) collective-permute-start(f32[18,8,128]{2,1,0:T(8,128)S(1)} %pad_maximum_fusion.2), channel_id=1, source_target_pairs={{0,96},{1,97},{2,98},{3,99},{4,100},{5,101},{6,102},{7,103},{8,104... | collective-permute-start | bytes 221192 | tf_op jit(solution)/shard_map/ppermute | solution.py:49

commit v6 on v5

--- a/solution.py
+++ b/solution.py
@@ -100,8 +100,9 @@
         for ref, name in zip(held_refs, held):
             blocks[name] = ref[:, across]
         for term, ((left, right), (left_1, right_1)) in zip(terms, group):
+            same = (left, right) == (left_1, right_1)
             left, right = blocks[left], blocks[right]
-            if left_1 != left:
+            if not same:
                 left = jnp.where(on_core_1, blocks[left_1], left)
                 right = jnp.where(on_core_1, blocks[right_1], right)
             term.append(

time: 110 us -> 110 us (level)
  no operation moved by 1% of the time
where the time goes in v6:
time: 110 us; the launch traced here: 109 us
  starting transfers between devices  53.2 us (48%)
  waiting for transfers between devices  28.6 us (26%)
  Pallas kernels  12.7 us (12%)
  other arithmetic  7.78 us (7%)
  local copies, waits for them, and re-layouts  6.7 us (6%)
    ppermute x13, starting transfers between devices, permute(): return lax.ppermute(value, tuple(AXES), pairs)  30.8 us
    ppermute x13, waiting for transfers between devices, permute(): return lax.ppermute(value, tuple(AXES), pairs)  21.8 us
    all_to_all x3, starting transfers between devices, scatter_over_par(): return lax.all_to_all(message, PAR, 0, 0)  16.5 us
    pallas_call x3, Pallas kernels, multiply(): pl.pallas_call(functools.partial(multiply_kernel, names, tuple(held), kep...  11.2 us
    all_to_all x3, waiting for transfers between devices, scatter_over_par(): return lax.all_to_all(message, PAR, 0, 0)  6.74 us
    all_to_all x1, starting transfers between devices, local(): lax.all_to_all(jnp.broadcast_to(sums, (blocks, *sums.shape)), SAMP, 0, 0)  5.91 us
    unnamed x11, local copies, waits for them, and re-layouts  5.21 us
    reduce_sum x3, other arithmetic, gather_sum(): return jnp.sum(message[:, :, :-1].astype(jnp.float32) * factor, axis=0)  2.88 us
  transfers between devices with their start and end apart: 17, of which 7 were waited for; matrix products, arithmetic and copies ran while one was open for 9% of the time, Pallas kernels for 10%

profile of v6, /device:TPU:2, one launch (start us, length us, event | category | flops | bytes accessed | tf_op | source)
XLA Modules:
  0.0 109.1 jit_solution(5921897503034385437)
XLA Ops:
  0.0 0.0 collective-permute-start
  0.0 1.3 %constant_dynamic-update-slice_fusion.1 = bf16[768,1024]{1,0:T(8,128)(2,1)S(1)} fusion(bf16[384,1024]{1,0:T(8,128)(2,1)} %param.1), kind=kLoop, calls=%fused_computation.24 | loop fusion | bytes 1572864
  1.3 1.2 %collective-permute-done = bf16[384,1024]{1,0:T(8,128)(2,1)S(1)} collective-permute-done((bf16[384,1024]{1,0:T(8,128)(2,1)}, bf16[384,1024]{1,0:T(8,128)(2,1)S(1)}, u32[]{:S(2)}, u32[]{:S(2)}) %collective-permute-start) | collective-permute-done | bytes 786464 | tf_op jit(solution)/shard_map/ppermute | solution.py:49
  2.5 0.1 constant_dynamic-update-slice_fusion.refs_0_
  2.6 5.9 %collective-permute-start.1 = (bf16[768,1024]{1,0:T(8,128)(2,1)S(1)}, bf16[768,1024]{1,0:T(8,128)(2,1)}, u32[]{:S(2)}, u32[]{:S(2)}) collective-permute-start(bf16[768,1024]{1,0:T(8,128)(2,1)S(1)} %constant_dynamic-update-slice_fusion.refs_0_), channel_id=1, source_target_pairs={{0,112},{1,17},{2,114},{3,19},{4,116},{5,21},{6,118},{7,23},{8,120... | collective-permute-start | bytes 4718600 | tf_op jit(solution)/shard_map/ppermute | solution.py:49
  8.5 1.8 %collective-permute-start.2 = (bf16[768,1024]{1,0:T(8,128)(2,1)S(1)}, bf16[768,1024]{1,0:T(8,128)(2,1)}, u32[]{:S(2)}, u32[]{:S(2)}) collective-permute-start(bf16[768,1024]{1,0:T(8,128)(2,1)S(1)} %constant_dynamic-update-slice_fusion.refs_0_), channel_id=1, source_target_pairs={{1,129},{3,131},{5,133},{7,135},{9,137},{11,139},{13,141},{15,143}... | collective-permute-start | bytes 4718600 | tf_op jit(solution)/shard_map/ppermute | solution.py:49
  10.3 0.1 convert_reduce_fusion.1
  10.4 0.1 convert_reduce_fusion
  10.6 0.7 broadcast_in_dim.3
  11.3 5.9 %all-to-all-start = ((f32[16,16,128]{2,1,0:T(8,128)}), f32[16,16,128]{2,1,0:T(8,128)S(1)}, u32[]{:S(2)}, u32[]{:S(2)}) async-start(f32[16,16,128]{2,1,0:T(8,128)} %broadcast_in_dim.3), calls=%async_computation | async-start | bytes 262144 | tf_op jit(solution)/shard_map/all_to_all | solution.py:187
  17.2 11.5 %collective-permute-done.1.refs_1_ = bf16[768,1024]{1,0:T(8,128)(2,1)} collective-permute-done((bf16[768,1024]{1,0:T(8,128)(2,1)S(1)}, bf16[768,1024]{1,0:T(8,128)(2,1)}, u32[]{:S(2)}, u32[]{:S(2)}) %collective-permute-start.1) | collective-permute-done | bytes 1572896 | tf_op jit(solution)/shard_map/ppermute | solution.py:49
  28.7 3.2 %collective-permute-start.6 = (bf16[768,1024]{1,0:T(8,128)(2,1)}, bf16[768,1024]{1,0:T(8,128)(2,1)S(1)}, u32[]{:S(2)}, u32[]{:S(2)}) collective-permute-start(bf16[768,1024]{1,0:T(8,128)(2,1)} %collective-permute-done.1.refs_1_), channel_id=1, source_target_pairs={{0,241},{1,16},{2,243},{3,18},{4,245},{5,20},{6,247},{7,22},{8,249... | collective-permute-start | bytes 4718600 | tf_op jit(solution)/shard_map/ppermute | solution.py:49
  31.9 0.0 all-to-all-done.mean_ref
  32.0 1.4 %copy-done.3 = bf16[768,1024]{1,0:T(8,128)(2,1)S(1)} copy-done((bf16[768,1024]{1,0:T(8,128)(2,1)S(1)}, bf16[768,1024]{1,0:T(8,128)(2,1)}, u32[]{:S(2)}) %copy-start.3) | copy-done | bytes 1572888
  33.4 4.9 %shard_map.17 = (bf16[384,2048]{1,0:T(8,128)(2,1)S(1)}, bf16[384,2048]{1,0:T(8,128)(2,1)S(1)}, f32[8,2048]{1,0:T(8,128)S(1)}, f32[16,28,8,128]{3,2,1,0:T(8,128)S(1)}) custom-call(s32[1]{0:T(128)} %bitcast.16.core_ref, f32[16,16,128]{2,1,0:T(8,128)S(1)} %all-to-all-done.mean_ref, bf16[768,1024]{1,0:T(8,128)(2,1)S(1)} %copy-done.3, ...), custom_call_target="tpu_custom_call" | custom-call | flops 49999998976 | bytes 1 | tf_op jit(solution)/shard_map/pallas_call | solution.py:140
  38.3 1.1 %copy-done = bf16[384,2048]{1,0:T(8,128)(2,1)} copy-done((bf16[384,2048]{1,0:T(8,128)(2,1)}, bf16[384,2048]{1,0:T(8,128)(2,1)S(1)}, u32[]{:S(2)}) %copy-start) | copy-done | bytes 1572888
  39.4 1.0 convert_element_type.35
  40.5 5.1 %all-to-all-start.1 = ((f16[16,28,8,128]{3,2,1,0:T(8,128)(2,1)}), f16[16,28,8,128]{3,2,1,0:T(8,128)(2,1)}, u32[]{:S(2)}, u32[]{:S(2)}) async-start(f16[16,28,8,128]{3,2,1,0:T(8,128)(2,1)} %convert_element_type.35), calls=%async_computation.1 | async-start | bytes 1835008 | tf_op jit(solution)/shard_map/all_to_all | solution.py:152
  45.6 3.4 %collective-permute-start.7 = (bf16[768,1024]{1,0:T(8,128)(2,1)}, bf16[768,1024]{1,0:T(8,128)(2,1)}, u32[]{:S(2)}, u32[]{:S(2)}) collective-permute-start(bf16[768,1024]{1,0:T(8,128)(2,1)} %collective-permute-done.1.refs_1_), channel_id=1, source_target_pairs={{0,112},{1,17},{2,114},{3,19},{4,116},{5,21},{6,118},{7,23},{8,120... | collective-permute-start | bytes 4718600 | tf_op jit(solution)/shard_map/ppermute | solution.py:49
  49.1 1.1 %collective-permute-done.6.refs_0_.refs_1_ = bf16[768,1024]{1,0:T(8,128)(2,1)S(1)} collective-permute-done((bf16[768,1024]{1,0:T(8,128)(2,1)}, bf16[768,1024]{1,0:T(8,128)(2,1)S(1)}, u32[]{:S(2)}, u32[]{:S(2)}) %collective-permute-start.6) | collective-permute-done | bytes 1572896 | tf_op jit(solution)/shard_map/ppermute | solution.py:49
  50.2 1.4 %copy-done.1 = bf16[384,2048]{1,0:T(8,128)(2,1)S(1)} copy-done((bf16[384,2048]{1,0:T(8,128)(2,1)S(1)}, bf16[384,2048]{1,0:T(8,128)(2,1)}, u32[]{:S(2)}) %copy-start.1) | copy-done | bytes 1572888
  51.6 2.9 %shard_map.18 = f32[16,28,8,128]{3,2,1,0:T(8,128)S(1)} custom-call(s32[1]{0:T(128)} %bitcast.16.core_ref, f32[8,2048]{1,0:T(8,128)S(1)} %get-tuple-element.31.mean_ref, bf16[768,1024]{1,0:T(8,128)(2,1)S(1)} %collective-permute-done.6.refs_0_.refs_1_, bf16[384,2048]{1,0:T(8,128)(2,1)S(1)} %get-tuple-element.32.refs_1_.refs_2_, bf16[384,2048]{1,0:T(8,128)(2,1)S(1)} %copy-done.1), custom_call_target="tpu_custom_call" | custom-call | flops 1 | bytes 1 | tf_op jit(solution)/shard_map/pallas_call | solution.py:140
  54.5 1.1 convert_element_type.38
  55.6 5.2 %all-to-all-done.1 = f16[16,28,8,128]{3,2,1,0:T(8,128)(2,1)} async-done(((f16[16,28,8,128]{3,2,1,0:T(8,128)(2,1)}), f16[16,28,8,128]{3,2,1,0:T(8,128)(2,1)}, u32[]{:S(2)}, u32[]{:S(2)}) %all-to-all-start.1) | async-done | bytes 917536 | tf_op jit(solution)/shard_map/all_to_all | solution.py:152
  60.7 5.7 %all-to-all-start.2 = ((f16[16,28,8,128]{3,2,1,0:T(8,128)(2,1)}), f16[16,28,8,128]{3,2,1,0:T(8,128)(2,1)}, u32[]{:S(2)}, u32[]{:S(2)}) async-start(f16[16,28,8,128]{3,2,1,0:T(8,128)(2,1)} %convert_element_type.38), calls=%async_computation.2 | async-start | bytes 1835008 | tf_op jit(solution)/shard_map/all_to_all | solution.py:152
  66.4 0.8 exponential_bitcast_fusion.2
  67.2 1.4 %multiply_reduce_fusion.1.refs_0_ = f32[2,27,8,128]{3,2,1,0:T(8,128)S(1)} fusion(f16[8,2,28,8,128]{4,3,2,1,0:T(8,128)(2,1)} %bitcast.19, f32[8,2,8,128]{3,2,1,0:T(8,128)S(1)} %exponential_bitcast_fusion.2), kind=kLoop, calls=%fused_computation.1 | loop fusion | flops 1271808 | bytes 1171456 | tf_op jit(solution)/shard_map/reduce_sum | solution.py:158
  68.6 0.7 slice_bitcast_fusion.8
  69.2 1.0 collective-permute-start.3
  70.2 2.3 %collective-permute-start.4 = (f32[9,8,128]{2,1,0:T(8,128)}, f32[9,8,128]{2,1,0:T(8,128)S(1)}, u32[]{:S(2)}, u32[]{:S(2)}) collective-permute-start(f32[9,8,128]{2,1,0:T(8,128)} %get-tuple-element.62), channel_id=1, source_target_pairs={{0,112},{1,113},{2,114},{3,115},{4,116},{5,117},{6,118},{7,119},{8... | collective-permute-start | bytes 110600 | tf_op jit(solution)/shard_map/ppermute | solution.py:49
  72.5 1.0 collective-permute-start.5
  73.5 3.4 %shard_map.19 = f32[16,19,8,128]{3,2,1,0:T(8,128)S(1)} custom-call(s32[1]{0:T(128)} %bitcast.16.core_ref, f32[8,2048]{1,0:T(8,128)S(1)} %get-tuple-element.31.mean_ref, bf16[768,1024]{1,0:T(8,128)(2,1)} %collective-permute-done.7.refs_0_, bf16[768,1024]{1,0:T(8,128)(2,1)S(1)} %collective-permute-done.6.refs_0_.refs_1_, ...), custom_call_target="tpu_custom_call" | custom-call | flops 1 | bytes 1 | tf_op jit(solution)/shard_map/pallas_call | solution.py:140
  76.9 0.9 convert_element_type.39
  77.8 1.6 %all-to-all-done.2 = f16[16,28,8,128]{3,2,1,0:T(8,128)(2,1)} async-done(((f16[16,28,8,128]{3,2,1,0:T(8,128)(2,1)}), f16[16,28,8,128]{3,2,1,0:T(8,128)(2,1)}, u32[]{:S(2)}, u32[]{:S(2)}) %all-to-all-start.2) | async-done | bytes 917536 | tf_op jit(solution)/shard_map/all_to_all | solution.py:152
  79.4 0.0 collective-permute-done.5.refs_3_
  79.4 0.8 exponential_bitcast_fusion.1
  80.2 5.7 %all-to-all-start.3 = ((f16[16,19,8,128]{3,2,1,0:T(8,128)(2,1)}), f16[16,19,8,128]{3,2,1,0:T(8,128)(2,1)S(1)}, u32[]{:S(2)}, u32[]{:S(2)}) async-start(f16[16,19,8,128]{3,2,1,0:T(8,128)(2,1)} %convert_element_type.39), calls=%async_computation.3 | async-start | bytes 1245184 | tf_op jit(solution)/shard_map/all_to_all | solution.py:152
  85.9 1.4 %multiply_reduce_fusion.refs_4_ = f32[2,27,8,128]{3,2,1,0:T(8,128)S(1)} fusion(f16[8,2,28,8,128]{4,3,2,1,0:T(8,128)(2,1)} %bitcast.24, f32[8,2,8,128]{3,2,1,0:T(8,128)S(1)} %exponential_bitcast_fusion.1), kind=kLoop, calls=%fused_computation | loop fusion | flops 1271808 | bytes 1171456 | tf_op jit(solution)/shard_map/reduce_sum | solution.py:158
  87.3 3.4 %collective-permute-start.8 = (f32[18,8,128]{2,1,0:T(8,128)S(1)}, f32[18,8,128]{2,1,0:T(8,128)S(1)}, u32[]{:S(2)}, u32[]{:S(2)}) collective-permute-start(f32[18,8,128]{2,1,0:T(8,128)S(1)} %pad_maximum_fusion), channel_id=1, source_target_pairs={{0,96},{1,97},{2,98},{3,99},{4,100},{5,101},{6,102},{7,103},{8,104... | collective-permute-start | bytes 221192 | tf_op jit(solution)/shard_map/ppermute | solution.py:49
  90.7 2.1 %collective-permute-start.9 = (f32[18,8,128]{2,1,0:T(8,128)S(1)}, f32[18,8,128]{2,1,0:T(8,128)S(1)}, u32[]{:S(2)}, u32[]{:S(2)}) collective-permute-start(f32[18,8,128]{2,1,0:T(8,128)S(1)} %pad_maximum_fusion.1), channel_id=1, source_target_pairs={{0,160},{1,161},{2,162},{3,163},{4,164},{5,165},{6,166},{7,167},{8... | collective-permute-start | bytes 221192 | tf_op jit(solution)/shard_map/ppermute | solution.py:49
  92.7 1.0 collective-permute-start.10
  93.8 3.2 %collective-permute-start.11 = (f32[9,8,128]{2,1,0:T(8,128)S(1)}, f32[9,8,128]{2,1,0:T(8,128)S(1)}, u32[]{:S(2)}, u32[]{:S(2)}) collective-permute-start(f32[9,8,128]{2,1,0:T(8,128)S(1)} %get-tuple-element.55), channel_id=1, source_target_pairs={{0,112},{1,113},{2,114},{3,115},{4,116},{5,117},{6,118},{7,119},{8... | collective-permute-start | bytes 110600 | tf_op jit(solution)/shard_map/ppermute | solution.py:49
  97.0 4.3 %collective-permute-done.10.refs_7_ = f32[9,8,128]{2,1,0:T(8,128)S(1)} collective-permute-done((f32[9,8,128]{2,1,0:T(8,128)S(1)}, f32[9,8,128]{2,1,0:T(8,128)S(1)}, u32[]{:S(2)}, u32[]{:S(2)}) %collective-permute-start.10) | collective-permute-done | bytes 36896 | tf_op jit(solution)/shard_map/ppermute | solution.py:49
  101.4 0.1 multiply_reduce_fusion.2.refs_9_
  101.6 2.5 %collective-permute-start.12 = (f32[18,8,128]{2,1,0:T(8,128)S(1)}, f32[18,8,128]{2,1,0:T(8,128)S(1)}, u32[]{:S(2)}, u32[]{:S(2)}) collective-permute-start(f32[18,8,128]{2,1,0:T(8,128)S(1)} %pad_maximum_fusion.2), channel_id=1, source_target_pairs={{0,96},{1,97},{2,98},{3,99},{4,100},{5,101},{6,102},{7,103},{8,104... | collective-permute-start | bytes 221192 | tf_op jit(solution)/shard_map/ppermute | solution.py:49
  104.0 0.1 stack.67.place_ref
  104.1 3.5 %collective-permute-done.12.refs_10_ = f32[18,8,128]{2,1,0:T(8,128)S(1)} collective-permute-done((f32[18,8,128]{2,1,0:T(8,128)S(1)}, f32[18,8,128]{2,1,0:T(8,128)S(1)}, u32[]{:S(2)}, u32[]{:S(2)}) %collective-permute-start.12) | collective-permute-done | bytes 73760 | tf_op jit(solution)/shard_map/ppermute | solution.py:49
  107.7 1.4 %shard_map.20 = f32[24,6144]{1,0:T(8,128)} custom-call(s32[16]{0:T(128)S(1)} %stack.67.place_ref, f32[2,27,8,128]{3,2,1,0:T(8,128)S(1)} %multiply_reduce_fusion.1.refs_0_, f32[9,8,128]{2,1,0:T(8,128)S(1)} %collective-permute-done.3.refs_1_, f32[9,8,128]{2,1,0:T(8,128)S(1)} %collective-permute-done.4.refs_2_, ...), custom_call_target="tpu_custom_call" | custom-call | tf_op jit(solution)/shard_map/pallas_call | solution.py:231
  (22 shorter events, 0.1 us)
Async XLA Ops:
  0.0 10.3 %copy-start.4 = (bf16[384,1024]{1,0:T(8,128)(2,1)S(1)}, bf16[384,1024]{1,0:T(8,128)(2,1)}, u32[]{:S(2)}) copy-start(bf16[384,1024]{1,0:T(8,128)(2,1)} %param.1) | copy-start | bytes 2359300
  0.0 2.5 %collective-permute-start = (bf16[384,1024]{1,0:T(8,128)(2,1)}, bf16[384,1024]{1,0:T(8,128)(2,1)S(1)}, u32[]{:S(2)}, u32[]{:S(2)}) collective-permute-start(bf16[384,1024]{1,0:T(8,128)(2,1)} %param.1), channel_id=1, source_target_pairs={{0,1},{1,0},{2,3},{3,2},{4,5},{5,4},{6,7},{7,6},{8,9},{9,8},{10,11... | collective-permute-start | bytes 2359304 | tf_op jit(solution)/shard_map/ppermute | solution.py:49
  2.6 29.4 %copy-start.2 = (bf16[768,1024]{1,0:T(8,128)(2,1)}, bf16[768,1024]{1,0:T(8,128)(2,1)S(1)}, u32[]{:S(2)}) copy-start(bf16[768,1024]{1,0:T(8,128)(2,1)S(1)} %constant_dynamic-update-slice_fusion.refs_0_) | copy-start | bytes 4718596
  2.6 26.2 %collective-permute-start.1 = (bf16[768,1024]{1,0:T(8,128)(2,1)S(1)}, bf16[768,1024]{1,0:T(8,128)(2,1)}, u32[]{:S(2)}, u32[]{:S(2)}) collective-permute-start(bf16[768,1024]{1,0:T(8,128)(2,1)S(1)} %constant_dynamic-update-slice_fusion.refs_0_), channel_id=1, source_target_pairs={{0,112},{1,17},{2,114},{3,19},{4,116},{5,21},{6,118},{7,23},{8,120... | collective-permute-start | bytes 4718600 | tf_op jit(solution)/shard_map/ppermute | solution.py:49
  8.5 23.4 %collective-permute-start.2 = (bf16[768,1024]{1,0:T(8,128)(2,1)S(1)}, bf16[768,1024]{1,0:T(8,128)(2,1)}, u32[]{:S(2)}, u32[]{:S(2)}) collective-permute-start(bf16[768,1024]{1,0:T(8,128)(2,1)S(1)} %constant_dynamic-update-slice_fusion.refs_0_), channel_id=1, source_target_pairs={{1,129},{3,131},{5,133},{7,135},{9,137},{11,139},{13,141},{15,143}... | collective-permute-start | bytes 4718600 | tf_op jit(solution)/shard_map/ppermute | solution.py:49
  11.3 20.7 %all-to-all-start = ((f32[16,16,128]{2,1,0:T(8,128)}), f32[16,16,128]{2,1,0:T(8,128)S(1)}, u32[]{:S(2)}, u32[]{:S(2)}) async-start(f32[16,16,128]{2,1,0:T(8,128)} %broadcast_in_dim.3), calls=%async_computation | async-start | bytes 262144 | tf_op jit(solution)/shard_map/all_to_all | solution.py:187
  28.7 21.5 %collective-permute-start.6 = (bf16[768,1024]{1,0:T(8,128)(2,1)}, bf16[768,1024]{1,0:T(8,128)(2,1)S(1)}, u32[]{:S(2)}, u32[]{:S(2)}) collective-permute-start(bf16[768,1024]{1,0:T(8,128)(2,1)} %collective-permute-done.1.refs_1_), channel_id=1, source_target_pairs={{0,241},{1,16},{2,243},{3,18},{4,245},{5,20},{6,247},{7,22},{8,249... | collective-permute-start | bytes 4718600 | tf_op jit(solution)/shard_map/ppermute | solution.py:49
  32.0 1.4 %copy-start.3 = (bf16[768,1024]{1,0:T(8,128)(2,1)S(1)}, bf16[768,1024]{1,0:T(8,128)(2,1)}, u32[]{:S(2)}) copy-start(bf16[768,1024]{1,0:T(8,128)(2,1)} %copy-done.2) | copy-start | bytes 4718596
  38.3 1.1 %copy-start = (bf16[384,2048]{1,0:T(8,128)(2,1)}, bf16[384,2048]{1,0:T(8,128)(2,1)S(1)}, u32[]{:S(2)}) copy-start(bf16[384,2048]{1,0:T(8,128)(2,1)S(1)} %get-tuple-element.34.refs_2_) | copy-start | bytes 4718596
  40.5 20.2 %all-to-all-start.1 = ((f16[16,28,8,128]{3,2,1,0:T(8,128)(2,1)}), f16[16,28,8,128]{3,2,1,0:T(8,128)(2,1)}, u32[]{:S(2)}, u32[]{:S(2)}) async-start(f16[16,28,8,128]{3,2,1,0:T(8,128)(2,1)} %convert_element_type.35), calls=%async_computation.1 | async-start | bytes 1835008 | tf_op jit(solution)/shard_map/all_to_all | solution.py:152
  45.6 27.8 %collective-permute-start.7 = (bf16[768,1024]{1,0:T(8,128)(2,1)}, bf16[768,1024]{1,0:T(8,128)(2,1)}, u32[]{:S(2)}, u32[]{:S(2)}) collective-permute-start(bf16[768,1024]{1,0:T(8,128)(2,1)} %collective-permute-done.1.refs_1_), channel_id=1, source_target_pairs={{0,112},{1,17},{2,114},{3,19},{4,116},{5,21},{6,118},{7,23},{8,120... | collective-permute-start | bytes 4718600 | tf_op jit(solution)/shard_map/ppermute | solution.py:49
  50.2 1.4 %copy-start.1 = (bf16[384,2048]{1,0:T(8,128)(2,1)S(1)}, bf16[384,2048]{1,0:T(8,128)(2,1)}, u32[]{:S(2)}) copy-start(bf16[384,2048]{1,0:T(8,128)(2,1)} %copy-done) | copy-start | bytes 4718596
  60.7 18.7 %all-to-all-start.2 = ((f16[16,28,8,128]{3,2,1,0:T(8,128)(2,1)}), f16[16,28,8,128]{3,2,1,0:T(8,128)(2,1)}, u32[]{:S(2)}, u32[]{:S(2)}) async-start(f16[16,28,8,128]{3,2,1,0:T(8,128)(2,1)} %convert_element_type.38), calls=%async_computation.2 | async-start | bytes 1835008 | tf_op jit(solution)/shard_map/all_to_all | solution.py:152
  69.2 10.2 %collective-permute-start.3 = (f32[9,8,128]{2,1,0:T(8,128)}, f32[9,8,128]{2,1,0:T(8,128)S(1)}, u32[]{:S(2)}, u32[]{:S(2)}) collective-permute-start(f32[9,8,128]{2,1,0:T(8,128)} %get-tuple-element.63), channel_id=1, source_target_pairs={{0,16},{1,17},{2,18},{3,19},{4,20},{5,21},{6,22},{7,23},{8,24},{9,... | collective-permute-start | bytes 110600 | tf_op jit(solution)/shard_map/ppermute | solution.py:49
  70.2 9.2 %collective-permute-start.4 = (f32[9,8,128]{2,1,0:T(8,128)}, f32[9,8,128]{2,1,0:T(8,128)S(1)}, u32[]{:S(2)}, u32[]{:S(2)}) collective-permute-start(f32[9,8,128]{2,1,0:T(8,128)} %get-tuple-element.62), channel_id=1, source_target_pairs={{0,112},{1,113},{2,114},{3,115},{4,116},{5,117},{6,118},{7,119},{8... | collective-permute-start | bytes 110600 | tf_op jit(solution)/shard_map/ppermute | solution.py:49
  72.5 7.0 %collective-permute-start.5 = (f32[9,8,128]{2,1,0:T(8,128)}, f32[9,8,128]{2,1,0:T(8,128)S(1)}, u32[]{:S(2)}, u32[]{:S(2)}) collective-permute-start(f32[9,8,128]{2,1,0:T(8,128)} %get-tuple-element.61), channel_id=1, source_target_pairs={{0,128},{1,129},{2,130},{3,131},{4,132},{5,133},{6,134},{7,135},{8... | collective-permute-start | bytes 110600 | tf_op jit(solution)/shard_map/ppermute | solution.py:49
  80.2 21.1 %all-to-all-start.3 = ((f16[16,19,8,128]{3,2,1,0:T(8,128)(2,1)}), f16[16,19,8,128]{3,2,1,0:T(8,128)(2,1)S(1)}, u32[]{:S(2)}, u32[]{:S(2)}) async-start(f16[16,19,8,128]{3,2,1,0:T(8,128)(2,1)} %convert_element_type.39), calls=%async_computation.3 | async-start | bytes 1245184 | tf_op jit(solution)/shard_map/all_to_all | solution.py:152
  87.3 14.1 %collective-permute-start.8 = (f32[18,8,128]{2,1,0:T(8,128)S(1)}, f32[18,8,128]{2,1,0:T(8,128)S(1)}, u32[]{:S(2)}, u32[]{:S(2)}) collective-permute-start(f32[18,8,128]{2,1,0:T(8,128)S(1)} %pad_maximum_fusion), channel_id=1, source_target_pairs={{0,96},{1,97},{2,98},{3,99},{4,100},{5,101},{6,102},{7,103},{8,104... | collective-permute-start | bytes 221192 | tf_op jit(solution)/shard_map/ppermute | solution.py:49
  90.7 10.7 %collective-permute-start.9 = (f32[18,8,128]{2,1,0:T(8,128)S(1)}, f32[18,8,128]{2,1,0:T(8,128)S(1)}, u32[]{:S(2)}, u32[]{:S(2)}) collective-permute-start(f32[18,8,128]{2,1,0:T(8,128)S(1)} %pad_maximum_fusion.1), channel_id=1, source_target_pairs={{0,160},{1,161},{2,162},{3,163},{4,164},{5,165},{6,166},{7,167},{8... | collective-permute-start | bytes 221192 | tf_op jit(solution)/shard_map/ppermute | solution.py:49
  92.7 8.6 %collective-permute-start.10 = (f32[9,8,128]{2,1,0:T(8,128)S(1)}, f32[9,8,128]{2,1,0:T(8,128)S(1)}, u32[]{:S(2)}, u32[]{:S(2)}) collective-permute-start(f32[9,8,128]{2,1,0:T(8,128)S(1)} %get-tuple-element.56), channel_id=1, source_target_pairs={{0,16},{1,17},{2,18},{3,19},{4,20},{5,21},{6,22},{7,23},{8,24},{9,... | collective-permute-start | bytes 110600 | tf_op jit(solution)/shard_map/ppermute | solution.py:49
  93.8 7.6 %collective-permute-start.11 = (f32[9,8,128]{2,1,0:T(8,128)S(1)}, f32[9,8,128]{2,1,0:T(8,128)S(1)}, u32[]{:S(2)}, u32[]{:S(2)}) collective-permute-start(f32[9,8,128]{2,1,0:T(8,128)S(1)} %get-tuple-element.55), channel_id=1, source_target_pairs={{0,112},{1,113},{2,114},{3,115},{4,116},{5,117},{6,118},{7,119},{8... | collective-permute-start | bytes 110600 | tf_op jit(solution)/shard_map/ppermute | solution.py:49
  101.6 6.1 %collective-permute-start.12 = (f32[18,8,128]{2,1,0:T(8,128)S(1)}, f32[18,8,128]{2,1,0:T(8,128)S(1)}, u32[]{:S(2)}, u32[]{:S(2)}) collective-permute-start(f32[18,8,128]{2,1,0:T(8,128)S(1)} %pad_maximum_fusion.2), channel_id=1, source_target_pairs={{0,96},{1,97},{2,98},{3,99},{4,100},{5,101},{6,102},{7,103},{8,104... | collective-permute-start | bytes 221192 | tf_op jit(solution)/shard_map/ppermute | solution.py:49

commit v7 on v6

--- a/solution.py
+++ b/solution.py
@@ -189,16 +189,17 @@
     scale = float(np.float32(1) / np.sqrt(np.float32(total_rows)))
 
     raw = {"S0": (own, False), "S1": (near, False), "T1": (mate, False)}
-    held, value = multiply(core, sums, raw, {}, ("S0", "S1"), GROUPS[0], scale, FLOPS)
+    held, value = multiply(core, sums, raw, {}, (), GROUPS[0], scale, FLOPS)
     mean = held.pop("mean")
     messages = [scatter_over_par(value.astype(jnp.float16))]
-    near, held["S1"] = lax.optimization_barrier((near, held["S1"]))
+    near, mean = lax.optimization_barrier((near, mean))
     far = permute(near, along_z)
-    _, value = multiply(core, mean, {"T3": (crossed, True)}, held, (), GROUPS[1], scale)
+    raw = {"S0": (own, False), "S1": (near, False), "T3": (crossed, True)}
+    _, value = multiply(core, mean, raw, {}, (), GROUPS[1], scale)
     messages.append(scatter_over_par(value.astype(jnp.float16)))
     far, crossed, _ = lax.optimization_barrier((far, crossed, value))
-    raw = {"S2": (far, False), "T3": (crossed, True)}
-    _, value = multiply(core, mean, raw, {"S0": held["S0"]}, (), GROUPS[2], scale)
+    raw = {"S0": (own, False), "S2": (far, False), "T3": (crossed, True)}
+    _, value = multiply(core, mean, raw, {}, (), GROUPS[2], scale)
     messages[1], message = lax.optimization_barrier((messages[1], value.astype(jnp.float16)))
     messages.append(scatter_over_par(message))
 

time: 110 us -> 110 us (level)
  local copies, waits for them, and re-layouts: 6.7 us -> 2.73 us
  waiting for transfers between devices: 28.6 us -> 31.7 us
  Pallas kernels: 12.7 us -> 14 us
    ppermute x13, waiting for transfers between devices: 21.8 us -> 27.6 us  [permute(): return lax.ppermute(value, tuple(AXES), pairs)]
    unnamed x11 -> x3, local copies, waits for them, and re-layouts: 5.21 us -> 1.26 us
    all_to_all x3, waiting for transfers between devices: 6.74 us -> 4.07 us  [scatter_over_par(): return lax.all_to_all(message, PAR, 0, 0)]
    all_to_all x3, starting transfers between devices: 16.5 us -> 18.4 us  [scatter_over_par(): return lax.all_to_all(message, PAR, 0, 0)]
    ppermute x13, starting transfers between devices: 30.8 us -> 28.9 us  [permute(): return lax.ppermute(value, tuple(AXES), pairs)]
    pallas_call x3, Pallas kernels: 11.2 us -> 12.6 us  [multiply(): pl.pallas_call(functools.partial(multiply_kernel, names, tuple(held), kep...]
  transfers between devices with their start and end apart: 17 -> 17, of which waited for: 7 -> 9; matrix products, arithmetic and copies ran while one was open for 9% -> 9% of each run, Pallas kernels for 10% -> 11%
where the time goes in v7:
time: 110 us
  starting transfers between devices  53.3 us (48%)
  waiting for transfers between devices  31.7 us (29%)
  Pallas kernels  14 us (13%)
  other arithmetic  7.77 us (7%)
  local copies, waits for them, and re-layouts  2.73 us (2%)
    ppermute x13, starting transfers between devices, permute(): return lax.ppermute(value, tuple(AXES), pairs)  28.9 us
    ppermute x13, waiting for transfers between devices, permute(): return lax.ppermute(value, tuple(AXES), pairs)  27.6 us
    all_to_all x3, starting transfers between devices, scatter_over_par(): return lax.all_to_all(message, PAR, 0, 0)  18.4 us
    pallas_call x3, Pallas kernels, multiply(): pl.pallas_call(functools.partial(multiply_kernel, names, tuple(held), kep...  12.6 us
    all_to_all x1, starting transfers between devices, local(): lax.all_to_all(jnp.broadcast_to(sums, (blocks, *sums.shape)), SAMP, 0, 0)  5.91 us
    all_to_all x3, waiting for transfers between devices, scatter_over_par(): return lax.all_to_all(message, PAR, 0, 0)  4.07 us
    reduce_sum x3, other arithmetic, gather_sum(): return jnp.sum(message[:, :, :-1].astype(jnp.float32) * factor, axis=0)  2.88 us
  transfers between devices with their start and end apart: 17, of which 9 were waited for; matrix products, arithmetic and copies ran while one was open for 9% of the time, Pallas kernels for 11%

profile of v7, /device:TPU:2, one launch (start us, length us, event | category | flops | bytes accessed | tf_op | source)
XLA Modules:
  0.0 109.6 jit_solution(1269023825253301220)
XLA Ops:
  0.0 1.3 %constant_dynamic-update-slice_fusion.1 = bf16[768,1024]{1,0:T(8,128)(2,1)S(1)} fusion(bf16[384,1024]{1,0:T(8,128)(2,1)} %param.1), kind=kLoop, calls=%fused_computation.24 | loop fusion | bytes 1572864
  1.3 1.2 %collective-permute-done = bf16[384,1024]{1,0:T(8,128)(2,1)S(1)} collective-permute-done((bf16[384,1024]{1,0:T(8,128)(2,1)}, bf16[384,1024]{1,0:T(8,128)(2,1)S(1)}, u32[]{:S(2)}, u32[]{:S(2)}) %collective-permute-start) | collective-permute-done | bytes 786464 | tf_op jit(solution)/shard_map/ppermute | solution.py:49
  2.5 0.1 constant_dynamic-update-slice_fusion.refs_0_
  2.6 5.9 %collective-permute-start.1 = (bf16[768,1024]{1,0:T(8,128)(2,1)S(1)}, bf16[768,1024]{1,0:T(8,128)(2,1)}, u32[]{:S(2)}, u32[]{:S(2)}) collective-permute-start(bf16[768,1024]{1,0:T(8,128)(2,1)S(1)} %constant_dynamic-update-slice_fusion.refs_0_), channel_id=1, source_target_pairs={{0,112},{1,17},{2,114},{3,19},{4,116},{5,21},{6,118},{7,23},{8,120... | collective-permute-start | bytes 4718600 | tf_op jit(solution)/shard_map/ppermute | solution.py:49
  8.5 1.8 %collective-permute-start.2 = (bf16[768,1024]{1,0:T(8,128)(2,1)S(1)}, bf16[768,1024]{1,0:T(8,128)(2,1)}, u32[]{:S(2)}, u32[]{:S(2)}) collective-permute-start(bf16[768,1024]{1,0:T(8,128)(2,1)S(1)} %constant_dynamic-update-slice_fusion.refs_0_), channel_id=1, source_target_pairs={{1,129},{3,131},{5,133},{7,135},{9,137},{11,139},{13,141},{15,143}... | collective-permute-start | bytes 4718600 | tf_op jit(solution)/shard_map/ppermute | solution.py:49
  10.3 0.1 convert_reduce_fusion.1
  10.4 0.1 convert_reduce_fusion
  10.6 0.7 broadcast_in_dim.3
  11.3 5.9 %all-to-all-start = ((f32[16,16,128]{2,1,0:T(8,128)}), f32[16,16,128]{2,1,0:T(8,128)S(1)}, u32[]{:S(2)}, u32[]{:S(2)}) async-start(f32[16,16,128]{2,1,0:T(8,128)} %broadcast_in_dim.3), calls=%async_computation | async-start | bytes 262144 | tf_op jit(solution)/shard_map/all_to_all | solution.py:187
  17.2 11.5 %collective-permute-done.1.refs_1_ = bf16[768,1024]{1,0:T(8,128)(2,1)} collective-permute-done((bf16[768,1024]{1,0:T(8,128)(2,1)S(1)}, bf16[768,1024]{1,0:T(8,128)(2,1)}, u32[]{:S(2)}, u32[]{:S(2)}) %collective-permute-start.1) | collective-permute-done | bytes 1572896 | tf_op jit(solution)/shard_map/ppermute | solution.py:49
  28.7 3.2 %collective-permute-start.6 = (bf16[768,1024]{1,0:T(8,128)(2,1)}, bf16[768,1024]{1,0:T(8,128)(2,1)S(1)}, u32[]{:S(2)}, u32[]{:S(2)}) collective-permute-start(bf16[768,1024]{1,0:T(8,128)(2,1)} %collective-permute-done.1.refs_1_), channel_id=1, source_target_pairs={{0,241},{1,16},{2,243},{3,18},{4,245},{5,20},{6,247},{7,22},{8,249... | collective-permute-start | bytes 4718600 | tf_op jit(solution)/shard_map/ppermute | solution.py:49
  31.9 0.0 all-to-all-done.mean_ref
  31.9 0.0 collective-permute-done.2.refs_2_
  31.9 4.8 %shard_map.17 = (f32[8,2048]{1,0:T(8,128)S(1)}, f32[16,28,8,128]{3,2,1,0:T(8,128)S(1)}) custom-call(s32[1]{0:T(128)} %bitcast.16.core_ref, f32[16,16,128]{2,1,0:T(8,128)S(1)} %all-to-all-done.mean_ref, bf16[768,1024]{1,0:T(8,128)(2,1)S(1)} %constant_dynamic-update-slice_fusion.refs_0_, bf16[768,1024]{1,0:T(8,128)(2,1)} %collective-permute-done.1.refs_1_, ...), custom_call_target="tpu_custom_call" | custom-call | flops 49999998976 | bytes 1 | tf_op jit(solution)/shard_map/pallas_call | solution.py:140
  36.8 1.1 convert_element_type.35
  37.9 5.1 %all-to-all-start.1 = ((f16[16,28,8,128]{3,2,1,0:T(8,128)(2,1)}), f16[16,28,8,128]{3,2,1,0:T(8,128)(2,1)}, u32[]{:S(2)}, u32[]{:S(2)}) async-start(f16[16,28,8,128]{3,2,1,0:T(8,128)(2,1)} %convert_element_type.35), calls=%async_computation.1 | async-start | bytes 1835008 | tf_op jit(solution)/shard_map/all_to_all | solution.py:152
  43.0 3.4 %collective-permute-start.7 = (bf16[768,1024]{1,0:T(8,128)(2,1)}, bf16[768,1024]{1,0:T(8,128)(2,1)}, u32[]{:S(2)}, u32[]{:S(2)}) collective-permute-start(bf16[768,1024]{1,0:T(8,128)(2,1)} %collective-permute-done.1.refs_1_), channel_id=1, source_target_pairs={{0,112},{1,17},{2,114},{3,19},{4,116},{5,21},{6,118},{7,23},{8,120... | collective-permute-start | bytes 4718600 | tf_op jit(solution)/shard_map/ppermute | solution.py:49
  46.4 5.8 %collective-permute-done.6.refs_2_ = bf16[768,1024]{1,0:T(8,128)(2,1)S(1)} collective-permute-done((bf16[768,1024]{1,0:T(8,128)(2,1)}, bf16[768,1024]{1,0:T(8,128)(2,1)S(1)}, u32[]{:S(2)}, u32[]{:S(2)}) %collective-permute-start.6) | collective-permute-done | bytes 1572896 | tf_op jit(solution)/shard_map/ppermute | solution.py:49
  52.2 4.3 %shard_map.18 = f32[16,28,8,128]{3,2,1,0:T(8,128)S(1)} custom-call(s32[1]{0:T(128)} %bitcast.16.core_ref, f32[8,2048]{1,0:T(8,128)S(1)} %get-tuple-element.30.mean_ref, bf16[768,1024]{1,0:T(8,128)(2,1)S(1)} %constant_dynamic-update-slice_fusion.refs_0_, bf16[768,1024]{1,0:T(8,128)(2,1)} %collective-permute-done.1.refs_1_, ...), custom_call_target="tpu_custom_call" | custom-call | flops 1 | bytes 1 | tf_op jit(solution)/shard_map/pallas_call | solution.py:140
  56.5 1.0 convert_element_type.38
  57.6 3.1 %all-to-all-done.1 = f16[16,28,8,128]{3,2,1,0:T(8,128)(2,1)} async-done(((f16[16,28,8,128]{3,2,1,0:T(8,128)(2,1)}), f16[16,28,8,128]{3,2,1,0:T(8,128)(2,1)}, u32[]{:S(2)}, u32[]{:S(2)}) %all-to-all-start.1) | async-done | bytes 917536 | tf_op jit(solution)/shard_map/all_to_all | solution.py:152
  60.7 7.3 %all-to-all-start.2 = ((f16[16,28,8,128]{3,2,1,0:T(8,128)(2,1)}), f16[16,28,8,128]{3,2,1,0:T(8,128)(2,1)}, u32[]{:S(2)}, u32[]{:S(2)}) async-start(f16[16,28,8,128]{3,2,1,0:T(8,128)(2,1)} %convert_element_type.38), calls=%async_computation.2 | async-start | bytes 1835008 | tf_op jit(solution)/shard_map/all_to_all | solution.py:152
  68.0 0.8 exponential_bitcast_fusion.2
  68.8 1.4 %multiply_reduce_fusion.1.refs_0_ = f32[2,27,8,128]{3,2,1,0:T(8,128)S(1)} fusion(f16[8,2,28,8,128]{4,3,2,1,0:T(8,128)(2,1)} %bitcast.19, f32[8,2,8,128]{3,2,1,0:T(8,128)S(1)} %exponential_bitcast_fusion.2), kind=kLoop, calls=%fused_computation.1 | loop fusion | flops 1271808 | bytes 1171456 | tf_op jit(solution)/shard_map/reduce_sum | solution.py:158
  70.2 0.6 slice_bitcast_fusion.8
  70.8 2.9 %collective-permute-start.5 = (f32[9,8,128]{2,1,0:T(8,128)}, f32[9,8,128]{2,1,0:T(8,128)S(1)}, u32[]{:S(2)}, u32[]{:S(2)}) collective-permute-start(f32[9,8,128]{2,1,0:T(8,128)} %get-tuple-element.57), channel_id=1, source_target_pairs={{0,128},{1,129},{2,130},{3,131},{4,132},{5,133},{6,134},{7,135},{8... | collective-permute-start | bytes 110600 | tf_op jit(solution)/shard_map/ppermute | solution.py:49
  73.7 1.5 %collective-permute-start.4 = (f32[9,8,128]{2,1,0:T(8,128)}, f32[9,8,128]{2,1,0:T(8,128)S(1)}, u32[]{:S(2)}, u32[]{:S(2)}) collective-permute-start(f32[9,8,128]{2,1,0:T(8,128)} %get-tuple-element.58), channel_id=1, source_target_pairs={{0,112},{1,113},{2,114},{3,115},{4,116},{5,117},{6,118},{7,119},{8... | collective-permute-start | bytes 110600 | tf_op jit(solution)/shard_map/ppermute | solution.py:49
  75.2 0.6 collective-permute-start.3
  75.8 0.0 collective-permute-done.7.refs_1_
  75.8 3.4 %shard_map.19 = f32[16,19,8,128]{3,2,1,0:T(8,128)S(1)} custom-call(s32[1]{0:T(128)} %bitcast.16.core_ref, f32[8,2048]{1,0:T(8,128)S(1)} %get-tuple-element.30.mean_ref, bf16[768,1024]{1,0:T(8,128)(2,1)S(1)} %constant_dynamic-update-slice_fusion.refs_0_, bf16[768,1024]{1,0:T(8,128)(2,1)} %collective-permute-done.7.refs_1_, ...), custom_call_target="tpu_custom_call" | custom-call | flops 1 | bytes 1 | tf_op jit(solution)/shard_map/pallas_call | solution.py:140
  79.2 0.9 convert_element_type.39
  80.1 0.9 all-to-all-done.2
  81.0 0.9 collective-permute-done.5.refs_3_
  81.9 6.0 %all-to-all-start.3 = ((f16[16,19,8,128]{3,2,1,0:T(8,128)(2,1)}), f16[16,19,8,128]{3,2,1,0:T(8,128)(2,1)S(1)}, u32[]{:S(2)}, u32[]{:S(2)}) async-start(f16[16,19,8,128]{3,2,1,0:T(8,128)(2,1)} %convert_element_type.39), calls=%async_computation.3 | async-start | bytes 1245184 | tf_op jit(solution)/shard_map/all_to_all | solution.py:152
  87.9 0.8 exponential_bitcast_fusion.1
  88.7 1.4 %multiply_reduce_fusion.refs_4_ = f32[2,27,8,128]{3,2,1,0:T(8,128)S(1)} fusion(f16[8,2,28,8,128]{4,3,2,1,0:T(8,128)(2,1)} %bitcast.24, f32[8,2,8,128]{3,2,1,0:T(8,128)S(1)} %exponential_bitcast_fusion.1), kind=kLoop, calls=%fused_computation | loop fusion | flops 1271808 | bytes 1171456 | tf_op jit(solution)/shard_map/reduce_sum | solution.py:158
  90.1 2.8 %collective-permute-start.8 = (f32[18,8,128]{2,1,0:T(8,128)S(1)}, f32[18,8,128]{2,1,0:T(8,128)S(1)}, u32[]{:S(2)}, u32[]{:S(2)}) collective-permute-start(f32[18,8,128]{2,1,0:T(8,128)S(1)} %pad_maximum_fusion), channel_id=1, source_target_pairs={{0,96},{1,97},{2,98},{3,99},{4,100},{5,101},{6,102},{7,103},{8,104... | collective-permute-start | bytes 221192 | tf_op jit(solution)/shard_map/ppermute | solution.py:49
  92.9 1.5 %collective-permute-start.9 = (f32[18,8,128]{2,1,0:T(8,128)S(1)}, f32[18,8,128]{2,1,0:T(8,128)S(1)}, u32[]{:S(2)}, u32[]{:S(2)}) collective-permute-start(f32[18,8,128]{2,1,0:T(8,128)S(1)} %pad_maximum_fusion.1), channel_id=1, source_target_pairs={{0,160},{1,161},{2,162},{3,163},{4,164},{5,165},{6,166},{7,167},{8... | collective-permute-start | bytes 221192 | tf_op jit(solution)/shard_map/ppermute | solution.py:49
  94.4 2.7 %collective-permute-start.11 = (f32[9,8,128]{2,1,0:T(8,128)S(1)}, f32[9,8,128]{2,1,0:T(8,128)S(1)}, u32[]{:S(2)}, u32[]{:S(2)}) collective-permute-start(f32[9,8,128]{2,1,0:T(8,128)S(1)} %get-tuple-element.51), channel_id=1, source_target_pairs={{0,112},{1,113},{2,114},{3,115},{4,116},{5,117},{6,118},{7,119},{8... | collective-permute-start | bytes 110600 | tf_op jit(solution)/shard_map/ppermute | solution.py:49
  97.1 0.0 collective-permute-start.10
  97.1 1.6 %collective-permute-done.11.refs_8_ = f32[9,8,128]{2,1,0:T(8,128)S(1)} collective-permute-done((f32[9,8,128]{2,1,0:T(8,128)S(1)}, f32[9,8,128]{2,1,0:T(8,128)S(1)}, u32[]{:S(2)}, u32[]{:S(2)}) %collective-permute-start.11) | collective-permute-done | bytes 36896 | tf_op jit(solution)/shard_map/ppermute | solution.py:49
  98.7 3.8 %collective-permute-done.10.refs_7_ = f32[9,8,128]{2,1,0:T(8,128)S(1)} collective-permute-done((f32[9,8,128]{2,1,0:T(8,128)S(1)}, f32[9,8,128]{2,1,0:T(8,128)S(1)}, u32[]{:S(2)}, u32[]{:S(2)}) %collective-permute-start.10) | collective-permute-done | bytes 36896 | tf_op jit(solution)/shard_map/ppermute | solution.py:49
  102.5 0.0 collective-permute-done.8.refs_5_
  102.6 0.1 multiply_reduce_fusion.2.refs_9_
  102.7 2.6 %collective-permute-start.12 = (f32[18,8,128]{2,1,0:T(8,128)S(1)}, f32[18,8,128]{2,1,0:T(8,128)S(1)}, u32[]{:S(2)}, u32[]{:S(2)}) collective-permute-start(f32[18,8,128]{2,1,0:T(8,128)S(1)} %pad_maximum_fusion.2), channel_id=1, source_target_pairs={{0,96},{1,97},{2,98},{3,99},{4,100},{5,101},{6,102},{7,103},{8,104... | collective-permute-start | bytes 221192 | tf_op jit(solution)/shard_map/ppermute | solution.py:49
  105.3 0.1 stack.67.place_ref
  105.4 2.7 %collective-permute-done.12.refs_10_ = f32[18,8,128]{2,1,0:T(8,128)S(1)} collective-permute-done((f32[18,8,128]{2,1,0:T(8,128)S(1)}, f32[18,8,128]{2,1,0:T(8,128)S(1)}, u32[]{:S(2)}, u32[]{:S(2)}) %collective-permute-start.12) | collective-permute-done | bytes 73760 | tf_op jit(solution)/shard_map/ppermute | solution.py:49
  108.2 1.4 %shard_map.20 = f32[24,6144]{1,0:T(8,128)} custom-call(s32[16]{0:T(128)S(1)} %stack.67.place_ref, f32[2,27,8,128]{3,2,1,0:T(8,128)S(1)} %multiply_reduce_fusion.1.refs_0_, f32[9,8,128]{2,1,0:T(8,128)S(1)} %collective-permute-done.3.refs_1_, f32[9,8,128]{2,1,0:T(8,128)S(1)} %collective-permute-done.4.refs_2_, ...), custom_call_target="tpu_custom_call" | custom-call | tf_op jit(solution)/shard_map/pallas_call | solution.py:232
  (14 shorter events, 0.1 us)
Async XLA Ops:
  0.0 10.3 %copy-start = (bf16[384,1024]{1,0:T(8,128)(2,1)S(1)}, bf16[384,1024]{1,0:T(8,128)(2,1)}, u32[]{:S(2)}) copy-start(bf16[384,1024]{1,0:T(8,128)(2,1)} %param.1) | copy-start | bytes 2359300
  0.0 2.5 %collective-permute-start = (bf16[384,1024]{1,0:T(8,128)(2,1)}, bf16[384,1024]{1,0:T(8,128)(2,1)S(1)}, u32[]{:S(2)}, u32[]{:S(2)}) collective-permute-start(bf16[384,1024]{1,0:T(8,128)(2,1)} %param.1), channel_id=1, source_target_pairs={{0,1},{1,0},{2,3},{3,2},{4,5},{5,4},{6,7},{7,6},{8,9},{9,8},{10,11... | collective-permute-start | bytes 2359304 | tf_op jit(solution)/shard_map/ppermute | solution.py:49
  2.6 26.2 %collective-permute-start.1 = (bf16[768,1024]{1,0:T(8,128)(2,1)S(1)}, bf16[768,1024]{1,0:T(8,128)(2,1)}, u32[]{:S(2)}, u32[]{:S(2)}) collective-permute-start(bf16[768,1024]{1,0:T(8,128)(2,1)S(1)} %constant_dynamic-update-slice_fusion.refs_0_), channel_id=1, source_target_pairs={{0,112},{1,17},{2,114},{3,19},{4,116},{5,21},{6,118},{7,23},{8,120... | collective-permute-start | bytes 4718600 | tf_op jit(solution)/shard_map/ppermute | solution.py:49
  8.5 23.4 %collective-permute-start.2 = (bf16[768,1024]{1,0:T(8,128)(2,1)S(1)}, bf16[768,1024]{1,0:T(8,128)(2,1)}, u32[]{:S(2)}, u32[]{:S(2)}) collective-permute-start(bf16[768,1024]{1,0:T(8,128)(2,1)S(1)} %constant_dynamic-update-slice_fusion.refs_0_), channel_id=1, source_target_pairs={{1,129},{3,131},{5,133},{7,135},{9,137},{11,139},{13,141},{15,143}... | collective-permute-start | bytes 4718600 | tf_op jit(solution)/shard_map/ppermute | solution.py:49
  11.3 20.7 %all-to-all-start = ((f32[16,16,128]{2,1,0:T(8,128)}), f32[16,16,128]{2,1,0:T(8,128)S(1)}, u32[]{:S(2)}, u32[]{:S(2)}) async-start(f32[16,16,128]{2,1,0:T(8,128)} %broadcast_in_dim.3), calls=%async_computation | async-start | bytes 262144 | tf_op jit(solution)/shard_map/all_to_all | solution.py:187
  28.7 23.5 %collective-permute-start.6 = (bf16[768,1024]{1,0:T(8,128)(2,1)}, bf16[768,1024]{1,0:T(8,128)(2,1)S(1)}, u32[]{:S(2)}, u32[]{:S(2)}) collective-permute-start(bf16[768,1024]{1,0:T(8,128)(2,1)} %collective-permute-done.1.refs_1_), channel_id=1, source_target_pairs={{0,241},{1,16},{2,243},{3,18},{4,245},{5,20},{6,247},{7,22},{8,249... | collective-permute-start | bytes 4718600 | tf_op jit(solution)/shard_map/ppermute | solution.py:49
  37.9 22.8 %all-to-all-start.1 = ((f16[16,28,8,128]{3,2,1,0:T(8,128)(2,1)}), f16[16,28,8,128]{3,2,1,0:T(8,128)(2,1)}, u32[]{:S(2)}, u32[]{:S(2)}) async-start(f16[16,28,8,128]{3,2,1,0:T(8,128)(2,1)} %convert_element_type.35), calls=%async_computation.1 | async-start | bytes 1835008 | tf_op jit(solution)/shard_map/all_to_all | solution.py:152
  43.0 32.8 %collective-permute-start.7 = (bf16[768,1024]{1,0:T(8,128)(2,1)}, bf16[768,1024]{1,0:T(8,128)(2,1)}, u32[]{:S(2)}, u32[]{:S(2)}) collective-permute-start(bf16[768,1024]{1,0:T(8,128)(2,1)} %collective-permute-done.1.refs_1_), channel_id=1, source_target_pairs={{0,112},{1,17},{2,114},{3,19},{4,116},{5,21},{6,118},{7,23},{8,120... | collective-permute-start | bytes 4718600 | tf_op jit(solution)/shard_map/ppermute | solution.py:49
  60.7 20.3 %all-to-all-start.2 = ((f16[16,28,8,128]{3,2,1,0:T(8,128)(2,1)}), f16[16,28,8,128]{3,2,1,0:T(8,128)(2,1)}, u32[]{:S(2)}, u32[]{:S(2)}) async-start(f16[16,28,8,128]{3,2,1,0:T(8,128)(2,1)} %convert_element_type.38), calls=%async_computation.2 | async-start | bytes 1835008 | tf_op jit(solution)/shard_map/all_to_all | solution.py:152
  70.8 11.1 %collective-permute-start.5 = (f32[9,8,128]{2,1,0:T(8,128)}, f32[9,8,128]{2,1,0:T(8,128)S(1)}, u32[]{:S(2)}, u32[]{:S(2)}) collective-permute-start(f32[9,8,128]{2,1,0:T(8,128)} %get-tuple-element.57), channel_id=1, source_target_pairs={{0,128},{1,129},{2,130},{3,131},{4,132},{5,133},{6,134},{7,135},{8... | collective-permute-start | bytes 110600 | tf_op jit(solution)/shard_map/ppermute | solution.py:49
  73.7 8.2 %collective-permute-start.4 = (f32[9,8,128]{2,1,0:T(8,128)}, f32[9,8,128]{2,1,0:T(8,128)S(1)}, u32[]{:S(2)}, u32[]{:S(2)}) collective-permute-start(f32[9,8,128]{2,1,0:T(8,128)} %get-tuple-element.58), channel_id=1, source_target_pairs={{0,112},{1,113},{2,114},{3,115},{4,116},{5,117},{6,118},{7,119},{8... | collective-permute-start | bytes 110600 | tf_op jit(solution)/shard_map/ppermute | solution.py:49
  75.2 6.7 %collective-permute-start.3 = (f32[9,8,128]{2,1,0:T(8,128)}, f32[9,8,128]{2,1,0:T(8,128)S(1)}, u32[]{:S(2)}, u32[]{:S(2)}) collective-permute-start(f32[9,8,128]{2,1,0:T(8,128)} %get-tuple-element.59), channel_id=1, source_target_pairs={{0,16},{1,17},{2,18},{3,19},{4,20},{5,21},{6,22},{7,23},{8,24},{9,... | collective-permute-start | bytes 110600 | tf_op jit(solution)/shard_map/ppermute | solution.py:49
  81.9 20.6 %all-to-all-start.3 = ((f16[16,19,8,128]{3,2,1,0:T(8,128)(2,1)}), f16[16,19,8,128]{3,2,1,0:T(8,128)(2,1)S(1)}, u32[]{:S(2)}, u32[]{:S(2)}) async-start(f16[16,19,8,128]{3,2,1,0:T(8,128)(2,1)} %convert_element_type.39), calls=%async_computation.3 | async-start | bytes 1245184 | tf_op jit(solution)/shard_map/all_to_all | solution.py:152
  90.1 12.4 %collective-permute-start.8 = (f32[18,8,128]{2,1,0:T(8,128)S(1)}, f32[18,8,128]{2,1,0:T(8,128)S(1)}, u32[]{:S(2)}, u32[]{:S(2)}) collective-permute-start(f32[18,8,128]{2,1,0:T(8,128)S(1)} %pad_maximum_fusion), channel_id=1, source_target_pairs={{0,96},{1,97},{2,98},{3,99},{4,100},{5,101},{6,102},{7,103},{8,104... | collective-permute-start | bytes 221192 | tf_op jit(solution)/shard_map/ppermute | solution.py:49
  92.9 9.6 %collective-permute-start.9 = (f32[18,8,128]{2,1,0:T(8,128)S(1)}, f32[18,8,128]{2,1,0:T(8,128)S(1)}, u32[]{:S(2)}, u32[]{:S(2)}) collective-permute-start(f32[18,8,128]{2,1,0:T(8,128)S(1)} %pad_maximum_fusion.1), channel_id=1, source_target_pairs={{0,160},{1,161},{2,162},{3,163},{4,164},{5,165},{6,166},{7,167},{8... | collective-permute-start | bytes 221192 | tf_op jit(solution)/shard_map/ppermute | solution.py:49
  94.4 4.3 %collective-permute-start.11 = (f32[9,8,128]{2,1,0:T(8,128)S(1)}, f32[9,8,128]{2,1,0:T(8,128)S(1)}, u32[]{:S(2)}, u32[]{:S(2)}) collective-permute-start(f32[9,8,128]{2,1,0:T(8,128)S(1)} %get-tuple-element.51), channel_id=1, source_target_pairs={{0,112},{1,113},{2,114},{3,115},{4,116},{5,117},{6,118},{7,119},{8... | collective-permute-start | bytes 110600 | tf_op jit(solution)/shard_map/ppermute | solution.py:49
  97.1 5.5 %collective-permute-start.10 = (f32[9,8,128]{2,1,0:T(8,128)S(1)}, f32[9,8,128]{2,1,0:T(8,128)S(1)}, u32[]{:S(2)}, u32[]{:S(2)}) collective-permute-start(f32[9,8,128]{2,1,0:T(8,128)S(1)} %get-tuple-element.52), channel_id=1, source_target_pairs={{0,16},{1,17},{2,18},{3,19},{4,20},{5,21},{6,22},{7,23},{8,24},{9,... | collective-permute-start | bytes 110600 | tf_op jit(solution)/shard_map/ppermute | solution.py:49
  102.7 5.4 %collective-permute-start.12 = (f32[18,8,128]{2,1,0:T(8,128)S(1)}, f32[18,8,128]{2,1,0:T(8,128)S(1)}, u32[]{:S(2)}, u32[]{:S(2)}) collective-permute-start(f32[18,8,128]{2,1,0:T(8,128)S(1)} %pad_maximum_fusion.2), channel_id=1, source_target_pairs={{0,96},{1,97},{2,98},{3,99},{4,100},{5,101},{6,102},{7,103},{8,104... | collective-permute-start | bytes 221192 | tf_op jit(solution)/shard_map/ppermute | solution.py:49
